TPU v7x, 32 devices: a whole 2x2x4 slice. The times are simulated.
32 devices in a mesh: dp: 4 (over y, x), expert: 8 (over z, core).
Axes of the slice: x: 2, y: 2, z: 4, core: 2. Of those that a mesh axis runs over, the one named last changes fastest.
Arguments:
- hidden_in: bfloat16 [32768, 768], P(('dp', 'expert')), may hold values from -6 to 6
- token_ids: int32 [32768], P(('dp', 'expert')), may hold values from 0 to 50256, as said below
- hash_table: int32 [50257], replicated, may hold values from 0 to 7, as said below
- segment_ids: int32 [32768], P(('dp', 'expert')), may hold values from 0 to 8, as said below
- ln1_gain: float32 [768], replicated, may hold values from 0.5 to 1.5
- ln1_bias: float32 [768], replicated, may hold values from -2 to 2
- qkv_weight: bfloat16 [768, 2304], replicated, may hold values from -0.21875 to 0.21875
- proj_weight: bfloat16 [768, 768], replicated, may hold values from -0.875 to 0.875
- ln2_gain: float32 [768], replicated, may hold values from 0.5 to 1.5
- ln2_bias: float32 [768], replicated, may hold values from -2 to 2
- expert_in: bfloat16 [8, 768, 3072], P('expert'), may hold values from -0.21875 to 0.21875
- expert_out: bfloat16 [8, 3072, 768], P('expert'), may hold values from -0.109375 to 0.109375
- out_grad: bfloat16 [32768, 768], P(('dp', 'expert'))
Outputs:
- block_out: bfloat16 [32768, 768], P(('dp', 'expert'))
- input_grad: float32 [32768, 768], P(('dp', 'expert'))
- ln1_gain_grad: float32 [768], replicated
- ln1_bias_grad: float32 [768], replicated
- qkv_grad: float32 [768, 2304], replicated
- proj_grad: float32 [768, 768], replicated
- ln2_gain_grad: float32 [768], replicated
- ln2_bias_grad: float32 [768], replicated
- expert_in_grad: float32 [8, 768, 3072], P('expert')
- expert_out_grad: float32 [8, 3072, 768], P('expert')
- load: float32 [8], replicated
Inputs may be any that keep to these rules, and one draw needn't show every extreme that they name: hash_table[v] is the expert of token id v; every expert is the expert of 50257 // 8 ids or more. `token_ids`: of the 1024 tokens of one device at most 256 have the same expert; one expert has exactly 256 tokens on every device. `segment_ids`: within each sequence of 1024 tokens the ids start at 0, never fall and end at 8; no new document starts between places 1024 // 4 and 768 of a sequence.
All inputs are finite; a program needn't handle non-finite values.
Results may differ from a plain program's by a relative error of at most 0.0095.
Values may be sent and summed in bfloat16 or wider, within the bound.
No kernel may reach another device: no remote copies, remote signals or barrier semaphores. Data moves between devices by JAX's collectives and lax.ppermute only.
A program may use at most 320 MiB of HBM per device.

v0:
```python
import jax
import jax.numpy as jnp
from jax import lax
from jax.sharding import PartitionSpec as P

HEAD = 64


EPSILON = 1e-05


def norm_parts(values_in):
    centred = values_in - jnp.mean(values_in, -1, keepdims=True)
    inv_scale = lax.rsqrt(jnp.mean(centred * centred, -1, keepdims=True) + EPSILON)
    return (centred * inv_scale, inv_scale)


def norm_back(grad_normed_out, normed, inv_scale, gain):
    scaled = grad_normed_out * gain
    centre = jnp.mean(scaled, -1, keepdims=True)
    along = jnp.mean(scaled * normed, -1, keepdims=True)
    return inv_scale * (scaled - centre - normed * along)


def angle_tables(position, head_width):
    half = head_width // 2
    freq = 10000.0 ** (-jnp.arange(half, dtype=jnp.float32) / half)
    angle = position.astype(jnp.float32)[:, None] * freq[None, :]
    return (jnp.cos(angle)[:, None, :], jnp.sin(angle)[:, None, :])


def turn(tensor, cosine, sine):
    half = tensor.shape[-1] // 2
    first = tensor[..., :half]
    second = tensor[..., half:]
    return jnp.concatenate([first * cosine - second * sine, second * cosine + first * sine], -1)


def turn_back(grad_in, cosine, sine):
    half = grad_in.shape[-1] // 2
    first = grad_in[..., :half]
    second = grad_in[..., half:]
    return jnp.concatenate([first * cosine + second * sine, second * cosine - first * sine], -1)


def contract_rows(left, right):
    return lax.dot_general(
        left, right, (((0,), (0,)), ((), ())), preferred_element_type=jnp.float32
    )


def contract_cols(left, right):
    return lax.dot_general(
        left, right, (((1,), (1,)), ((), ())), preferred_element_type=jnp.float32
    )


def local(
    hidden_in,
    token_ids,
    hash_table,
    segment_ids,
    ln1_gain,
    ln1_bias,
    qkv_weight,
    proj_weight,
    ln2_gain,
    ln2_bias,
    expert_in,
    expert_out,
    out_grad,
):
    tok_rows, model_width = hidden_in.shape
    head_count = model_width // HEAD
    group_size = lax.axis_size("expert")
    device_total = lax.axis_size("dp") * group_size
    position = jnp.arange(tok_rows, dtype=jnp.int32)
    cosine, sine = angle_tables(position, HEAD)
    hidden = hidden_in.astype(jnp.float32)
    normed_one, scale_one = norm_parts(hidden)
    h_one = (normed_one * ln1_gain + ln1_bias).astype(jnp.bfloat16)
    projected = jnp.dot(h_one, qkv_weight, preferred_element_type=jnp.float32).reshape(
        tok_rows, 3, head_count, HEAD
    )
    query = turn(projected[:, 0], cosine, sine).astype(jnp.bfloat16)
    keys = turn(projected[:, 1], cosine, sine).astype(jnp.bfloat16)
    values = projected[:, 2].astype(jnp.bfloat16)
    block_rows = min(tok_rows, 512)
    block_count = tok_rows // block_rows
    query_blocks = query.reshape(block_count, block_rows, head_count, HEAD)
    place_blocks = position.reshape(block_count, block_rows)
    seg_blocks = segment_ids.reshape(block_count, block_rows)

    def block_scores(block_query, block_place, block_seg):
        raw_scores = (
            jnp.einsum("qhd,khd->hqk", block_query, keys, preferred_element_type=jnp.float32)
            * 0.125
        )
        allowed = (position[None, :] <= block_place[:, None]) & (
            segment_ids[None, :] == block_seg[:, None]
        )
        return jnp.where(allowed[None], raw_scores, -1e30)

    def forward_block(packed):
        scores = block_scores(packed[0], packed[1], packed[2])
        row_top = jnp.max(scores, -1, keepdims=True)
        exponent = jnp.exp(scores - row_top)
        row_total = jnp.sum(exponent, -1, keepdims=True)
        weights = (exponent / row_total).astype(jnp.bfloat16)
        mixed_block = jnp.einsum(
            "hqk,khd->qhd", weights, values, preferred_element_type=jnp.float32
        )
        return (mixed_block, row_top + jnp.log(row_total))

    mixed, log_totals = lax.map(forward_block, (query_blocks, place_blocks, seg_blocks))
    mixed_low = mixed.reshape(tok_rows, model_width).astype(jnp.bfloat16)
    branch = jnp.dot(mixed_low, proj_weight, preferred_element_type=jnp.float32)
    middle = hidden + branch
    normed_two, scale_two = norm_parts(middle)
    h_two = (normed_two * ln2_gain + ln2_bias).astype(jnp.bfloat16)
    chosen = hash_table[token_ids]
    capacity = 2 * tok_rows // group_size
    member = (chosen[:, None] == jnp.arange(group_size, dtype=jnp.int32)[None, :]).astype(jnp.int32)
    slot = jnp.sum((jnp.cumsum(member, 0) - 1) * member, 1)
    target = chosen * capacity + slot
    dispatch = (
        target[None, :] == jnp.arange(group_size * capacity, dtype=jnp.int32)[:, None]
    ).astype(jnp.bfloat16)
    outgoing = jnp.dot(dispatch, h_two, preferred_element_type=jnp.float32).astype(jnp.bfloat16)
    outgoing = outgoing.reshape(group_size, capacity, model_width)
    sent_grads = jnp.dot(dispatch, out_grad, preferred_element_type=jnp.float32).astype(
        jnp.bfloat16
    )
    sent_grads = sent_grads.reshape(group_size, capacity, model_width)
    weight_in = expert_in[0]
    weight_out = expert_out[0]
    hidden_units = weight_in.shape[1]
    grad_final = out_grad.astype(jnp.float32)
    arrived_rows = lax.all_to_all(outgoing, "expert", split_axis=0, concat_axis=0, tiled=True)
    lead = arrived_rows.shape[:2]
    flat_rows = arrived_rows.reshape(-1, model_width)
    inner_rows = jnp.dot(flat_rows, weight_in, preferred_element_type=jnp.float32)
    activated = jax.nn.gelu(inner_rows).astype(jnp.bfloat16)
    produced_rows = jnp.dot(activated, weight_out, preferred_element_type=jnp.float32).astype(
        jnp.bfloat16
    )
    produced_rows = produced_rows.reshape(lead + (model_width,))
    results_back = lax.all_to_all(produced_rows, "expert", split_axis=0, concat_axis=0, tiled=True)
    grad_rows = lax.all_to_all(
        sent_grads, "expert", split_axis=0, concat_axis=0, tiled=True
    ).reshape(-1, model_width)
    arrived_flat = arrived_rows.reshape(-1, model_width)
    inner = inner_rows.reshape(lead + (hidden_units,)).reshape(-1, hidden_units)
    act_value, act_pull = jax.vjp(jax.nn.gelu, inner)
    act_low = act_value.astype(jnp.bfloat16)
    grad_act = contract_cols(grad_rows, weight_out)
    grad_inner = act_pull(grad_act)[0].astype(jnp.bfloat16)
    grad_arrived = contract_cols(grad_inner, weight_in).astype(jnp.bfloat16)
    back_rows = lax.all_to_all(
        grad_arrived.reshape(group_size, capacity, model_width),
        "expert",
        split_axis=0,
        concat_axis=0,
        tiled=True,
    )
    combined = contract_rows(dispatch, results_back.reshape(-1, model_width))
    block_out = (middle + combined).astype(jnp.bfloat16)
    grad_h_two = contract_rows(dispatch, back_rows.reshape(-1, model_width))
    grad_in_w, grad_out_w = lax.psum(
        (contract_rows(arrived_flat, grad_inner), contract_rows(act_low, grad_rows)), "dp"
    )
    gain_two_grad = jnp.sum(grad_h_two * normed_two, 0)
    bias_two_grad = jnp.sum(grad_h_two, 0)
    grad_middle = grad_final + norm_back(grad_h_two, normed_two, scale_two, ln2_gain)
    grad_branch = grad_middle.astype(jnp.bfloat16)
    proj_grad = contract_rows(mixed_low, grad_branch)
    grad_mixed = contract_cols(grad_branch, proj_weight).astype(jnp.bfloat16)
    grad_blocks = grad_mixed.reshape(block_count, block_rows, head_count, HEAD)

    def backward_block(carry, packed):
        block_query, block_place, block_seg, block_log, block_grad = packed
        scores = block_scores(block_query, block_place, block_seg)
        chance = jnp.exp(scores - block_log)
        chance_low = chance.astype(jnp.bfloat16)
        grad_weights = jnp.einsum(
            "qhd,khd->hqk", block_grad, values, preferred_element_type=jnp.float32
        )
        centre = jnp.sum(chance * grad_weights, -1, keepdims=True)
        grad_scores = (chance * (grad_weights - centre)).astype(jnp.bfloat16)
        grad_query_block = (
            jnp.einsum("hqk,khd->qhd", grad_scores, keys, preferred_element_type=jnp.float32)
            * 0.125
        )
        grad_key_block = (
            jnp.einsum("hqk,qhd->khd", grad_scores, block_query, preferred_element_type=jnp.float32)
            * 0.125
        )
        grad_value_block = jnp.einsum(
            "hqk,qhd->khd", chance_low, block_grad, preferred_element_type=jnp.float32
        )
        return ((carry[0] + grad_key_block, carry[1] + grad_value_block), grad_query_block)

    empty_keys = jnp.zeros((tok_rows, head_count, HEAD), jnp.float32)
    (key_grad, value_grad), grad_query = lax.scan(
        backward_block,
        (empty_keys, empty_keys),
        (query_blocks, place_blocks, seg_blocks, log_totals, grad_blocks),
    )
    grad_query = grad_query.reshape(tok_rows, head_count, HEAD)
    grad_raw = jnp.stack(
        [turn_back(grad_query, cosine, sine), turn_back(key_grad, cosine, sine), value_grad], 1
    )
    grad_raw = grad_raw.reshape(tok_rows, 3 * model_width).astype(jnp.bfloat16)
    qkv_grad = contract_rows(h_one, grad_raw)
    grad_h_one = contract_cols(grad_raw, qkv_weight)
    gain_one_grad = jnp.sum(grad_h_one * normed_one, 0)
    bias_one_grad = jnp.sum(grad_h_one, 0)
    input_grad = grad_middle + norm_back(grad_h_one, normed_one, scale_one, ln1_gain)
    counts = jnp.sum(member, 0).astype(jnp.float32)
    summed = lax.psum(
        (qkv_grad, proj_grad, gain_one_grad, bias_one_grad, gain_two_grad, bias_two_grad, counts),
        ("dp", "expert"),
    )
    load = summed[6] * (group_size / (tok_rows * device_total))
    return (
        block_out,
        input_grad,
        summed[2],
        summed[3],
        summed[0],
        summed[1],
        summed[4],
        summed[5],
        grad_in_w[None],
        grad_out_w[None],
        load,
    )


def solution(mesh):
    in_specs = (
        P(("dp", "expert"), None),
        P(("dp", "expert")),
        P(),
        P(("dp", "expert")),
        P(),
        P(),
        P(),
        P(),
        P(),
        P(),
        P("expert", None, None),
        P("expert", None, None),
        P(("dp", "expert"), None),
    )
    out_specs = (
        P(("dp", "expert"), None),
        P(("dp", "expert"), None),
        P(),
        P(),
        P(),
        P(),
        P(),
        P(),
        P("expert", None, None),
        P("expert", None, None),
        P(),
    )
    return jax.shard_map(local, mesh=mesh, in_specs=in_specs, out_specs=out_specs, check_vma=False)
```

profile of v0, /device:TPU:0, one launch (start us, length us, event | category | flops | bytes accessed | tf_op | source)
XLA Modules:
  0.0 1316.1 jit_solution(10889000615408639206)
XLA Ops:
  49.4 79.1 %while.28 = (s32[]{:T(128)}, bf16[2,512,12,64]{1,3,2,0:T(8,128)(2,1)}, f32[2,12,512,1]{2,1,3,0:T(8,128)}, s32[2,512]{1,0:T(2,128)S(1)}, s32[1024]{0:T(1024)S(1)}...) while((s32[]{:T(128)}, ...), condition=%wide.region_5.6_spmd.clone, body=%wide.region_2.5_spmd.clone.sunk | while | flops 1687676928 | bytes 190685408 | solution.py:115
  50.2 14.4 %fusion.146 = (f32[12,512]{1,0:T(8,128)S(1)}, f32[12,512,1024]{2,1,0:T(8,128)}) fusion(pred[512,1024]{1,0:T(8,128)(4,1)S(1)} %fusion.145, bf16[1024,12,64]{0,2,1:T(8,128)(2,1)} %get-tuple-element.507, bf16[2,512,12,64]{1,3,2,0:T(8,128)(2,1)} %get-tuple-element.506, s32[]{:T(128)S(6)} %copy.87), kind=kOutput, calls=%fused_computation.6.clone.1 | convolution fusion | flops 824174592 | bytes 28073988 | tf_op jit(solution)/shard_map/while/body/eval_jaxpr/qhd,khd->hqk/dot_general | solution.py:96
  64.5 12.3 fusion.147
  89.6 14.4 %fusion.146 = (f32[12,512]{1,0:T(8,128)S(1)}, f32[12,512,1024]{2,1,0:T(8,128)}) fusion(pred[512,1024]{1,0:T(8,128)(4,1)S(1)} %fusion.145, bf16[1024,12,64]{0,2,1:T(8,128)(2,1)} %get-tuple-element.507, bf16[2,512,12,64]{1,3,2,0:T(8,128)(2,1)} %get-tuple-element.506, s32[]{:T(128)S(6)} %copy.87), kind=kOutput, calls=%fused_computation.6.clone.1 | convolution fusion | flops 824174592 | bytes 28073988 | tf_op jit(solution)/shard_map/while/body/eval_jaxpr/qhd,khd->hqk/dot_general | solution.py:96
  104.0 12.3 fusion.147
  134.5 16.7 %fusion.74 = bf16[2048,768]{1,0:T(8,128)(2,1)} fusion(s32[1024]{0:T(1024)S(1)} %copy-done.40, f32[1024,768]{0,1:T(8,128)S(1)} %get-tuple-element.329, f32[768]{0:T(1024)S(1)} %copy-done.47, f32[768]{0:T(1024)S(1)} %copy-done.35, f32[1024]{0:T(1024)S(1)} %add_rsqrt_fusion, f32[1024]{0:T(1024)S(1)} %broadcast_multiply_fusion.4), kind=kOutput, calls=%fused_computation.92 | convolution fusion | flops 3228827648 | bytes 6309888 | tf_op jit(solution)/shard_map/dot_general | solution.py:129
  164.0 65.1 %all-to-all-done = bf16[8,256,768]{2,1,0:T(8,128)(2,1)} async-done(((bf16[8,256,768]{2,1,0:T(8,128)(2,1)}), bf16[8,256,768]{2,1,0:T(8,128)(2,1)}, u32[]{:S(2)}, u32[]{:S(2)}) %all-to-all-start) | async-done | bytes 3145760 | tf_op jit(solution)/shard_map/all_to_all | solution.py:139
  233.6 17.4 %fusion.56 = f32[2048,3072]{1,0:T(8,128)} fusion(bf16[2048,768]{1,0:T(8,128)(2,1)} %bitcast.7, bf16[1,768,3072]{2,1,0:T(8,128)(2,1)} %param.27), kind=kOutput, calls=%fused_computation.78 | convolution fusion | flops 9663676416 | bytes 33030144 | tf_op jit(solution)/shard_map/dot_general | solution.py:142
  251.0 54.1 %all-to-all-done.2 = bf16[8,256,768]{2,1,0:T(8,128)(2,1)} async-done(((bf16[8,256,768]{2,1,0:T(8,128)(2,1)}), bf16[8,256,768]{2,1,0:T(8,128)(2,1)}, u32[]{:S(2)}, u32[]{:S(2)}) %all-to-all-start.2) | async-done | bytes 3145760 | tf_op jit(solution)/shard_map/all_to_all | solution.py:149
  305.1 31.3 %fusion.43 = bf16[2048,3072]{1,0:T(8,128)(2,1)} fusion(f32[2048,3072]{1,0:T(8,128)} %fusion.56, bf16[2048,768]{1,0:T(8,128)(2,1)} %bitcast.13, bf16[1,3072,768]{2,1,0:T(8,128)(2,1)} %param.28), kind=kOutput, calls=%fused_computation.59 | convolution fusion | flops 9789505536 | bytes 45613056 | tf_op jit(solution)/shard_map/dot_general | solution.py:53
  336.4 15.8 %fusion.68 = bf16[2048,768]{1,0:T(8,128)(2,1)} fusion(bf16[2048,3072]{1,0:T(8,128)(2,1)} %fusion.43, bf16[1,768,3072]{2,1,0:T(8,128)(2,1)} %param.27), kind=kOutput, calls=%fused_computation.90 | convolution fusion | flops 9665249280 | bytes 20447232 | tf_op jit(solution)/shard_map/dot_general | solution.py:53
  359.3 68.9 %all-to-all-done.3 = bf16[8,256,768]{2,1,0:T(8,128)(2,1)} async-done(((bf16[8,256,768]{2,1,0:T(8,128)(2,1)}), bf16[8,256,768]{2,1,0:T(8,128)(2,1)}, u32[]{:S(2)}, u32[]{:S(2)}) %all-to-all-start.3) | async-done | bytes 3145760 | tf_op jit(solution)/shard_map/all_to_all | solution.py:159
  461.9 242.0 %while.29 = (s32[]{:T(128)}, f32[1024,12,64]{0,2,1:T(8,128)}, f32[1024,12,64]{0,2,1:T(8,128)}, f32[2,512,12,64]{1,0,3,2:T(2,128)}, bf16[2,512,12,64]{1,3,2,0:T(8...) while((s32[]{:T(128)}, f32[1024,12,64]{0,2,1:T(8,128)}, ...), condition=%wide.region_15.16_spmd.clone, body=%wide.region_13.15_spmd.clone.sunk | while | flops 4126795776 | bytes 234135840 | solution.py:204
  463.4 13.6 %fusion.157 = f32[12,512,1024]{2,1,0:T(8,128)} fusion(bf16[1024,12,64]{0,2,1:T(8,128)(2,1)} %get-tuple-element.546, bf16[2,512,12,64]{1,3,2,0:T(8,128)(2,1)} %get-tuple-element.542, s32[]{:T(128)S(6)} %copy.97), kind=kOutput, calls=%fused_computation.36.clone.1 | convolution fusion | flops 805306368 | bytes 27525124 | tf_op jit(solution)/shard_map/while/body/eval_jaxpr/qhd,khd->hqk/dot_general | solution.py:96
  477.0 13.4 %bitcast_add_fusion.5 = f32[1024,12,64]{0,2,1:T(8,128)} fusion(f32[1024,12,64]{0,2,1:T(8,128)} %get-tuple-element.526, f32[12,512,1024]{2,1,0:T(8,128)} %fusion.157, f32[12,512]{1,0:T(8,128)S(1)} %dynamic-slice_bitcast_fusion.2, pred[512,1024]{1,0:T(8,128)(4,1)S(1)} %fusion.158, pred[]{:T(512)S(6)} %compare.3, ...), kind=kOutput, calls=%fused_computation.27.clone.1 | convolution fusion | flops 832045056 | bytes 32800772 | tf_op jit(solution)/shard_map/while/body/eval_jaxpr/hqk,qhd->khd/dot_general | solution.py:198
  490.4 18.8 %multiply_reduce_fusion.7 = (f32[12,512]{1,0:T(8,128)}, f32[12,512,1024]{2,1,0:T(8,128)}) fusion(f32[12,512,1024]{2,1,0:T(8,128)} %fusion.157, f32[12,512]{1,0:T(8,128)} %copy-done.17, pred[512,1024]{1,0:T(8,128)(4,1)} %copy-done.4, bf16[1024,12,64]{0,2,1:T(8,128)(2,1)} %get-tuple-element.549, bf16[2,512,12,64]{1,3,2,0:T(8,128)(2,1)} %get-tuple-element.548, ...), kind=kOutput, calls=%fused_computation.22.clone.1 | convolution fusion | flops 836757504 | bytes 53272580 | tf_op jit(solution)/shard_map/while/body/eval_jaxpr/qhd,khd->hqk/dot_general | solution.py:185
  509.2 22.2 %multiply_convert_fusion.5 = bf16[12,512,1024]{2,1,0:T(8,128)(2,1)} fusion(f32[12,512,1024]{2,1,0:T(8,128)} %get-tuple-element.478, f32[12,512,1024]{2,1,0:T(8,128)} %fusion.157, f32[12,512]{1,0:T(8,128)} %get-tuple-element.479, f32[12,512]{1,0:T(8,128)} %copy-done.17, pred[512,1024]{1,0:T(8,128)(4,1)} %copy-done.4), kind=kLoop, calls=%fused_computation.21.clone.1 | loop fusion | flops 37748736 | bytes 63488000 | tf_op jit(solution)/shard_map/while/body/eval_jaxpr/convert_element_type | solution.py:189
  531.4 10.1 multiply_bitcast_fusion.2
  553.1 28.8 %dynamic_update_slice.21 = f32[2,512,12,64]{1,0,3,2:T(2,128)} dynamic-update-slice(f32[2,512,12,64]{1,0,3,2:T(2,128)} %get-tuple-element.527, f32[1,512,12,64]{1,0,3,2:T(1,128)} %copy.79, s32[]{:T(128)S(6)} %copy.97, s32[]{:T(128)} %constant.77.clone.1..sunk, s32[]{:T(128)} %constant.77.clone.1..sunk, s32[]{:T(128)} %constant.77.clone.1..sunk) | dynamic-update-slice | bytes 3145732 | tf_op jit(solution)/shard_map/while/body/jit(dynamic_update_index_in_dim)/dynamic_update_slice | solution.py:115
  583.2 13.6 %fusion.157 = f32[12,512,1024]{2,1,0:T(8,128)} fusion(bf16[1024,12,64]{0,2,1:T(8,128)(2,1)} %get-tuple-element.546, bf16[2,512,12,64]{1,3,2,0:T(8,128)(2,1)} %get-tuple-element.542, s32[]{:T(128)S(6)} %copy.97), kind=kOutput, calls=%fused_computation.36.clone.1 | convolution fusion | flops 805306368 | bytes 27525124 | tf_op jit(solution)/shard_map/while/body/eval_jaxpr/qhd,khd->hqk/dot_general | solution.py:96
  596.8 14.3 %bitcast_add_fusion.5 = f32[1024,12,64]{0,2,1:T(8,128)} fusion(f32[1024,12,64]{0,2,1:T(8,128)} %get-tuple-element.526, f32[12,512,1024]{2,1,0:T(8,128)} %fusion.157, f32[12,512]{1,0:T(8,128)S(1)} %dynamic-slice_bitcast_fusion.2, pred[512,1024]{1,0:T(8,128)(4,1)S(1)} %fusion.158, pred[]{:T(512)S(6)} %compare.3, ...), kind=kOutput, calls=%fused_computation.27.clone.1 | convolution fusion | flops 832045056 | bytes 32800772 | tf_op jit(solution)/shard_map/while/body/eval_jaxpr/hqk,qhd->khd/dot_general | solution.py:198
  611.1 18.8 %multiply_reduce_fusion.7 = (f32[12,512]{1,0:T(8,128)}, f32[12,512,1024]{2,1,0:T(8,128)}) fusion(f32[12,512,1024]{2,1,0:T(8,128)} %fusion.157, f32[12,512]{1,0:T(8,128)} %copy-done.17, pred[512,1024]{1,0:T(8,128)(4,1)} %copy-done.4, bf16[1024,12,64]{0,2,1:T(8,128)(2,1)} %get-tuple-element.549, bf16[2,512,12,64]{1,3,2,0:T(8,128)(2,1)} %get-tuple-element.548, ...), kind=kOutput, calls=%fused_computation.22.clone.1 | convolution fusion | flops 836757504 | bytes 53272580 | tf_op jit(solution)/shard_map/while/body/eval_jaxpr/qhd,khd->hqk/dot_general | solution.py:185
  629.9 22.2 %multiply_convert_fusion.5 = bf16[12,512,1024]{2,1,0:T(8,128)(2,1)} fusion(f32[12,512,1024]{2,1,0:T(8,128)} %get-tuple-element.478, f32[12,512,1024]{2,1,0:T(8,128)} %fusion.157, f32[12,512]{1,0:T(8,128)} %get-tuple-element.479, f32[12,512]{1,0:T(8,128)} %copy-done.17, pred[512,1024]{1,0:T(8,128)(4,1)} %copy-done.4), kind=kLoop, calls=%fused_computation.21.clone.1 | loop fusion | flops 37748736 | bytes 63488000 | tf_op jit(solution)/shard_map/while/body/eval_jaxpr/convert_element_type | solution.py:189
  652.1 10.1 multiply_bitcast_fusion.2
  662.2 9.8 bitcast_add_fusion.4
  674.7 28.8 %dynamic_update_slice.21 = f32[2,512,12,64]{1,0,3,2:T(2,128)} dynamic-update-slice(f32[2,512,12,64]{1,0,3,2:T(2,128)} %get-tuple-element.527, f32[1,512,12,64]{1,0,3,2:T(1,128)} %copy.79, s32[]{:T(128)S(6)} %copy.97, s32[]{:T(128)} %constant.77.clone.1..sunk, s32[]{:T(128)} %constant.77.clone.1..sunk, s32[]{:T(128)} %constant.77.clone.1..sunk) | dynamic-update-slice | bytes 3145732 | tf_op jit(solution)/shard_map/while/body/jit(dynamic_update_index_in_dim)/dynamic_update_slice | solution.py:115
  724.7 16.1 %convolution_bitcast_fusion.1 = f32[1,768,3072]{2,1,0:T(8,128)} fusion(bf16[2048,768]{1,0:T(8,128)(2,1)} %bitcast.7, bf16[2048,3072]{1,0:T(8,128)(2,1)} %fusion.43), kind=kOutput, calls=%fused_computation.67 | convolution fusion | flops 9663676416 | bytes 25165824 | tf_op jit(solution)/shard_map/dot_general | solution.py:47
  740.8 21.8 %convolution_bitcast_fusion = f32[1,3072,768]{2,1,0:T(8,128)} fusion(bf16[2048,768]{1,0:T(8,128)(2,1)} %bitcast.13, f32[2048,3072]{1,0:T(8,128)} %fusion.56), kind=kOutput, calls=%fused_computation.66 | convolution fusion | flops 9720299520 | bytes 37748736 | tf_op jit(solution)/shard_map/dot_general | solution.py:47
  762.6 22.4 %fusion.71 = bf16[2048,768]{1,0:T(8,128)(2,1)} fusion(bf16[1,3072,768]{2,1,0:T(8,128)(2,1)} %param.28, f32[2048,3072]{1,0:T(8,128)} %fusion.56), kind=kOutput, calls=%fused_computation.91 | convolution fusion | flops 9721872384 | bytes 33030144 | tf_op jit(solution)/shard_map/dot_general | solution.py:144
  790.8 89.7 %all-to-all-done.1 = bf16[8,256,768]{2,1,0:T(8,128)(2,1)} async-done(((bf16[8,256,768]{2,1,0:T(8,128)(2,1)}), bf16[8,256,768]{2,1,0:T(8,128)(2,1)}, u32[]{:S(2)}, u32[]{:S(2)}) %all-to-all-start.1) | async-done | bytes 3145760 | tf_op jit(solution)/shard_map/all_to_all | solution.py:148
  915.1 38.5 %all-reduce = (f32[768]{0:T(1024)}, f32[768]{0:T(1024)}, f32[768]{0:T(1024)}, f32[768]{0:T(1024)}, f32[8]{0:T(128)}) all-reduce(f32[768]{0:T(1024)S(1)} %get-tuple-element.247, f32[768]{0:T(1024)S(1)} %copy-done.44, f32[768]{0:T(1024)S(1)} %copy-done.39, f32[768]{0:T(1024)S(1)} %copy-done.43, ...), channel_id=1, replica_groups=mesh['dp'=4,'expert'=8] {'dp','expert'}, use_global_device_ids=true, to_apply=%region_19.20 | all-reduce | flops 3080 | bytes 24640 | tf_op jit(solution)/shard_map/psum | solution.py:220
  954.8 333.2 %all-reduce.8.cloned.1.call-done = (f32[1,768,3072]{2,1,0:T(8,128)}, f32[1,3072,768]{2,1,0:T(8,128)}) async-done(((f32[1,768,3072]{2,1,0:T(8,128)}, f32[1,3072,768]{2,1,0:T(8,128)}), (f32[1,768,3072]{2,1,0:T(8,128)}, f32[1,3072,768]{2,1,0:T(8,128)})) %all-reduce.8.cloned.1.call-update) | async-done | bytes 18874384 | tf_op jit(solution)/shard_map/psum | solution.py:169
  (220 shorter events, 231.5 us)
Async XLA Ops:
  7.2 7.4 copy-start
  8.3 6.3 copy-start.37
  8.3 6.3 copy-start.48
  12.7 6.3 copy-start.29
  50.2 26.7 %copy-start.6 = (bf16[1024,12,64]{0,2,1:T(8,128)(2,1)S(1)}, bf16[1024,12,64]{0,2,1:T(8,128)(2,1)}, u32[]{:S(2)}) copy-start(bf16[1024,12,64]{0,2,1:T(8,128)(2,1)} %get-tuple-element.508) | copy-start | bytes 4718596 | tf_op jit(solution)/shard_map/while
  64.5 15.4 %copy-start.1 = (f32[12,512,1024]{2,1,0:T(8,128)S(1)}, f32[12,512,1024]{2,1,0:T(8,128)}, u32[]{:S(2)}) copy-start(f32[12,512,1024]{2,1,0:T(8,128)} %get-tuple-element.462) | copy-start | bytes 75497472 | tf_op jit(solution)/shard_map/while
  79.9 8.5 copy-start.27
  89.6 26.7 %copy-start.6 = (bf16[1024,12,64]{0,2,1:T(8,128)(2,1)S(1)}, bf16[1024,12,64]{0,2,1:T(8,128)(2,1)}, u32[]{:S(2)}) copy-start(bf16[1024,12,64]{0,2,1:T(8,128)(2,1)} %get-tuple-element.508) | copy-start | bytes 4718596 | tf_op jit(solution)/shard_map/while
  104.0 15.4 %copy-start.1 = (f32[12,512,1024]{2,1,0:T(8,128)S(1)}, f32[12,512,1024]{2,1,0:T(8,128)}, u32[]{:S(2)}) copy-start(f32[12,512,1024]{2,1,0:T(8,128)} %get-tuple-element.462) | copy-start | bytes 75497472 | tf_op jit(solution)/shard_map/while
  119.3 8.5 copy-start.27
  133.6 17.5 %copy-start.11 = (f32[1024,768]{0,1:T(8,128)}, f32[1024,768]{0,1:T(8,128)S(1)}, u32[]{:S(2)}) copy-start(f32[1024,768]{0,1:T(8,128)S(1)} %get-tuple-element.329) | copy-start | bytes 9437188
  134.5 16.7 %copy-start.33 = (f32[1024]{0:T(1024)}, f32[1024]{0:T(1024)S(1)}, u32[]{:S(2)}) copy-start(f32[1024]{0:T(1024)S(1)} %add_rsqrt_fusion) | copy-start | bytes 12292
  151.2 78.0 %all-to-all-start = ((bf16[8,256,768]{2,1,0:T(8,128)(2,1)}), bf16[8,256,768]{2,1,0:T(8,128)(2,1)}, u32[]{:S(2)}, u32[]{:S(2)}) async-start(bf16[8,256,768]{2,1,0:T(8,128)(2,1)} %bitcast.190), calls=%async_computation | async-start | bytes 6291456 | tf_op jit(solution)/shard_map/all_to_all | solution.py:139
  229.1 76.0 %all-to-all-start.2 = ((bf16[8,256,768]{2,1,0:T(8,128)(2,1)}), bf16[8,256,768]{2,1,0:T(8,128)(2,1)}, u32[]{:S(2)}, u32[]{:S(2)}) async-start(bf16[8,256,768]{2,1,0:T(8,128)(2,1)} %bitcast.188), calls=%async_computation.2 | async-start | bytes 6291456 | tf_op jit(solution)/shard_map/all_to_all | solution.py:149
  352.2 76.0 %all-to-all-start.3 = ((bf16[8,256,768]{2,1,0:T(8,128)(2,1)}), bf16[8,256,768]{2,1,0:T(8,128)(2,1)}, u32[]{:S(2)}, u32[]{:S(2)}) async-start(bf16[8,256,768]{2,1,0:T(8,128)(2,1)} %bitcast.187), calls=%async_computation.3 | async-start | bytes 6291456 | tf_op jit(solution)/shard_map/all_to_all | solution.py:159
  356.7 598.2 %all-reduce.6.cloned.1.call-start = ((), (), s32[]{:S(2)}) async-start(), calls=%async_computation.4 | async-start | bytes 18874368 | tf_op jit(solution)/shard_map/psum | solution.py:220
  439.8 4.7 copy-start.36
  462.8 14.2 %copy-start.17 = (f32[12,512]{1,0:T(8,128)}, f32[12,512]{1,0:T(8,128)S(1)}, u32[]{:S(2)}) copy-start(f32[12,512]{1,0:T(8,128)S(1)} %dynamic-slice_bitcast_fusion.2) | copy-start | bytes 73732 | tf_op jit(solution)/shard_map/while
  463.3 13.7 %copy-start.4 = (pred[512,1024]{1,0:T(8,128)(4,1)}, pred[512,1024]{1,0:T(8,128)(4,1)S(1)}, u32[]{:S(2)}) copy-start(pred[512,1024]{1,0:T(8,128)(4,1)S(1)} %fusion.158) | copy-start | bytes 1572868 | tf_op jit(solution)/shard_map/while
  463.4 13.6 %copy-start.15 = (bf16[2,512,12,64]{1,3,2,0:T(8,128)(2,1)S(1)}, bf16[2,512,12,64]{1,3,2,0:T(8,128)(2,1)}, u32[]{:S(2)}) copy-start(bf16[2,512,12,64]{1,3,2,0:T(8,128)(2,1)} %get-tuple-element.548) | copy-start | bytes 4718596 | tf_op jit(solution)/shard_map/while
  541.4 8.9 copy-start.3
  582.7 14.2 %copy-start.17 = (f32[12,512]{1,0:T(8,128)}, f32[12,512]{1,0:T(8,128)S(1)}, u32[]{:S(2)}) copy-start(f32[12,512]{1,0:T(8,128)S(1)} %dynamic-slice_bitcast_fusion.2) | copy-start | bytes 73732 | tf_op jit(solution)/shard_map/while
  583.2 13.7 %copy-start.4 = (pred[512,1024]{1,0:T(8,128)(4,1)}, pred[512,1024]{1,0:T(8,128)(4,1)S(1)}, u32[]{:S(2)}) copy-start(pred[512,1024]{1,0:T(8,128)(4,1)S(1)} %fusion.158) | copy-start | bytes 1572868 | tf_op jit(solution)/shard_map/while
  583.2 13.6 %copy-start.15 = (bf16[2,512,12,64]{1,3,2,0:T(8,128)(2,1)S(1)}, bf16[2,512,12,64]{1,3,2,0:T(8,128)(2,1)}, u32[]{:S(2)}) copy-start(bf16[2,512,12,64]{1,3,2,0:T(8,128)(2,1)} %get-tuple-element.548) | copy-start | bytes 4718596 | tf_op jit(solution)/shard_map/while
  662.2 9.8 copy-start.3
  724.7 563.4 %all-reduce.8.cloned.1.call-start = ((), (), s32[]{:S(2)}) async-start(), calls=%async_computation.5 | async-start | bytes 37748736 | tf_op jit(solution)/shard_map/psum | solution.py:169
  785.0 95.4 %copy-start.41 = (s32[1024]{0:T(1024)S(1)}, s32[1024]{0:T(1024)}, u32[]{:S(2)}) copy-start(s32[1024]{0:T(1024)} %multiply_add_fusion.1) | copy-start | bytes 12292
  785.0 95.4 %all-to-all-start.1 = ((bf16[8,256,768]{2,1,0:T(8,128)(2,1)}), bf16[8,256,768]{2,1,0:T(8,128)(2,1)}, u32[]{:S(2)}, u32[]{:S(2)}) async-start(bf16[8,256,768]{2,1,0:T(8,128)(2,1)} %bitcast.189), calls=%async_computation.1 | async-start | bytes 6291456 | tf_op jit(solution)/shard_map/all_to_all | solution.py:148
  1288.1 6.6 copy-start.19
  1294.6 10.7 slice-start
  1296.0 9.3 slice-start.1
  1296.0 9.3 slice-start.2
  (35 other events, 101.4 us)
Sparse Core Ops, SparseCore 0:
  724.8 215.5 all-reduce.5
  945.2 342.8 all-reduce.7
where the time goes:
time: 1320 us
  waiting for transfers between devices  611 us (46%)
  matrix products  367 us (28%)
  local copies, waits for them, and re-layouts  148 us (11%)
  other arithmetic  116 us (9%)
  blocking collectives  38.5 us (3%)
  starting transfers between devices  19.9 us (2%)
  between operations  14.7 us (1%)
    psum x1, waiting for transfers between devices, local(): lax.psum((contract_rows(arrived_flat, grad_inner), contract_rows(act_low,...  333 us
    all_to_all x1, waiting for transfers between devices, local(): lax.all_to_all(produced_rows, 'expert', split_axis=0, concat_axis=0, tile...  89.7 us
    all_to_all x1, waiting for transfers between devices, local(): lax.all_to_all(grad_arrived.reshape(group_size, capacity, model_width), '...  68.9 us
    all_to_all x1, waiting for transfers between devices, local(): lax.all_to_all(outgoing, 'expert', split_axis=0, concat_axis=0, tiled=True)  65.1 us
    dynamic_update_slice x4, local copies, waits for them, and re-layouts, local(): lax.map(forward_block, (query_blocks, place_blocks, seg_blocks))  63.1 us
    dot_general x6, matrix products, contract_rows(): lax.dot_general(left, right, (((0,), (0,)), ((), ())), preferred_element_...  62.2 us
    dot_general x4, matrix products, contract_cols(): lax.dot_general(left, right, (((1,), (1,)), ((), ())), preferred_element_...  58.9 us
    dot_general x4, matrix products, block_scores(): jnp.einsum('qhd,khd->hqk', block_query, keys, preferred_element_type=jnp....  56 us
  transfers between devices with their start and end apart: 6, of which 5 were waited for; matrix products, arithmetic and copies ran while one was open for 9% of the time, Pallas kernels for 0%

commit v1 on v0

v1 whole, which is shorter than its diff:
```python
import functools
import numpy as np
import jax
import jax.numpy as jnp
from jax import lax
from jax.experimental import pallas as pl
from jax.experimental.pallas import tpu as pltpu
from jax.sharding import PartitionSpec as P

HEAD = 64
EPSILON = 1e-05
BF = jnp.bfloat16
F32 = jnp.float32
I32 = jnp.int32
PAIR = 2 * HEAD
NEG = -1e30


def params(mib):
    return pltpu.CompilerParams(vmem_limit_bytes=mib << 20)


def cost(flops, bytes_accessed, transcendentals=0):
    return pl.CostEstimate(flops=1, bytes_accessed=1, transcendentals=0)


def dot(left, right, left_dim=1, right_dim=0):
    return lax.dot_general(
        left, right, (((left_dim,), (right_dim,)), ((), ())), preferred_element_type=F32
    )


def whole(shape):
    return pl.BlockSpec(shape, lambda *_: (0,) * len(shape))


def iota(shape, dim):
    return lax.broadcasted_iota(I32, shape, dim)


def norm_parts(rows):
    centred = rows - jnp.mean(rows, -1, keepdims=True)
    inv_scale = lax.rsqrt(jnp.mean(centred * centred, -1, keepdims=True) + EPSILON)
    return centred * inv_scale, inv_scale


def norm_back(grad_out, normed, inv_scale, gain):
    scaled = grad_out * gain
    centre = jnp.mean(scaled, -1, keepdims=True)
    along = jnp.mean(scaled * normed, -1, keepdims=True)
    return inv_scale * (scaled - centre - normed * along)


def one_hot_rows(target, first, count):
    return (iota((count, target.shape[1]), 0) + first == target).astype(F32).astype(BF)


def route_kernel(experts, half, block, ids_ref, table_ref, grad_ref, target_ref, counts_ref, sent_ref, place):
    tokens = ids_ref.shape[1]
    rows = table_ref.shape[0]
    padded = counts_ref.shape[0]
    step = pl.program_id(0)

    @pl.when(step == 0)
    def _():
        ids = ids_ref[...]
        picked = (iota((rows, tokens), 0) == (ids >> 7)).astype(F32).astype(BF)
        found = dot(table_ref[...], picked, 0, 0)
        chosen = jnp.sum(
            jnp.where(iota((128, tokens), 0) == (ids & 127), found, 0.0), 0, keepdims=True
        ).astype(I32)
        member = (iota((padded, tokens), 0) == chosen).astype(F32)
        earlier = (iota((tokens, tokens), 0) < iota((tokens, tokens), 1)).astype(F32).astype(BF)
        rank = dot(member.astype(BF), earlier)
        slot = jnp.sum(member * rank, 0, keepdims=True).astype(I32)
        place[...] = chosen * (2 * half) + slot
        later = (slot >= half).astype(I32)
        target_ref[...] = later * (experts * half) + chosen * half + slot - later * half
        counts_ref[...] = jnp.broadcast_to(jnp.sum(member, 1, keepdims=True), counts_ref.shape)

    sent_ref[...] = dot(one_hot_rows(place[...], step * block, block), grad_ref[...]).astype(BF)


def route(token_ids, hash_table, out_grad, experts, half):
    tokens, width = out_grad.shape
    slots = 2 * tokens
    block = 256
    padded = max(experts, 16)
    rows = -(-hash_table.shape[0] // (128 * 128)) * 128
    table = jnp.pad(hash_table, (0, rows * 128 - hash_table.shape[0])).reshape(rows, 128).astype(BF)
    target, counts, sent = pl.pallas_call(
        functools.partial(route_kernel, experts, half, block),
        name="route",
        grid=(slots // block,),
        in_specs=[whole((1, tokens)), whole((rows, 128)), whole((tokens, width))],
        out_specs=[
            whole((1, tokens)),
            whole((padded, 128)),
            pl.BlockSpec((block, width), lambda s: (s, 0)),
        ],
        out_shape=[
            jax.ShapeDtypeStruct((1, tokens), I32),
            jax.ShapeDtypeStruct((padded, 128), F32),
            jax.ShapeDtypeStruct((slots, width), BF),
        ],
        scratch_shapes=[pltpu.VMEM((1, tokens), I32)],
        compiler_params=params(40),
        cost_estimate=cost(2 * slots * tokens * width, 8 * tokens * width),
    )(token_ids.reshape(1, tokens), table, out_grad)
    return target, counts[:experts, 0], sent


def swap_halves(rows):
    half = HEAD // 2
    width = rows.shape[1]
    low = (iota(rows.shape, 1) & half) == 0
    return jnp.where(low, pltpu.roll(rows, width - half, 1), pltpu.roll(rows, half, 1))


def pre_kernel(x_ref, gain_ref, bias_ref, weight_ref, cos_ref, sin_ref, qkv_ref, h_ref):
    width = x_ref.shape[1]
    normed, _ = norm_parts(x_ref[...].astype(F32))
    h_one = (normed * gain_ref[...] + bias_ref[...]).astype(BF)
    h_ref[...] = h_one
    cosine, sine = cos_ref[...], sin_ref[...]
    for part in range(3):
        raw = dot(h_one, weight_ref[:, part * width : (part + 1) * width])
        for pair in range(width // PAIR):
            piece = raw[:, pair * PAIR : (pair + 1) * PAIR]
            if part < 2:
                piece = piece * cosine + swap_halves(piece) * sine
            if part == 0:
                piece = piece * 0.125
            start = part * width + pair * PAIR
            qkv_ref[:, start : start + PAIR] = piece.astype(BF)


def angle_tables(tokens):
    half = HEAD // 2
    freq = np.float32(10000.0) ** (-np.arange(half, dtype=np.float32) / np.float32(half))
    angle = np.arange(tokens, dtype=np.float32)[:, None] * freq[None, :].astype(np.float32)
    cosine = np.cos(angle).astype(np.float32)
    sine = np.sin(angle).astype(np.float32)
    cosine = np.concatenate([cosine, cosine], 1)
    sine = np.concatenate([-sine, sine], 1)
    return np.concatenate([cosine, cosine], 1), np.concatenate([sine, sine], 1)


def first_half(x, gain, bias, weight, cosine, sine):
    tokens, width = x.shape
    block = 256
    row = lambda w: pl.BlockSpec((block, w), lambda s: (s, 0))
    return pl.pallas_call(
        pre_kernel,
        name="norm_project",
        grid=(tokens // block,),
        in_specs=[
            row(width), whole((1, width)), whole((1, width)), whole(weight.shape), row(PAIR), row(PAIR),
        ],
        out_specs=[row(3 * width), row(width)],
        out_shape=[
            jax.ShapeDtypeStruct((tokens, 3 * width), BF),
            jax.ShapeDtypeStruct((tokens, width), BF),
        ],
        compiler_params=params(40),
        cost_estimate=cost(6 * tokens * width * width, 6 * width * width + 12 * tokens * width),
    )(x, gain, bias, weight, cosine, sine)


def head_lanes(rows, head):
    return jnp.where((iota((1, PAIR), 1) >= HEAD) == bool(head), rows, jnp.zeros_like(rows))


def attend_kernel(block, q_ref, k_ref, v_ref, seg_row_ref, seg_col_ref, mixed_ref, lse_ref, stats):
    tokens = q_ref.shape[0]
    pair = pl.program_id(0)
    upper = iota((1, PAIR), 1) >= HEAD
    for first in range(0, tokens, block):
        last = first + block
        query = q_ref[first:last, :]
        allowed = seg_col_ref[first:last, :] == seg_row_ref[:, :last]
        allowed &= iota((block, last), 1) <= iota((block, last), 0) + first
        halves = []
        for head in range(2):
            scores = dot(head_lanes(query, head), k_ref[:last, :], 1, 1)
            scores = jnp.where(allowed, scores, NEG)
            top = jnp.max(scores, -1, keepdims=True)
            weights = jnp.exp(scores - top)
            total = jnp.sum(weights, -1, keepdims=True)
            halves.append(dot(weights.astype(BF), v_ref[:last, :]) * (1.0 / total))
            lane = iota((1, 128), 1) == 2 * pair + head
            stats[first:last, :] = jnp.where(lane, top + jnp.log(total), stats[first:last, :])
        mixed_ref[first:last, :] = jnp.where(upper, halves[1], halves[0]).astype(BF)

    @pl.when(pair == pl.num_programs(0) - 1)
    def _():
        lse_ref[...] = stats[...].T


def attend(qkv, seg_row, seg_col):
    tokens, width = qkv.shape[0], qkv.shape[1] // 3
    pairs = width // PAIR
    column = lambda part: pl.BlockSpec((tokens, PAIR), lambda g: (0, part * pairs + g))
    return pl.pallas_call(
        functools.partial(attend_kernel, 256),
        name="attend",
        grid=(pairs,),
        in_specs=[column(0), column(1), column(2), whole((1, tokens)), whole((tokens, 1))],
        out_specs=[column(0), whole((128, tokens))],
        out_shape=[
            jax.ShapeDtypeStruct((tokens, width), BF),
            jax.ShapeDtypeStruct((128, tokens), F32),
        ],
        scratch_shapes=[pltpu.VMEM((tokens, 128), F32)],
        compiler_params=params(40),
        cost_estimate=cost(8 * tokens * tokens * width, 8 * tokens * width, tokens * tokens * width // HEAD),
    )(qkv, qkv, qkv, seg_row, seg_col)


def middle_kernel(block, mixed_ref, weight_ref, x_ref, gain_ref, bias_ref, target_ref, middle_ref, sent_ref, h_two):
    tokens = x_ref.shape[0]
    step = pl.program_id(0)

    @pl.when(step == 0)
    def _():
        for first in range(0, tokens, block):
            rows = slice(first, first + block)
            middle = x_ref[rows, :].astype(F32) + dot(mixed_ref[rows, :], weight_ref[...])
            middle_ref[rows, :] = middle
            normed, _ = norm_parts(middle)
            h_two[rows, :] = (normed * gain_ref[...] + bias_ref[...]).astype(BF)

    sent_ref[...] = dot(one_hot_rows(target_ref[...], step * block, block), h_two[...]).astype(BF)


def middle_part(mixed, weight, x, gain, bias, target):
    tokens, width = x.shape
    block = 256
    slots = 2 * tokens
    return pl.pallas_call(
        functools.partial(middle_kernel, block),
        name="project_dispatch",
        grid=(slots // block,),
        in_specs=[
            whole((tokens, width)), whole(weight.shape), whole((tokens, width)),
            whole((1, width)), whole((1, width)), whole((1, tokens)),
        ],
        out_specs=[whole((tokens, width)), pl.BlockSpec((block, width), lambda s: (s, 0))],
        out_shape=[
            jax.ShapeDtypeStruct((tokens, width), F32),
            jax.ShapeDtypeStruct((slots, width), BF),
        ],
        scratch_shapes=[pltpu.VMEM((tokens, width), BF)],
        compiler_params=params(40),
        cost_estimate=cost(2 * slots * tokens * width + 2 * tokens * width * width, 16 * tokens * width),
    )(mixed, weight, x, gain, bias, target)


ROOT = 0.7978845608028654
CUBE = 0.044715


def once(shape):
    return pl.BlockSpec(shape, lambda *_: (0,) * len(shape), pipeline_mode=pl.Buffered(1))


def slope_kernel(grads_ref, wout_ref, out_ref):
    experts, rows, width = grads_ref.shape
    half = rows // 2
    for chunk in range(2):
        grads = grads_ref[:, chunk * half : (chunk + 1) * half, :].reshape(experts * half, width)
        out_ref[chunk * experts * half : (chunk + 1) * experts * half, :] = dot(grads, wout_ref[...], 1, 1)


def grads_inside(grads, weight_out):
    experts, rows, width = grads.shape
    count = experts * rows
    units = weight_out.shape[0]
    tile = 512
    return pl.pallas_call(
        slope_kernel,
        name="grads_inside",
        grid=(units // tile,),
        in_specs=[once(grads.shape), pl.BlockSpec((tile, width), lambda s: (s, 0))],
        out_specs=pl.BlockSpec((count, tile), lambda s: (0, s)),
        out_shape=jax.ShapeDtypeStruct((count, units), F32),
        compiler_params=params(48),
        cost_estimate=cost(2 * count * width * units, 4 * count * units),
    )(grads, weight_out)


def expert_kernel(block, has_previous, groups, perm_ref, rows_ref, grads_ref, slope_ref, win_ref, *refs):
    refs = list(refs)
    previous_ref = refs.pop(0) if has_previous else None
    act_ref, back_ref, back = refs[-3:]
    grad_refs = refs[:-3]
    count, width = rows_ref.shape
    step = pl.program_id(0)

    @pl.when(step == 0)
    def _():
        back[...] = jnp.zeros_like(back)

    weight_in = win_ref[...]
    all_grads = grads_ref[...].reshape(count, width)
    din = dout = None
    for first in range(0, count, block):
        span = slice(first, first + block)
        rows, grads = rows_ref[span, :], all_grads[span, :]
        inner = dot(rows, weight_in)
        square = inner * inner
        tanh = jnp.tanh(inner * (ROOT + (ROOT * CUBE) * square))
        gate = 0.5 + 0.5 * tanh
        act = inner * gate
        slope = gate + act * (1.0 - tanh) * (ROOT + (3.0 * ROOT * CUBE) * square)
        act = act.astype(BF)
        act_ref[span, :] = act
        grad_inner = (slope_ref[span, :] * slope).astype(BF)
        back[span, :] += dot(grad_inner, weight_in, 1, 1)
        part_in = dot(rows, grad_inner, 0, 0)
        part_out = dot(act, grads, 0, 0)
        din = part_in if din is None else din + part_in
        dout = part_out if dout is None else dout + part_out
    if has_previous:
        din = din + previous_ref[0, 0]
        dout = dout + previous_ref[0, 1]
        swap = perm_ref[groups + step % 2] == 1
        early = jnp.where(swap, din, dout).astype(BF)
        late = jnp.where(swap, dout, din).astype(BF)
        keep_ref = grad_refs[4]
        for group in range(2):

            @pl.when(step == group)
            def _():
                grad_refs[2 * group][...] = early
                grad_refs[2 * group + 1][...] = late

        @pl.when(step >= 2)
        def _():
            keep_ref[0, 0] = early
            keep_ref[0, 1] = late
    else:
        grad_refs[0][0, 0] = din
        grad_refs[0][0, 1] = dout

    @pl.when(step == groups - 1)
    def _():
        back_ref[...] = back[...].astype(BF)


def expert_rows(chunk, rows, grads, slopes, weight_in, perm, previous=None):
    count, width = rows.shape
    experts, slots, _ = grads.shape
    groups = 4
    units = weight_in.shape[1]
    tile = units // groups
    grad_spec = pl.BlockSpec((1, 2, tile, width), lambda s, perm: (s, 0, 0, 0))
    in_specs = [
        once((count, width)),
        pl.BlockSpec((experts, slots // 2, width), lambda s, perm: (0, chunk, 0), pipeline_mode=pl.Buffered(1)),
        pl.BlockSpec((count, tile), lambda s, perm: (chunk, perm[s])),
        pl.BlockSpec((width, tile), lambda s, perm: (0, perm[s])),
    ]
    operands = [rows, grads, slopes, weight_in]
    if previous is None:
        grad_specs = [grad_spec]
        grad_shapes = [jax.ShapeDtypeStruct((groups, 2, tile, width), F32)]
    else:
        in_specs.append(grad_spec)
        operands.append(previous)
        grad_specs = [
            *([once((tile, width))] * 4),
            pl.BlockSpec((1, 2, tile, width), lambda s, perm: (jnp.maximum(s - 2, 0), 0, 0, 0)),
        ]
        grad_shapes = [jax.ShapeDtypeStruct((tile, width), BF)] * 4
        grad_shapes += [jax.ShapeDtypeStruct((2, 2, tile, width), BF)]
    return pl.pallas_call(
        functools.partial(expert_kernel, 512, previous is not None, groups),
        name="expert_rows",
        grid_spec=pltpu.PrefetchScalarGridSpec(
            num_scalar_prefetch=1,
            grid=(groups,),
            in_specs=in_specs,
            out_specs=grad_specs
            + [pl.BlockSpec((count, tile), lambda s, perm: (0, perm[s])), whole((count, width))],
            scratch_shapes=[pltpu.VMEM((count, width), F32)],
        ),
        out_shape=grad_shapes
        + [jax.ShapeDtypeStruct((count, units), BF), jax.ShapeDtypeStruct((count, width), BF)],
        compiler_params=params(60),
        cost_estimate=cost(8 * count * width * units, 12 * width * units + 6 * count * units, count * units),
    )(perm, *operands)


def result_kernel(act_ref, wout_ref, out_ref, total):
    step = pl.program_id(0)

    @pl.when(step == 0)
    def _():
        total[...] = jnp.zeros_like(total)

    total[...] += dot(act_ref[...], wout_ref[...])

    @pl.when(step == pl.num_programs(0) - 1)
    def _():
        out_ref[...] = total[...].astype(BF)


def expert_result(act, weight_out):
    count, units = act.shape
    width = weight_out.shape[1]
    tile = 768
    return pl.pallas_call(
        result_kernel,
        name="expert_result",
        grid=(units // tile,),
        in_specs=[pl.BlockSpec((count, tile), lambda s: (0, s)), pl.BlockSpec((tile, width), lambda s: (s, 0))],
        out_specs=whole((count, width)),
        out_shape=jax.ShapeDtypeStruct((count, width), BF),
        scratch_shapes=[pltpu.VMEM((count, width), F32)],
        compiler_params=params(48),
        cost_estimate=cost(2 * count * width * units, 2 * count * units),
    )(act, weight_out)


def assemble_kernel(flags_ref, *refs):
    sources, (in_ref, out_ref) = refs[:8], refs[8:]
    step = pl.program_id(0)
    for group in range(4):
        first, second = sources[2 * group], sources[2 * group + 1]
        flag = flags_ref[4 + group // 2]

        @pl.when((step == group) & (flag == 0))
        def _():
            in_ref[...] = first[...].astype(F32)
            out_ref[...] = second[...].astype(F32)

        @pl.when((step == group) & (flag != 0))
        def _():
            in_ref[...] = second[...].astype(F32)
            out_ref[...] = first[...].astype(F32)


def assemble(flags, sources):
    tile, width = sources[0].shape
    return pl.pallas_call(
        assemble_kernel,
        name="assemble",
        grid_spec=pltpu.PrefetchScalarGridSpec(
            num_scalar_prefetch=1,
            grid=(4,),
            in_specs=[whole((tile, width))] * 8,
            out_specs=[
                pl.BlockSpec((tile, width), lambda s, flags: (0, flags[s])),
                pl.BlockSpec((tile, width), lambda s, flags: (flags[s], 0)),
            ],
        ),
        out_shape=[
            jax.ShapeDtypeStruct((width, 4 * tile), F32),
            jax.ShapeDtypeStruct((4 * tile, width), F32),
        ],
        compiler_params=params(48),
        cost_estimate=cost(8 * tile * width, 48 * tile * width),
    )(flags, *sources)


def gather_rows(block, target_ref, sources):
    count = sources[0].shape[0]
    target = target_ref[...]
    total = None
    for chunk, source in enumerate(sources):
        picked = (iota((block, count), 1) + chunk * count == target).astype(F32).astype(BF)
        part = dot(picked, source[...])
        total = part if total is None else total + part
    return total


def back_kernel(
    block, back_first_ref, back_second_ref, target_ref, middle_ref, mixed_ref, out_grad_ref, gain_ref, weight_ref, sel_ref,
    grad_middle_ref, grad_mixed_ref, branch_ref, delta_ref, small_ref,
):
    step = pl.program_id(0)
    grad_h = gather_rows(block, target_ref, (back_first_ref, back_second_ref))
    normed, inv_scale = norm_parts(middle_ref[...])
    gain = gain_ref[...]
    grad_middle = out_grad_ref[...].astype(F32) + norm_back(grad_h, normed, inv_scale, gain)
    grad_middle_ref[...] = grad_middle
    branch = grad_middle.astype(BF)
    branch_ref[...] = branch
    mixed = mixed_ref[...]
    grad_mixed = dot(branch, weight_ref[...], 1, 1).astype(BF)
    grad_mixed_ref[...] = grad_mixed
    product = grad_mixed.astype(F32) * mixed.astype(F32)
    high = product.astype(BF)
    low = (product - high.astype(F32)).astype(BF)
    sel = sel_ref[...]
    delta_ref[...] = dot(sel, high, 1, 1) + dot(sel, low, 1, 1)
    gain_grad = jnp.sum(grad_h * normed, 0, keepdims=True)
    bias_grad = jnp.sum(grad_h, 0, keepdims=True)

    @pl.when(step == 0)
    def _():
        small_ref[0:1, :] = gain_grad
        small_ref[1:2, :] = bias_grad

    @pl.when(step > 0)
    def _():
        small_ref[0:1, :] += gain_grad
        small_ref[1:2, :] += bias_grad


def middle_back(back_first, back_second, target_col, middle, mixed, out_grad, gain, weight):
    tokens, width = middle.shape
    slots = 2 * back_first.shape[0]
    block = 256
    heads = np.zeros((16, width), np.float32)
    for head in range(width // HEAD):
        heads[head, head * HEAD : (head + 1) * HEAD] = 1.0
    row = lambda w: pl.BlockSpec((block, w), lambda s: (s, 0))
    return pl.pallas_call(
        functools.partial(back_kernel, block),
        name="middle_back",
        grid=(tokens // block,),
        in_specs=[
            once((slots // 2, width)), once((slots // 2, width)), row(1), row(width), row(width), row(width),
            whole((1, width)), whole(weight.shape), whole((16, width)),
        ],
        out_specs=[
            row(width), row(width), row(width), pl.BlockSpec((16, block), lambda s: (0, s)),
            whole((8, width)),
        ],
        out_shape=[
            jax.ShapeDtypeStruct((tokens, width), F32),
            jax.ShapeDtypeStruct((tokens, width), BF),
            jax.ShapeDtypeStruct((tokens, width), BF),
            jax.ShapeDtypeStruct((16, tokens), F32),
            jax.ShapeDtypeStruct((8, width), F32),
        ],
        compiler_params=params(48),
        cost_estimate=cost(2 * slots * tokens * width + 4 * tokens * width * width, 24 * tokens * width),
    )(back_first, back_second, target_col, middle, mixed, out_grad, gain, weight, jnp.asarray(heads, BF))


def attend_back_kernel(
    block, start, q_ref, k_ref, v_ref, do_ref, lse_ref, delta_ref, seg_row_ref, seg_col_ref, cos_ref, sin_ref,
    dq_ref, dk_ref, dv_ref, total,
):
    tokens = q_ref.shape[0]
    pair = pl.program_id(0) + start
    cosine, sine = cos_ref[...], sin_ref[...]
    lse = [lse_ref[pl.ds(2 * pair + head, 1), :] for head in range(2)]
    delta = [delta_ref[pl.ds(2 * pair + head, 1), :] for head in range(2)]
    for first in range(0, tokens, block):
        last = first + block
        span = tokens - first
        keys, values = k_ref[first:last, :], v_ref[first:last, :]
        allowed = seg_col_ref[first:last, :] == seg_row_ref[:, first:]
        allowed &= iota((block, span), 0) <= iota((block, span), 1)
        dk = dv = dq = None
        for head in range(2):
            query = head_lanes(q_ref[first:, :], head)
            grads = head_lanes(do_ref[first:, :], head)
            scores = dot(keys, query, 1, 1)
            chance = jnp.where(allowed, jnp.exp(scores - lse[head][:, first:]), 0.0)
            grad_weights = dot(values, grads, 1, 1)
            grad_scores = (chance * (grad_weights - delta[head][:, first:])).astype(BF)
            part_v = dot(chance.astype(BF), grads)
            part_k = dot(grad_scores, query)
            part_q = dot(grad_scores, head_lanes(keys, head), 0, 0)
            dk = part_k if dk is None else dk + part_k
            dv = part_v if dv is None else dv + part_v
            dq = part_q if dq is None else dq + part_q
        dv_ref[first:last, :] = dv.astype(BF)
        cos_k, sin_k = cosine[first:last, :], sine[first:last, :]
        dk_ref[first:last, :] = (dk * cos_k - swap_halves(dk) * sin_k).astype(BF)
        if first == 0:
            total[...] = dq
        else:
            total[first:, :] += dq
    dq = total[...] * 0.125
    dq_ref[...] = (dq * cosine - swap_halves(dq) * sine).astype(BF)


def attend_back(qkv, grad_mixed, lse, delta, seg_row, seg_col, cosine, sine, start, count):
    tokens, width = grad_mixed.shape
    pairs = width // PAIR
    column = lambda part: pl.BlockSpec((tokens, PAIR), lambda g: (0, part * pairs + start + g))
    out = jax.ShapeDtypeStruct((tokens, count * PAIR), BF)
    return pl.pallas_call(
        functools.partial(attend_back_kernel, 256, start),
        name="attend_back",
        grid=(count,),
        in_specs=[
            column(0), column(1), column(2), column(0), whole(lse.shape), whole(delta.shape),
            whole((1, tokens)), whole((tokens, 1)), whole((tokens, PAIR)), whole((tokens, PAIR)),
        ],
        out_specs=[pl.BlockSpec((tokens, PAIR), lambda g: (0, g))] * 3,
        out_shape=[out] * 3,
        scratch_shapes=[pltpu.VMEM((tokens, PAIR), F32)],
        compiler_params=params(48),
        cost_estimate=cost(20 * tokens * tokens * PAIR * count, 14 * tokens * PAIR * count, 2 * tokens * tokens * count),
    )(qkv, qkv, qkv, grad_mixed, lse, delta, seg_row, seg_col, cosine, sine)


def shared_kernel(side_ref, h_ref, dq_ref, dk_ref, dv_ref, mixed_ref, branch_ref, keep_ref, send_ref):
    parts = [dot(h_ref[...], ref[...], 0, 0) for ref in (dq_ref, dk_ref, dv_ref)]
    parts.append(dot(mixed_ref[...], branch_ref[...], 0, 0))
    second = side_ref[0] == 1
    for part in range(2):
        keep_ref[part] = jnp.where(second, parts[2 + part], parts[part])
        send_ref[part] = jnp.where(second, parts[part], parts[2 + part]).astype(BF)


def shared_grads(side, h_one, grads, mixed, branch, which):
    tokens, width = h_one.shape
    columns = grads[0].shape[1]
    block = 256
    row = pl.BlockSpec((tokens, block), lambda s, side: (0, s))
    out = pl.BlockSpec((2, block, columns), lambda s, side: (0, s, 0))
    return pl.pallas_call(
        shared_kernel,
        name="shared_grads",
        grid_spec=pltpu.PrefetchScalarGridSpec(
            num_scalar_prefetch=1,
            grid=(width // block,),
            in_specs=[row] + [once((tokens, columns))] * 3
            + [row, pl.BlockSpec((tokens, columns), lambda s, side: (0, which), pipeline_mode=pl.Buffered(1))],
            out_specs=[out, out],
        ),
        out_shape=[
            jax.ShapeDtypeStruct((2, width, columns), F32),
            jax.ShapeDtypeStruct((2, width, columns), BF),
        ],
        compiler_params=params(40),
        cost_estimate=cost(8 * tokens * width * columns, 16 * width * columns + 12 * tokens * columns),
    )(side, h_one, *grads, mixed, branch)


def final_kernel(x_ref, *refs):
    grad_refs = refs[:6]
    grad_middle_ref, weight_ref, gain_ref, input_grad_ref, small_ref = refs[6:]
    step = pl.program_id(0)
    width = x_ref.shape[1]
    columns = grad_refs[0].shape[1]
    normed, inv_scale = norm_parts(x_ref[...].astype(F32))
    grad_h = None
    for index, ref in enumerate(grad_refs):
        start = (index % 3) * width + (index // 3) * columns
        piece = dot(ref[...], weight_ref[:, start : start + columns], 1, 1)
        grad_h = piece if grad_h is None else grad_h + piece
    input_grad_ref[...] = grad_middle_ref[...] + norm_back(grad_h, normed, inv_scale, gain_ref[...])
    gain_grad = jnp.sum(grad_h * normed, 0, keepdims=True)
    bias_grad = jnp.sum(grad_h, 0, keepdims=True)

    @pl.when(step == 0)
    def _():
        small_ref[0:1, :] = gain_grad
        small_ref[1:2, :] = bias_grad

    @pl.when(step > 0)
    def _():
        small_ref[0:1, :] += gain_grad
        small_ref[1:2, :] += bias_grad


def final_part(x, grads, grad_middle, weight, gain):
    tokens, width = x.shape
    columns = grads[0].shape[1]
    block = 256
    row = lambda w: pl.BlockSpec((block, w), lambda s: (s, 0))
    return pl.pallas_call(
        final_kernel,
        name="first_back",
        grid=(tokens // block,),
        in_specs=[row(width)] + [row(columns)] * 6 + [row(width), once(weight.shape), whole((1, width))],
        out_specs=[row(width), whole((8, width))],
        out_shape=[
            jax.ShapeDtypeStruct((tokens, width), F32),
            jax.ShapeDtypeStruct((8, width), F32),
        ],
        compiler_params=params(48),
        cost_estimate=cost(6 * tokens * width * width, 6 * width * width + 16 * tokens * width),
    )(x, *grads, grad_middle, weight, gain)


def output_kernel(block, first_ref, second_ref, target_ref, middle_ref, out_ref):
    out_ref[...] = (middle_ref[...] + gather_rows(block, target_ref, (first_ref, second_ref))).astype(BF)


def block_output(first, second, target_col, middle):
    tokens, width = middle.shape
    slots = 2 * first.shape[0]
    block = 256
    row = lambda w: pl.BlockSpec((block, w), lambda s: (s, 0))
    return pl.pallas_call(
        functools.partial(output_kernel, block),
        name="block_output",
        grid=(tokens // block,),
        in_specs=[once((slots // 2, width)), once((slots // 2, width)), row(1), row(width)],
        out_specs=row(width),
        out_shape=jax.ShapeDtypeStruct((tokens, width), BF),
        compiler_params=params(40),
        cost_estimate=cost(2 * slots * tokens * width, 10 * tokens * width),
    )(first, second, target_col, middle)


def partner(axis, bit):
    return [(i, i ^ bit) for i in range(lax.axis_size(axis))]


def side(axis, bit):
    return (lax.axis_index(axis) // bit) % 2


def axis_bits(axis):
    bits, bit = [], 1
    while bit < lax.axis_size(axis):
        bits.append((axis, bit))
        bit *= 2
    return bits


def reduce_step(total, axis, bit):
    if total.shape[0] == 1:
        total = total.astype(BF)
        return total.astype(F32) + lax.ppermute(total, axis, partner(axis, bit)).astype(F32)
    mine = side(axis, bit)
    half = total.shape[0] // 2
    keep = lax.dynamic_slice_in_dim(total, mine * half, half, 0)
    send = lax.dynamic_slice_in_dim(total, (1 - mine) * half, half, 0)
    return keep + lax.ppermute(send.astype(BF), axis, partner(axis, bit)).astype(F32)


def gather_step(total, axis, bit):
    got = lax.ppermute(total, axis, partner(axis, bit))
    return jnp.where(side(axis, bit) == 0, jnp.concatenate([total, got], 0), jnp.concatenate([got, total], 0))


def sum_small(rows):
    for axis, bit in axis_bits("expert") + axis_bits("dp"):
        rows = rows + lax.ppermute(rows, axis, partner(axis, bit))
    return rows


def local(
    hidden_in, token_ids, hash_table, segment_ids, ln1_gain, ln1_bias, qkv_weight, proj_weight,
    ln2_gain, ln2_bias, expert_in, expert_out, out_grad,
):
    tokens, width = hidden_in.shape
    experts = lax.axis_size("expert")
    devices = lax.axis_size("dp") * experts
    half = tokens // experts
    row = lambda vector: vector.reshape(1, width)
    cosine, sine = (jnp.asarray(table) for table in angle_tables(tokens))
    seg_row, seg_col = segment_ids.reshape(1, tokens), segment_ids.reshape(tokens, 1)
    weight_in, weight_out = expert_in[0], expert_out[0]

    def exchange(rows):
        sent = rows.reshape(experts, rows.shape[0] // experts, width)
        return lax.all_to_all(sent, "expert", split_axis=0, concat_axis=0, tiled=True)

    def exchange_half(rows):
        return exchange(rows).reshape(tokens, width)

    def split(rows):
        return rows[:tokens], rows[tokens:]

    x_side, y_side = side("dp", 1), side("dp", 2)
    perm = jnp.stack([1 - x_side, 3 - y_side, x_side, 2 + y_side, y_side, x_side]).astype(I32)
    tie = lambda *values: lax.optimization_barrier(values)

    target, counts, sent_grads = route(token_ids, hash_table, out_grad, experts, half)
    target_col = target.reshape(tokens, 1)
    sent_grads, hidden_in = tie(sent_grads, hidden_in)
    grad_rows = exchange(sent_grads)
    qkv, h_one = first_half(hidden_in, row(ln1_gain), row(ln1_bias), qkv_weight, cosine, sine)
    mixed, lse = attend(qkv, seg_row, seg_col)
    middle, sent_rows = middle_part(mixed, proj_weight, hidden_in, row(ln2_gain), row(ln2_bias), target)
    sent_first, sent_second = split(sent_rows)
    sent_first, grad_rows = tie(sent_first, grad_rows)
    rows_first = exchange_half(sent_first)
    slopes = grads_inside(grad_rows, weight_out)
    sent_second, rows_first, slopes = tie(sent_second, rows_first, slopes)
    rows_second = exchange_half(sent_second)

    previous, act_first, back_first = expert_rows(0, rows_first, grad_rows, slopes, weight_in, perm)
    back_first, rows_second = tie(back_first, rows_second)
    back_first = exchange_half(back_first)
    early_x, late_x, early_y, late_y, keep, act_second, back_second = expert_rows(
        1, rows_second, grad_rows, slopes, weight_in, perm, previous
    )
    across_x = lambda value: lax.ppermute(value, "dp", partner("dp", 1))
    across_y = lambda value: lax.ppermute(value, "dp", partner("dp", 2))
    back_second, back_first = tie(back_second, back_first)
    back_second = exchange_half(back_second)
    early_x, early_y = across_x(early_x), across_y(early_y)
    late_x, late_y = across_x(late_x), across_y(late_y)
    result_first = expert_result(act_first, weight_out)
    result_second = expert_result(act_second, weight_out)
    result_first, result_second, back_second, early_x, early_y = tie(
        result_first, result_second, back_second, early_x, early_y
    )

    plus = lambda *values: sum(value.astype(F32) for value in values).astype(BF)
    send_x, send_y = plus(keep[0, 0], early_x), plus(keep[1, 0], early_y)
    send_x, send_y, back_second = tie(send_x, send_y, back_second)
    other_x, other_y = across_y(send_x), across_x(send_y)
    grad_middle, grad_mixed, branch, delta, small_two = middle_back(
        back_first, back_second, target_col, middle, mixed, out_grad, row(ln2_gain), proj_weight
    )
    grad_mixed, late_x, late_y, result_first = tie(grad_mixed, late_x, late_y, result_first)
    result_first = exchange_half(result_first)

    pairs = width // PAIR
    back_of = lambda grads, start: attend_back(
        qkv, grads, lse, delta, seg_row, seg_col, cosine, sine, start, pairs // 2
    )
    core_side = jnp.reshape(side("expert", 1), (1,)).astype(I32)
    across_core = lambda value: lax.ppermute(value, "expert", partner("expert", 1))
    grads_low = back_of(grad_mixed, 0)
    low, send_low = shared_grads(core_side, h_one, grads_low, mixed, branch, 0)
    other_x, other_y, send_low, grad_mixed = tie(other_x, other_y, send_low, grad_mixed)
    total_x, total_y = plus(keep[0, 1], late_x, other_x), plus(keep[1, 1], late_y, other_y)
    total_x, total_y, grad_mixed = tie(total_x, total_y, grad_mixed)
    near_x, near_y = across_y(total_x), across_x(total_y)
    got_low = across_core(send_low)
    grads_high = back_of(grad_mixed, pairs // 2)
    high, send_high = shared_grads(core_side, h_one, grads_high, mixed, branch, 1)
    near_x, near_y, got_low, send_high, result_first = tie(near_x, near_y, got_low, send_high, result_first)
    result_second = exchange_half(result_second)
    far_x, far_y = across_x(total_x), across_y(total_y)

    low = (low + got_low.astype(F32)).reshape(8, width // 4, width // 2)
    high = (high + across_core(send_high).astype(F32)).reshape(8, width // 4, width // 2)
    far_bits = axis_bits("expert")[1:]
    low_order = axis_bits("dp") + far_bits
    high_order = axis_bits("dp")[::-1] + far_bits

    def reduce_both(low, high, step):
        return reduce_step(low, *low_order[step]), reduce_step(high, *high_order[step])

    low, high = reduce_both(low, high, 0)
    input_grad, small_one = final_part(
        hidden_in, list(grads_low) + list(grads_high), grad_middle, qkv_weight, row(ln1_gain)
    )
    low, high, far_x, far_y, small_one = tie(low, high, far_x, far_y, small_one)
    small = jnp.concatenate(
        [small_one[:2], small_two[:2], jnp.pad(counts, (0, width - experts))[None], jnp.zeros((3, width), F32)], 0
    )
    low, high = reduce_both(low, high, 1)
    low, high, small, near_x, near_y = tie(low, high, small, near_x, near_y)
    last_x, last_y = across_x(near_x), across_y(near_y)
    small = sum_small(small)
    for step in range(2, len(low_order)):
        low, high = reduce_both(low, high, step)
    block_out = block_output(result_first, result_second, target_col, middle)
    low, high, last_x, last_y, block_out, small = tie(low, high, last_x, last_y, block_out, small)
    sums_x = [total_x, near_x, far_x, last_x]
    sums_y = [total_y, near_y, far_y, last_y]
    flags = jnp.stack([x_side, 1 - x_side, 2 + y_side, 3 - y_side, y_side, x_side]).astype(I32)
    grad_in, grad_out = assemble(flags, sums_x + sums_y)
    low, high = low.astype(BF), high.astype(BF)
    for step in (2, 1, 0):
        low, high = gather_step(low, *low_order[step]), gather_step(high, *high_order[step])
        if step == 1:
            low, high, grad_in, grad_out = tie(low, high, grad_in, grad_out)
    low, high = gather_step(low, "expert", 1), gather_step(high, "expert", 1)
    low = low.reshape(4, width, width // 2).astype(F32)
    high = high.reshape(4, width, width // 2).astype(F32)
    qkv_grad = jnp.concatenate([low[0], high[0], low[1], high[1], low[2], high[2]], 1)
    proj_sum = jnp.concatenate([low[3], high[3]], 1)
    load = small[4, :experts] * (experts / (tokens * devices))
    return (
        block_out,
        input_grad,
        small[0],
        small[1],
        qkv_grad,
        proj_sum,
        small[2],
        small[3],
        grad_in[None],
        grad_out[None],
        load,
    )


def solution(mesh):
    split, copied, owned = P(("dp", "expert")), P(), P("expert")
    in_specs = (
        split, split, copied, split, copied, copied, copied, copied, copied, copied, owned, owned, split,
    )
    out_specs = (
        split, split, copied, copied, copied, copied, copied, copied, owned, owned, copied,
    )
    return jax.shard_map(local, mesh=mesh, in_specs=in_specs, out_specs=out_specs, check_vma=False)
```

time: 1320 us -> 515 us (0.39)
  waiting for transfers between devices: 611 us -> 124 us
  matrix products: 367 us -> 0 us
  Pallas kernels: 0 us -> 226 us
  local copies, waits for them, and re-layouts: 148 us -> 51.8 us
  other arithmetic: 116 us -> 33.1 us
  starting transfers between devices: 19.9 us -> 71.4 us
  blocking collectives: 38.5 us -> 0 us
    dot_general x30 -> x0, matrix products: 367 us -> none  [the longest x6 62.2 us: contract_rows(): lax.dot_general(left, right, (((0,), (0,)), ((), ())), preferred_element_...]
    psum x2 -> x0, waiting for transfers between devices: 333 us -> none  [the longest x1 333 us: local(): lax.psum((contract_rows(arrived_flat, grad_inner), contract_rows(act_low,...]
    pallas_call x0 -> x17, Pallas kernels: none -> 226 us  [the longest x2 65.6 us: expert_rows(): pl.pallas_call(functools.partial(expert_kernel, 512, previous is not None...]
    all_to_all x4 -> x7, waiting for transfers between devices: 278 us -> 58.8 us  [exchange(): lax.all_to_all(sent, 'expert', split_axis=0, concat_axis=0, tiled=True)]
    ppermute x0 -> x35, waiting for transfers between devices: none -> 65.6 us  [the longest x6 19.6 us: reduce_step(): lax.ppermute(send.astype(BF), axis, partner(axis, bit)).astype(F32)]
    dynamic_update_slice x4 -> x0, local copies, waits for them, and re-layouts: 63.1 us -> none  [local(): lax.map(forward_block, (query_blocks, place_blocks, seg_blocks))]
    ppermute x0 -> x35, starting transfers between devices: none -> 39.1 us  [the longest x8 7.27 us: gather_step(): got = lax.ppermute(total, axis, partner(axis, bit))]
    psum x1 -> x0, blocking collectives: 38.5 us -> none  [local(): lax.psum((qkv_grad, proj_grad, gain_one_grad, bias_one_grad, gain_two_gra...]
  transfers between devices with their start and end apart: 6 -> 42, of which waited for: 5 -> 17; matrix products, arithmetic and copies ran while one was open for 9% -> 8% of each run, Pallas kernels for 0% -> 43%
where the time goes in v1:
time: 515 us; the launch traced here: 508 us
  Pallas kernels  226 us (44%)
  waiting for transfers between devices  124 us (24%)
  starting transfers between devices  71.4 us (14%)
  local copies, waits for them, and re-layouts  51.8 us (10%)
  other arithmetic  33.1 us (6%)
    pallas_call x2, Pallas kernels, expert_rows(): pl.pallas_call(functools.partial(expert_kernel, 512, previous is not None...  65.6 us
    all_to_all x7, waiting for transfers between devices, exchange(): lax.all_to_all(sent, 'expert', split_axis=0, concat_axis=0, tiled=True)  58.8 us
    unnamed x151, local copies, waits for them, and re-layouts  41.7 us
    all_to_all x7, starting transfers between devices, exchange(): lax.all_to_all(sent, 'expert', split_axis=0, concat_axis=0, tiled=True)  32.3 us
    pallas_call x2, Pallas kernels, attend_back(): pl.pallas_call(functools.partial(attend_back_kernel, 256, start), name='a...  28.8 us
    pallas_call x1, Pallas kernels, attend(): pl.pallas_call(functools.partial(attend_kernel, 256), name='attend', grid...  22.4 us
    ppermute x6, waiting for transfers between devices, reduce_step(): lax.ppermute(send.astype(BF), axis, partner(axis, bit)).astype(F32)  19.6 us
    pallas_call x2, Pallas kernels, shared_grads(): pl.pallas_call(shared_kernel, name='shared_grads', grid_spec=pltpu.Prefet...  19.4 us
  transfers between devices with their start and end apart: 42, of which 17 were waited for; matrix products, arithmetic and copies ran while one was open for 8% of the time, Pallas kernels for 43%

profile of v1, /device:TPU:0, one launch (start us, length us, event | category | flops | bytes accessed | tf_op | source)
XLA Modules:
  0.0 508.4 jit_solution(9611979606852527741)
XLA Ops:
  3.7 5.4 %route.1 = (s32[1,1024]{1,0:T(1,128)S(1)}, f32[16,128]{1,0:T(8,128)S(1)}, bf16[2048,768]{1,0:T(8,128)(2,1)S(1)}) custom-call(s32[1,1024]{1,0:T(1,128)S(1)} %bitcast.60, bf16[512,128]{1,0:T(8,128)(2,1)S(1)} %pad_bitcast_fusion.table_ref, bf16[1024,768]{1,0:T(8,128)(2,1)S(1)} %copy-done.18), custom_call_target="tpu_custom_call" | custom-call | flops 1 | bytes 1 | tf_op jit(solution)/shard_map/route/pallas_call | solution.py:91
  10.8 6.4 %all-to-all-start = ((bf16[8,256,768]{2,1,0:T(8,128)(2,1)}), bf16[8,256,768]{2,1,0:T(8,128)(2,1)S(1)}, u32[]{:S(2)}, u32[]{:S(2)}) async-start(bf16[8,256,768]{2,1,0:T(8,128)(2,1)} %bitcast.54), calls=%async_computation | async-start | bytes 6291456 | tf_op jit(solution)/shard_map/all_to_all | solution.py:760
  22.7 5.6 %norm_project.1 = (bf16[1024,2304]{1,0:T(8,128)(2,1)S(1)}, bf16[1024,768]{1,0:T(8,128)(2,1)S(1)}) custom-call(bf16[1024,768]{1,0:T(8,128)(2,1)S(1)} %copy-done.6, f32[1,768]{1,0:T(1,128)S(1)} %reshape.138.gain_ref.refs_8_, f32[1,768]{1,0:T(1,128)S(1)} %reshape.139.bias_ref, bf16[768,2304]{1,0:T(8,128)(2,1)S(1)} %copy-done.5, f32[1024,128]{1,0:T(8,128)S(1)} %copy-done.24, ...), custom_call_target="tpu_custom_call" | custom-call | flops 1 | bytes 1 | tf_op jit(solution)/shard_map/norm_project/pallas_call | solution.py:153
  36.1 22.4 %attend.1 = (bf16[1024,768]{1,0:T(8,128)(2,1)S(1)}, f32[128,1024]{1,0:T(8,128)S(1)}) custom-call(bf16[1024,2304]{1,0:T(8,128)(2,1)S(1)} %copy-done.1, bf16[1024,2304]{1,0:T(8,128)(2,1)S(1)} %copy-done.1, bf16[1024,2304]{1,0:T(8,128)(2,1)S(1)} %copy-done.1, s32[1,1024]{1,0:T(1,128)S(1)} %bitcast.56, s32[1024,1]{1,0:T(8,128)S(1)} %copy-done.10), custom_call_target="tpu_custom_call" | custom-call | flops 1 | bytes 1 | tf_op jit(solution)/shard_map/attend/pallas_call | solution.py:204
  59.3 6.6 %project_dispatch.1 = (f32[1024,768]{1,0:T(8,128)S(1)}, bf16[2048,768]{1,0:T(8,128)(2,1)S(1)}) custom-call(bf16[1024,768]{1,0:T(8,128)(2,1)S(1)} %get-tuple-element.108.mixed_ref, bf16[768,768]{1,0:T(8,128)(2,1)S(1)} %copy-done.32, bf16[1024,768]{1,0:T(8,128)(2,1)S(1)} %copy-done.7, f32[1,768]{1,0:T(1,128)S(1)} %reshape.142.gain_ref, ...), custom_call_target="tpu_custom_call" | custom-call | flops 1 | bytes 1 | tf_op jit(solution)/shard_map/project_dispatch/pallas_call | solution.py:240
  69.4 19.3 %all-to-all-done.grads_ref = bf16[8,256,768]{2,1,0:T(8,128)(2,1)S(1)} async-done(((bf16[8,256,768]{2,1,0:T(8,128)(2,1)}), bf16[8,256,768]{2,1,0:T(8,128)(2,1)S(1)}, u32[]{:S(2)}, u32[]{:S(2)}) %all-to-all-start) | async-done | bytes 3145760 | tf_op jit(solution)/shard_map/all_to_all | solution.py:760
  88.8 4.3 all-to-all-start.1
  93.1 14.7 %grads_inside.1.slope_ref = f32[2048,3072]{1,0:T(8,128)} custom-call(bf16[8,256,768]{2,1,0:T(8,128)(2,1)S(1)} %all-to-all-done.grads_ref, bf16[3072,768]{1,0:T(8,128)(2,1)} %bitcast.61), custom_call_target="tpu_custom_call" | custom-call | flops 1 | bytes 1 | tf_op jit(solution)/shard_map/grads_inside/pallas_call | solution.py:280
  107.7 23.2 %all-to-all-done.1 = bf16[8,128,768]{2,1,0:T(8,128)(2,1)} async-done(((bf16[8,128,768]{2,1,0:T(8,128)(2,1)}), bf16[8,128,768]{2,1,0:T(8,128)(2,1)}, u32[]{:S(2)}, u32[]{:S(2)}) %all-to-all-start.1) | async-done | bytes 1572896 | tf_op jit(solution)/shard_map/all_to_all | solution.py:760
  135.6 31.2 %expert_rows.2 = (f32[4,2,768,768]{3,2,1,0:T(8,128)}, bf16[1024,3072]{1,0:T(8,128)(2,1)}, bf16[1024,768]{1,0:T(8,128)(2,1)}) custom-call(s32[6]{0:T(128)} %stack.33.perm_ref, bf16[1024,768]{1,0:T(8,128)(2,1)} %bitcast.12.rows_ref, bf16[8,256,768]{2,1,0:T(8,128)(2,1)} %copy-done.2, f32[2048,3072]{1,0:T(8,128)} %grads_inside.1.slope_ref, ...), custom_call_target="tpu_custom_call" | custom-call | flops 1 | bytes 1 | tf_op jit(solution)/shard_map/expert_rows/pallas_call | solution.py:377
  166.8 5.9 %all-to-all-done.2 = bf16[8,128,768]{2,1,0:T(8,128)(2,1)S(1)} async-done(((bf16[8,128,768]{2,1,0:T(8,128)(2,1)}), bf16[8,128,768]{2,1,0:T(8,128)(2,1)S(1)}, u32[]{:S(2)}, u32[]{:S(2)}) %all-to-all-start.2) | async-done | bytes 1572896 | tf_op jit(solution)/shard_map/all_to_all | solution.py:760
  177.6 34.4 %expert_rows.3 = (bf16[768,768]{1,0:T(8,128)(2,1)}, bf16[768,768]{1,0:T(8,128)(2,1)}, bf16[768,768]{1,0:T(8,128)(2,1)}, bf16[768,768]{1,0:T(8,128)(2,1)}, bf16[2...) custom-call(s32[6]{0:T(128)} %stack.33.perm_ref, bf16[1024,768]{1,0:T(8,128)(2,1)} %bitcast.70, ...), custom_call_target="tpu_custom_call" | custom-call | flops 1 | bytes 1 | tf_op jit(solution)/shard_map/expert_rows/pallas_call | solution.py:377
  224.4 8.2 %expert_result.2 = bf16[1024,768]{1,0:T(8,128)(2,1)S(1)} custom-call(bf16[1024,3072]{1,0:T(8,128)(2,1)} %get-tuple-element.124.act_ref, bf16[3072,768]{1,0:T(8,128)(2,1)} %bitcast.62), custom_call_target="tpu_custom_call" | custom-call | flops 1 | bytes 1 | tf_op jit(solution)/shard_map/expert_result/pallas_call | solution.py:413
  233.7 9.3 %expert_result.3 = bf16[1024,768]{1,0:T(8,128)(2,1)} custom-call(bf16[1024,3072]{1,0:T(8,128)(2,1)} %get-tuple-element.125.act_ref, bf16[3072,768]{1,0:T(8,128)(2,1)} %bitcast.63), custom_call_target="tpu_custom_call" | custom-call | flops 1 | bytes 1 | tf_op jit(solution)/shard_map/expert_result/pallas_call | solution.py:413
  243.0 6.3 %collective-permute-done = bf16[768,768]{1,0:T(8,128)(2,1)S(1)} collective-permute-done((bf16[768,768]{1,0:T(8,128)(2,1)}, bf16[768,768]{1,0:T(8,128)(2,1)S(1)}, u32[]{:S(2)}, u32[]{:S(2)}) %collective-permute-start) | collective-permute-done | bytes 1179680 | tf_op jit(solution)/shard_map/ppermute | solution.py:792
  250.9 7.1 %all-to-all-done.4 = bf16[8,128,768]{2,1,0:T(8,128)(2,1)S(1)} async-done(((bf16[8,128,768]{2,1,0:T(8,128)(2,1)}), bf16[8,128,768]{2,1,0:T(8,128)(2,1)S(1)}, u32[]{:S(2)}, u32[]{:S(2)}) %all-to-all-start.4) | async-done | bytes 1572896 | tf_op jit(solution)/shard_map/all_to_all | solution.py:760
  266.6 13.0 %middle_back.1 = (f32[1024,768]{1,0:T(8,128)}, bf16[1024,768]{1,0:T(8,128)(2,1)S(1)}, bf16[1024,768]{1,0:T(8,128)(2,1)S(1)}, f32[16,1024]{1,0:T(8,128)S(1)}, f32[8,768]{1,0:T(8,128)S(1)}) custom-call(bf16[1024,768]{1,0:T(8,128)(2,1)} %bitcast.73, bf16[1024,768]{1,0:T(8,128)(2,1)} %bitcast.74, s32[1024,1]{1,0:T(8,128)S(1)} %copy.28.target_ref, ...), custom_call_target="tpu_custom_call" | custom-call | flops 1 | bytes 1 | tf_op jit(solution)/shard_map/middle_back/pallas_call | solution.py:520
  280.8 4.8 all-to-all-start.5
  288.0 14.5 %attend_back.2 = (bf16[1024,384]{1,0:T(8,128)(2,1)S(1)}, bf16[1024,384]{1,0:T(8,128)(2,1)S(1)}, bf16[1024,384]{1,0:T(8,128)(2,1)S(1)}) custom-call(bf16[1024,2304]{1,0:T(8,128)(2,1)} %copy-done, bf16[1024,2304]{1,0:T(8,128)(2,1)} %copy-done, bf16[1024,2304]{1,0:T(8,128)(2,1)} %copy-done, bf16[1024,768]{1,0:T(8,128)(2,1)S(1)} %copy-done.15, ...), custom_call_target="tpu_custom_call" | custom-call | flops 1 | bytes 1 | tf_op jit(solution)/shard_map/attend_back/pallas_call | solution.py:589
  302.6 5.1 %shared_grads.2 = (f32[2,768,384]{2,1,0:T(8,128)S(1)}, bf16[2,768,384]{2,1,0:T(8,128)(2,1)}) custom-call(s32[1]{0:T(128)} %bitcast.side_ref, bf16[1024,768]{1,0:T(8,128)(2,1)S(1)} %copy-done.13, bf16[1024,384]{1,0:T(8,128)(2,1)S(1)} %get-tuple-element.141.dq_ref.refs_0_, bf16[1024,384]{1,0:T(8,128)(2,1)S(1)} %get-tuple-element.142.dk_ref.refs_1_, ...), custom_call_target="tpu_custom_call" | custom-call | flops 1 | bytes 1 | tf_op jit(solution)/shard_map/shared_grads/pallas_call | solution.py:620
  307.8 4.8 fusion.3
  313.7 14.4 %attend_back.3 = (bf16[1024,384]{1,0:T(8,128)(2,1)S(1)}, bf16[1024,384]{1,0:T(8,128)(2,1)S(1)}, bf16[1024,384]{1,0:T(8,128)(2,1)S(1)}) custom-call(bf16[1024,2304]{1,0:T(8,128)(2,1)} %copy-done, bf16[1024,2304]{1,0:T(8,128)(2,1)} %copy-done, bf16[1024,2304]{1,0:T(8,128)(2,1)} %copy-done, bf16[1024,768]{1,0:T(8,128)(2,1)S(1)} %copy-done.16, ...), custom_call_target="tpu_custom_call" | custom-call | flops 1 | bytes 1 | tf_op jit(solution)/shard_map/attend_back/pallas_call | solution.py:589
  328.1 14.2 %shared_grads.3 = (f32[2,768,384]{2,1,0:T(8,128)S(1)}, bf16[2,768,384]{2,1,0:T(8,128)(2,1)S(1)}) custom-call(s32[1]{0:T(128)} %bitcast.side_ref, bf16[1024,768]{1,0:T(8,128)(2,1)S(1)} %copy-done.13, bf16[1024,384]{1,0:T(8,128)(2,1)S(1)} %get-tuple-element.158.dq_ref.refs_3_, bf16[1024,384]{1,0:T(8,128)(2,1)S(1)} %get-tuple-element.159.dk_ref.refs_4_, ...), custom_call_target="tpu_custom_call" | custom-call | flops 1 | bytes 1 | tf_op jit(solution)/shard_map/shared_grads/pallas_call | solution.py:620
  346.4 5.2 %all-to-all-start.6 = ((bf16[8,128,768]{2,1,0:T(8,128)(2,1)}), bf16[8,128,768]{2,1,0:T(8,128)(2,1)}, u32[]{:S(2)}, u32[]{:S(2)}) async-start(bf16[8,128,768]{2,1,0:T(8,128)(2,1)} %bitcast.30), calls=%async_computation.6 | async-start | bytes 3145728 | tf_op jit(solution)/shard_map/all_to_all | solution.py:760
  368.8 10.2 %first_back.1 = (f32[1024,768]{1,0:T(8,128)}, f32[8,768]{1,0:T(8,128)S(1)}) custom-call(bf16[1024,768]{1,0:T(8,128)(2,1)} %x_ref.2, bf16[1024,384]{1,0:T(8,128)(2,1)S(1)} %copy-done.35, bf16[1024,384]{1,0:T(8,128)(2,1)S(1)} %copy-done.37, bf16[1024,384]{1,0:T(8,128)(2,1)S(1)} %copy-done.39, bf16[1024,384]{1,0:T(8,128)(2,1)S(1)} %copy-done.41, ...), custom_call_target="tpu_custom_call" | custom-call | flops 1 | bytes 1 | tf_op jit(solution)/shard_map/first_back/pallas_call | solution.py:671
  379.0 13.8 %collective-permute-done.9 = bf16[4,192,384]{2,1,0:T(8,128)(2,1)} collective-permute-done((bf16[4,192,384]{2,1,0:T(8,128)(2,1)}, bf16[4,192,384]{2,1,0:T(8,128)(2,1)}, u32[]{:S(2)}, u32[]{:S(2)}) %collective-permute-start.9) | collective-permute-done | bytes 589856 | tf_op jit(solution)/shard_map/ppermute | solution.py:731
  398.4 5.4 %collective-permute-done.15 = bf16[2,192,384]{2,1,0:T(8,128)(2,1)S(1)} collective-permute-done((bf16[2,192,384]{2,1,0:T(8,128)(2,1)S(1)}, bf16[2,192,384]{2,1,0:T(8,128)(2,1)S(1)}, u32[]{:S(2)}, u32[]{:S(2)}) %collective-permute-start.15) | collective-permute-done | bytes 294944 | tf_op jit(solution)/shard_map/ppermute | solution.py:731
  418.6 6.9 %block_output.1 = bf16[1024,768]{1,0:T(8,128)(2,1)} custom-call(bf16[1024,768]{1,0:T(8,128)(2,1)} %bitcast.27.first_ref, bf16[1024,768]{1,0:T(8,128)(2,1)} %bitcast.31.second_ref, s32[1024,1]{1,0:T(8,128)S(1)} %copy-done.31, f32[1024,768]{1,0:T(8,128)S(1)} %copy-done.9), custom_call_target="tpu_custom_call" | custom-call | flops 1 | bytes 1 | tf_op jit(solution)/shard_map/block_output/pallas_call | solution.py:695
  425.5 11.6 %collective-permute-done.25 = f32[8,768]{1,0:T(8,128)S(1)} collective-permute-done((f32[8,768]{1,0:T(8,128)S(1)}, f32[8,768]{1,0:T(8,128)S(1)}, u32[]{:S(2)}, u32[]{:S(2)}) %collective-permute-start.25) | collective-permute-done | bytes 24608 | tf_op jit(solution)/shard_map/ppermute | solution.py:741
  447.6 7.6 %collective-permute-done.19 = bf16[1,192,384]{2,1,0:T(8,128)(2,1)S(1)} collective-permute-done((bf16[1,192,384]{2,1,0:T(8,128)(2,1)S(1)}, bf16[1,192,384]{2,1,0:T(8,128)(2,1)S(1)}, u32[]{:S(2)}, u32[]{:S(2)}) %collective-permute-start.19) | collective-permute-done | bytes 147488 | tf_op jit(solution)/shard_map/ppermute | solution.py:726
  471.0 10.2 %assemble.1 = (f32[768,3072]{1,0:T(8,128)}, f32[3072,768]{1,0:T(8,128)}) custom-call(s32[6]{0:T(128)S(1)} %stack.34.flags_ref, bf16[768,768]{1,0:T(8,128)(2,1)S(1)} %copy-done.23, bf16[768,768]{1,0:T(8,128)(2,1)S(1)} %copy-done.54, bf16[768,768]{1,0:T(8,128)(2,1)} %collective-permute-done.12.refs_2_, bf16[768,768]{1,0:T(8,128)(2,1)} %collective-permute-done.20.refs_3_, ...), custom_call_target="tpu_custom_call" | custom-call | flops 1 | bytes 1 | tf_op jit(solution)/shard_map/assemble/pallas_call | solution.py:446
  485.0 11.0 %collective-permute-done.33 = bf16[4,192,384]{2,1,0:T(8,128)(2,1)S(1)} collective-permute-done((bf16[4,192,384]{2,1,0:T(8,128)(2,1)S(1)}, bf16[4,192,384]{2,1,0:T(8,128)(2,1)S(1)}, u32[]{:S(2)}, u32[]{:S(2)}) %collective-permute-start.33) | collective-permute-done | bytes 589856 | tf_op jit(solution)/shard_map/ppermute | solution.py:735
  (276 shorter events, 144.1 us)
Async XLA Ops:
  10.8 78.0 %all-to-all-start = ((bf16[8,256,768]{2,1,0:T(8,128)(2,1)}), bf16[8,256,768]{2,1,0:T(8,128)(2,1)S(1)}, u32[]{:S(2)}, u32[]{:S(2)}) async-start(bf16[8,256,768]{2,1,0:T(8,128)(2,1)} %bitcast.54), calls=%async_computation | async-start | bytes 6291456 | tf_op jit(solution)/shard_map/all_to_all | solution.py:760
  88.8 42.1 %all-to-all-start.1 = ((bf16[8,128,768]{2,1,0:T(8,128)(2,1)}), bf16[8,128,768]{2,1,0:T(8,128)(2,1)}, u32[]{:S(2)}, u32[]{:S(2)}) async-start(bf16[8,128,768]{2,1,0:T(8,128)(2,1)} %bitcast.72), calls=%async_computation.1 | async-start | bytes 3145728 | tf_op jit(solution)/shard_map/all_to_all | solution.py:760
  130.9 41.8 %all-to-all-start.2 = ((bf16[8,128,768]{2,1,0:T(8,128)(2,1)}), bf16[8,128,768]{2,1,0:T(8,128)(2,1)S(1)}, u32[]{:S(2)}, u32[]{:S(2)}) async-start(bf16[8,128,768]{2,1,0:T(8,128)(2,1)} %bitcast.71), calls=%async_computation.2 | async-start | bytes 3145728 | tf_op jit(solution)/shard_map/all_to_all | solution.py:760
  173.8 41.5 %all-to-all-start.3 = ((bf16[8,128,768]{2,1,0:T(8,128)(2,1)}), bf16[8,128,768]{2,1,0:T(8,128)(2,1)S(1)}, u32[]{:S(2)}, u32[]{:S(2)}) async-start(bf16[8,128,768]{2,1,0:T(8,128)(2,1)} %bitcast.84), calls=%async_computation.3 | async-start | bytes 3145728 | tf_op jit(solution)/shard_map/all_to_all | solution.py:760
  216.5 41.5 %all-to-all-start.4 = ((bf16[8,128,768]{2,1,0:T(8,128)(2,1)}), bf16[8,128,768]{2,1,0:T(8,128)(2,1)S(1)}, u32[]{:S(2)}, u32[]{:S(2)}) async-start(bf16[8,128,768]{2,1,0:T(8,128)(2,1)} %bitcast.83), calls=%async_computation.4 | async-start | bytes 3145728 | tf_op jit(solution)/shard_map/all_to_all | solution.py:760
  220.3 29.0 %collective-permute-start = (bf16[768,768]{1,0:T(8,128)(2,1)}, bf16[768,768]{1,0:T(8,128)(2,1)S(1)}, u32[]{:S(2)}, u32[]{:S(2)}) collective-permute-start(bf16[768,768]{1,0:T(8,128)(2,1)} %get-tuple-element.127), channel_id=1, source_target_pairs={{0,8},{8,0},{16,24},{24,16},{1,9},{9,1},{17,25},{25,17},{2,10},{10... | collective-permute-start | bytes 3538952 | tf_op jit(solution)/shard_map/ppermute | solution.py:792
  221.8 29.1 %collective-permute-start.1 = (bf16[768,768]{1,0:T(8,128)(2,1)}, bf16[768,768]{1,0:T(8,128)(2,1)}, u32[]{:S(2)}, u32[]{:S(2)}) collective-permute-start(bf16[768,768]{1,0:T(8,128)(2,1)} %get-tuple-element.128), channel_id=1, source_target_pairs={{0,16},{8,24},{16,0},{24,8},{1,17},{9,25},{17,1},{25,9},{2,18},{10... | collective-permute-start | bytes 3538952 | tf_op jit(solution)/shard_map/ppermute | solution.py:793
  223.3 57.4 %collective-permute-start.2 = (bf16[768,768]{1,0:T(8,128)(2,1)}, bf16[768,768]{1,0:T(8,128)(2,1)}, u32[]{:S(2)}, u32[]{:S(2)}) collective-permute-start(bf16[768,768]{1,0:T(8,128)(2,1)} %get-tuple-element.135), channel_id=1, source_target_pairs={{0,8},{8,0},{16,24},{24,16},{1,9},{9,1},{17,25},{25,17},{2,10},{10... | collective-permute-start | bytes 3538952 | tf_op jit(solution)/shard_map/ppermute | solution.py:792
  223.9 56.9 %collective-permute-start.3 = (bf16[768,768]{1,0:T(8,128)(2,1)}, bf16[768,768]{1,0:T(8,128)(2,1)}, u32[]{:S(2)}, u32[]{:S(2)}) collective-permute-start(bf16[768,768]{1,0:T(8,128)(2,1)} %get-tuple-element.136), channel_id=1, source_target_pairs={{0,16},{8,24},{16,0},{24,8},{1,17},{9,25},{17,1},{25,9},{2,18},{10... | collective-permute-start | bytes 3538952 | tf_op jit(solution)/shard_map/ppermute | solution.py:793
  263.3 44.4 %collective-permute-start.4 = (bf16[768,768]{1,0:T(8,128)(2,1)}, bf16[768,768]{1,0:T(8,128)(2,1)}, u32[]{:S(2)}, u32[]{:S(2)}) collective-permute-start(bf16[768,768]{1,0:T(8,128)(2,1)} %get-tuple-element.147), channel_id=1, source_target_pairs={{0,16},{8,24},{16,0},{24,8},{1,17},{9,25},{17,1},{25,9},{2,18},{10... | collective-permute-start | bytes 3538952 | tf_op jit(solution)/shard_map/ppermute | solution.py:793
  264.8 42.9 %collective-permute-start.5 = (bf16[768,768]{1,0:T(8,128)(2,1)}, bf16[768,768]{1,0:T(8,128)(2,1)}, u32[]{:S(2)}, u32[]{:S(2)}) collective-permute-start(bf16[768,768]{1,0:T(8,128)(2,1)} %get-tuple-element.148), channel_id=1, source_target_pairs={{0,8},{8,0},{16,24},{24,16},{1,9},{9,1},{17,25},{25,17},{2,10},{10... | collective-permute-start | bytes 3538952 | tf_op jit(solution)/shard_map/ppermute | solution.py:792
  280.8 65.2 %all-to-all-start.5 = ((bf16[8,128,768]{2,1,0:T(8,128)(2,1)}), bf16[8,128,768]{2,1,0:T(8,128)(2,1)}, u32[]{:S(2)}, u32[]{:S(2)}) async-start(bf16[8,128,768]{2,1,0:T(8,128)(2,1)} %bitcast.53), calls=%async_computation.5 | async-start | bytes 3145728 | tf_op jit(solution)/shard_map/all_to_all | solution.py:760
  312.6 32.3 %collective-permute-start.6 = (bf16[768,768]{1,0:T(8,128)(2,1)S(1)}, bf16[768,768]{1,0:T(8,128)(2,1)S(1)}, u32[]{:S(2)}, u32[]{:S(2)}) collective-permute-start(bf16[768,768]{1,0:T(8,128)(2,1)S(1)} %get-tuple-element.154.refs_0_), channel_id=1, source_target_pairs={{0,16},{8,24},{16,0},{24,8},{1,17},{9,25},{17,1},{25,9},{2,18},{10... | collective-permute-start | bytes 3538952 | tf_op jit(solution)/shard_map/ppermute | solution.py:793
  313.1 31.7 %collective-permute-start.7 = (bf16[768,768]{1,0:T(8,128)(2,1)S(1)}, bf16[768,768]{1,0:T(8,128)(2,1)}, u32[]{:S(2)}, u32[]{:S(2)}) collective-permute-start(bf16[768,768]{1,0:T(8,128)(2,1)S(1)} %get-tuple-element.155.refs_4_), channel_id=1, source_target_pairs={{0,8},{8,0},{16,24},{24,16},{1,9},{9,1},{17,25},{25,17},{2,10},{10... | collective-permute-start | bytes 3538952 | tf_op jit(solution)/shard_map/ppermute | solution.py:792
  313.7 32.3 %collective-permute-start.8 = (bf16[2,768,384]{2,1,0:T(8,128)(2,1)}, bf16[2,768,384]{2,1,0:T(8,128)(2,1)}, u32[]{:S(2)}, u32[]{:S(2)}) collective-permute-start(bf16[2,768,384]{2,1,0:T(8,128)(2,1)} %get-tuple-element.156), channel_id=1, source_target_pairs={{0,1},{1,0},{2,3},{3,2},{4,5},{5,4},{6,7},{7,6},{8,9},{9,8},{10,11... | collective-permute-start | bytes 3538952 | tf_op jit(solution)/shard_map/ppermute | solution.py:819
  345.9 12.7 %collective-permute-start.10 = (bf16[2,768,384]{2,1,0:T(8,128)(2,1)}, bf16[2,768,384]{2,1,0:T(8,128)(2,1)}, u32[]{:S(2)}, u32[]{:S(2)}) collective-permute-start(bf16[2,768,384]{2,1,0:T(8,128)(2,1)} %copy-done.58), channel_id=1, source_target_pairs={{0,1},{1,0},{2,3},{3,2},{4,5},{5,4},{6,7},{7,6},{8,9},{9,8},{10,11... | collective-permute-start | bytes 3538952 | tf_op jit(solution)/shard_map/ppermute | solution.py:819
  346.4 71.1 %all-to-all-start.6 = ((bf16[8,128,768]{2,1,0:T(8,128)(2,1)}), bf16[8,128,768]{2,1,0:T(8,128)(2,1)}, u32[]{:S(2)}, u32[]{:S(2)}) async-start(bf16[8,128,768]{2,1,0:T(8,128)(2,1)} %bitcast.30), calls=%async_computation.6 | async-start | bytes 3145728 | tf_op jit(solution)/shard_map/all_to_all | solution.py:760
  351.6 43.5 %collective-permute-start.12 = (bf16[768,768]{1,0:T(8,128)(2,1)S(1)}, bf16[768,768]{1,0:T(8,128)(2,1)}, u32[]{:S(2)}, u32[]{:S(2)}) collective-permute-start(bf16[768,768]{1,0:T(8,128)(2,1)S(1)} %copy-done.22), channel_id=1, source_target_pairs={{0,8},{8,0},{16,24},{24,16},{1,9},{9,1},{17,25},{25,17},{2,10},{10... | collective-permute-start | bytes 3538952 | tf_op jit(solution)/shard_map/ppermute | solution.py:792
  353.2 42.0 %collective-permute-start.13 = (bf16[768,768]{1,0:T(8,128)(2,1)S(1)}, bf16[768,768]{1,0:T(8,128)(2,1)}, u32[]{:S(2)}, u32[]{:S(2)}) collective-permute-start(bf16[768,768]{1,0:T(8,128)(2,1)S(1)} %get-tuple-element.155.refs_4_), channel_id=1, source_target_pairs={{0,16},{8,24},{16,0},{24,8},{1,17},{9,25},{17,1},{25,9},{2,18},{10... | collective-permute-start | bytes 3538952 | tf_op jit(solution)/shard_map/ppermute | solution.py:793
  358.0 34.7 %collective-permute-start.9 = (bf16[4,192,384]{2,1,0:T(8,128)(2,1)}, bf16[4,192,384]{2,1,0:T(8,128)(2,1)}, u32[]{:S(2)}, u32[]{:S(2)}) collective-permute-start(bf16[4,192,384]{2,1,0:T(8,128)(2,1)} %dynamic-slice_convert_fusion.1), channel_id=1, source_target_pairs={{0,8},{8,0},{16,24},{24,16},{1,9},{9,1},{17,25},{25,17},{2,10},{10... | collective-permute-start | bytes 1769480 | tf_op jit(solution)/shard_map/ppermute | solution.py:731
  362.4 31.5 %collective-permute-start.11 = (bf16[4,192,384]{2,1,0:T(8,128)(2,1)}, bf16[4,192,384]{2,1,0:T(8,128)(2,1)}, u32[]{:S(2)}, u32[]{:S(2)}) collective-permute-start(bf16[4,192,384]{2,1,0:T(8,128)(2,1)} %dynamic-slice_convert_fusion), channel_id=1, source_target_pairs={{0,16},{8,24},{16,0},{24,8},{1,17},{9,25},{17,1},{25,9},{2,18},{10... | collective-permute-start | bytes 1769480 | tf_op jit(solution)/shard_map/ppermute | solution.py:731
  408.6 48.9 %collective-permute-start.20 = (bf16[768,768]{1,0:T(8,128)(2,1)}, bf16[768,768]{1,0:T(8,128)(2,1)}, u32[]{:S(2)}, u32[]{:S(2)}) collective-permute-start(bf16[768,768]{1,0:T(8,128)(2,1)} %copy-done.53), channel_id=1, source_target_pairs={{0,8},{8,0},{16,24},{24,16},{1,9},{9,1},{17,25},{25,17},{2,10},{10... | collective-permute-start | bytes 3538952 | tf_op jit(solution)/shard_map/ppermute | solution.py:792
  409.6 47.9 %collective-permute-start.21 = (bf16[768,768]{1,0:T(8,128)(2,1)}, bf16[768,768]{1,0:T(8,128)(2,1)}, u32[]{:S(2)}, u32[]{:S(2)}) collective-permute-start(bf16[768,768]{1,0:T(8,128)(2,1)} %collective-permute-done.7.refs_5_), channel_id=1, source_target_pairs={{0,16},{8,24},{16,0},{24,8},{1,17},{9,25},{17,1},{25,9},{2,18},{10... | collective-permute-start | bytes 3538952 | tf_op jit(solution)/shard_map/ppermute | solution.py:793
  415.2 26.3 %collective-permute-start.18 = (bf16[1,192,384]{2,1,0:T(8,128)(2,1)}, bf16[1,192,384]{2,1,0:T(8,128)(2,1)}, u32[]{:S(2)}, u32[]{:S(2)}) collective-permute-start(bf16[1,192,384]{2,1,0:T(8,128)(2,1)} %dynamic-slice_convert_fusion.4), channel_id=1, source_target_pairs={{0,2},{1,3},{2,0},{3,1},{4,6},{5,7},{6,4},{7,5},{8,10},{9,11},{10,... | collective-permute-start | bytes 442376 | tf_op jit(solution)/shard_map/ppermute | solution.py:731
  416.4 20.6 %collective-permute-start.25 = (f32[8,768]{1,0:T(8,128)S(1)}, f32[8,768]{1,0:T(8,128)S(1)}, u32[]{:S(2)}, u32[]{:S(2)}) collective-permute-start(f32[8,768]{1,0:T(8,128)S(1)} %add.167), channel_id=1, source_target_pairs={{0,8},{8,0},{16,24},{24,16},{1,9},{9,1},{17,25},{25,17},{2,10},{10... | collective-permute-start | bytes 73736 | tf_op jit(solution)/shard_map/ppermute | solution.py:741
  442.6 12.6 %collective-permute-start.19 = (bf16[1,192,384]{2,1,0:T(8,128)(2,1)S(1)}, bf16[1,192,384]{2,1,0:T(8,128)(2,1)S(1)}, u32[]{:S(2)}, u32[]{:S(2)}) collective-permute-start(bf16[1,192,384]{2,1,0:T(8,128)(2,1)S(1)} %add_convert_fusion), channel_id=1, source_target_pairs={{0,4},{1,5},{2,6},{3,7},{4,0},{5,1},{6,2},{7,3},{8,12},{9,13},{10,... | collective-permute-start | bytes 442376 | tf_op jit(solution)/shard_map/ppermute | solution.py:726
  445.1 11.7 %collective-permute-start.17 = (bf16[1,192,384]{2,1,0:T(8,128)(2,1)S(1)}, bf16[1,192,384]{2,1,0:T(8,128)(2,1)S(1)}, u32[]{:S(2)}, u32[]{:S(2)}) collective-permute-start(bf16[1,192,384]{2,1,0:T(8,128)(2,1)S(1)} %add_convert_fusion.1), channel_id=1, source_target_pairs={{0,4},{1,5},{2,6},{3,7},{4,0},{5,1},{6,2},{7,3},{8,12},{9,13},{10,... | collective-permute-start | bytes 442376 | tf_op jit(solution)/shard_map/ppermute | solution.py:726
  457.5 9.1 %collective-permute-start.27 = (bf16[1,192,384]{2,1,0:T(8,128)(2,1)}, bf16[1,192,384]{2,1,0:T(8,128)(2,1)}, u32[]{:S(2)}, u32[]{:S(2)}) collective-permute-start(bf16[1,192,384]{2,1,0:T(8,128)(2,1)} %convert_add_fusion.11), channel_id=1, source_target_pairs={{0,2},{1,3},{2,0},{3,1},{4,6},{5,7},{6,4},{7,5},{8,10},{9,11},{10,... | collective-permute-start | bytes 442376 | tf_op jit(solution)/shard_map/ppermute | solution.py:735
  465.5 15.7 %collective-permute-start.30 = (bf16[2,192,384]{2,1,0:T(8,128)(2,1)}, bf16[2,192,384]{2,1,0:T(8,128)(2,1)}, u32[]{:S(2)}, u32[]{:S(2)}) collective-permute-start(bf16[2,192,384]{2,1,0:T(8,128)(2,1)} %maximum_select_fusion.7), channel_id=1, source_target_pairs={{0,8},{8,0},{16,24},{24,16},{1,9},{9,1},{17,25},{25,17},{2,10},{10... | collective-permute-start | bytes 884744 | tf_op jit(solution)/shard_map/ppermute | solution.py:735
  468.4 14.1 %collective-permute-start.28 = (bf16[2,192,384]{2,1,0:T(8,128)(2,1)}, bf16[2,192,384]{2,1,0:T(8,128)(2,1)}, u32[]{:S(2)}, u32[]{:S(2)}) collective-permute-start(bf16[2,192,384]{2,1,0:T(8,128)(2,1)} %maximum_select_fusion.6), channel_id=1, source_target_pairs={{0,16},{8,24},{16,0},{24,8},{1,17},{9,25},{17,1},{25,9},{2,18},{10... | collective-permute-start | bytes 884744 | tf_op jit(solution)/shard_map/ppermute | solution.py:735
  483.9 12.2 %collective-permute-start.33 = (bf16[4,192,384]{2,1,0:T(8,128)(2,1)S(1)}, bf16[4,192,384]{2,1,0:T(8,128)(2,1)S(1)}, u32[]{:S(2)}, u32[]{:S(2)}) collective-permute-start(bf16[4,192,384]{2,1,0:T(8,128)(2,1)S(1)} %maximum_select_fusion.5), channel_id=1, source_target_pairs={{0,16},{8,24},{16,0},{24,8},{1,17},{9,25},{17,1},{25,9},{2,18},{10... | collective-permute-start | bytes 1769480 | tf_op jit(solution)/shard_map/ppermute | solution.py:735
  483.9 12.4 %collective-permute-start.31 = (bf16[4,192,384]{2,1,0:T(8,128)(2,1)S(1)}, bf16[4,192,384]{2,1,0:T(8,128)(2,1)S(1)}, u32[]{:S(2)}, u32[]{:S(2)}) collective-permute-start(bf16[4,192,384]{2,1,0:T(8,128)(2,1)S(1)} %maximum_select_fusion.4), channel_id=1, source_target_pairs={{0,8},{8,0},{16,24},{24,16},{1,9},{9,1},{17,25},{25,17},{2,10},{10... | collective-permute-start | bytes 1769480 | tf_op jit(solution)/shard_map/ppermute | solution.py:735
  (83 other events, 641.9 us)

commit v2 on v1

--- a/solution.py
+++ b/solution.py
@@ -55,7 +55,7 @@
     return (iota((count, target.shape[1]), 0) + first == target).astype(F32).astype(BF)
 
 
-def route_kernel(experts, half, block, ids_ref, table_ref, grad_ref, target_ref, counts_ref, sent_ref, place):
+def route_kernel(experts, half, block, ids_ref, table_ref, grad_ref, target_ref, place, counts_ref, sent_ref):
     tokens = ids_ref.shape[1]
     rows = table_ref.shape[0]
     padded = counts_ref.shape[0]
@@ -88,26 +88,27 @@
     padded = max(experts, 16)
     rows = -(-hash_table.shape[0] // (128 * 128)) * 128
     table = jnp.pad(hash_table, (0, rows * 128 - hash_table.shape[0])).reshape(rows, 128).astype(BF)
-    target, counts, sent = pl.pallas_call(
+    target, place, counts, sent = pl.pallas_call(
         functools.partial(route_kernel, experts, half, block),
         name="route",
         grid=(slots // block,),
         in_specs=[whole((1, tokens)), whole((rows, 128)), whole((tokens, width))],
         out_specs=[
             whole((1, tokens)),
+            whole((1, tokens)),
             whole((padded, 128)),
             pl.BlockSpec((block, width), lambda s: (s, 0)),
         ],
         out_shape=[
+            jax.ShapeDtypeStruct((1, tokens), I32),
             jax.ShapeDtypeStruct((1, tokens), I32),
             jax.ShapeDtypeStruct((padded, 128), F32),
             jax.ShapeDtypeStruct((slots, width), BF),
         ],
-        scratch_shapes=[pltpu.VMEM((1, tokens), I32)],
-        compiler_params=params(40),
+        compiler_params=params(62),
         cost_estimate=cost(2 * slots * tokens * width, 8 * tokens * width),
     )(token_ids.reshape(1, tokens), table, out_grad)
-    return target, counts[:experts, 0], sent
+    return target, place, counts[:experts, 0], sent
 
 
 def swap_halves(rows):
@@ -162,7 +163,7 @@
             jax.ShapeDtypeStruct((tokens, 3 * width), BF),
             jax.ShapeDtypeStruct((tokens, width), BF),
         ],
-        compiler_params=params(40),
+        compiler_params=params(62),
         cost_estimate=cost(6 * tokens * width * width, 6 * width * width + 12 * tokens * width),
     )(x, gain, bias, weight, cosine, sine)
 
@@ -212,7 +213,7 @@
             jax.ShapeDtypeStruct((128, tokens), F32),
         ],
         scratch_shapes=[pltpu.VMEM((tokens, 128), F32)],
-        compiler_params=params(40),
+        compiler_params=params(62),
         cost_estimate=cost(8 * tokens * tokens * width, 8 * tokens * width, tokens * tokens * width // HEAD),
     )(qkv, qkv, qkv, seg_row, seg_col)
 
@@ -251,7 +252,7 @@
             jax.ShapeDtypeStruct((slots, width), BF),
         ],
         scratch_shapes=[pltpu.VMEM((tokens, width), BF)],
-        compiler_params=params(40),
+        compiler_params=params(62),
         cost_estimate=cost(2 * slots * tokens * width + 2 * tokens * width * width, 16 * tokens * width),
     )(mixed, weight, x, gain, bias, target)
 
@@ -284,7 +285,7 @@
         in_specs=[once(grads.shape), pl.BlockSpec((tile, width), lambda s: (s, 0))],
         out_specs=pl.BlockSpec((count, tile), lambda s: (0, s)),
         out_shape=jax.ShapeDtypeStruct((count, units), F32),
-        compiler_params=params(48),
+        compiler_params=params(62),
         cost_estimate=cost(2 * count * width * units, 4 * count * units),
     )(grads, weight_out)
 
@@ -387,81 +388,95 @@
         ),
         out_shape=grad_shapes
         + [jax.ShapeDtypeStruct((count, units), BF), jax.ShapeDtypeStruct((count, width), BF)],
-        compiler_params=params(60),
+        compiler_params=params(62),
         cost_estimate=cost(8 * count * width * units, 12 * width * units + 6 * count * units, count * units),
     )(perm, *operands)
 
 
-def result_kernel(act_ref, wout_ref, out_ref, total):
+def result_kernel(first_ref, second_ref, wout_ref, out_ref, total):
     step = pl.program_id(0)
+    experts, rows, width = out_ref.shape
+    half = rows // 2
 
     @pl.when(step == 0)
     def _():
         total[...] = jnp.zeros_like(total)
 
-    total[...] += dot(act_ref[...], wout_ref[...])
+    weight_out = wout_ref[...]
+    total[0] += dot(first_ref[...], weight_out)
+    total[1] += dot(second_ref[...], weight_out)
 
     @pl.when(step == pl.num_programs(0) - 1)
     def _():
-        out_ref[...] = total[...].astype(BF)
-
-
-def expert_result(act, weight_out):
-    count, units = act.shape
+        for chunk in range(2):
+            out_ref[:, chunk * half : (chunk + 1) * half, :] = (
+                total[chunk].astype(BF).reshape(experts, half, width)
+            )
+
+
+def expert_result(first, second, weight_out, experts):
+    count, units = first.shape
     width = weight_out.shape[1]
     tile = 768
+    col = pl.BlockSpec((count, tile), lambda s: (0, s))
+    shape = (experts, 2 * count // experts, width)
     return pl.pallas_call(
         result_kernel,
         name="expert_result",
         grid=(units // tile,),
-        in_specs=[pl.BlockSpec((count, tile), lambda s: (0, s)), pl.BlockSpec((tile, width), lambda s: (s, 0))],
-        out_specs=whole((count, width)),
-        out_shape=jax.ShapeDtypeStruct((count, width), BF),
-        scratch_shapes=[pltpu.VMEM((count, width), F32)],
-        compiler_params=params(48),
-        cost_estimate=cost(2 * count * width * units, 2 * count * units),
-    )(act, weight_out)
-
-
-def assemble_kernel(flags_ref, *refs):
-    sources, (in_ref, out_ref) = refs[:8], refs[8:]
-    step = pl.program_id(0)
-    for group in range(4):
-        first, second = sources[2 * group], sources[2 * group + 1]
-        flag = flags_ref[4 + group // 2]
-
-        @pl.when((step == group) & (flag == 0))
+        in_specs=[col, col, pl.BlockSpec((tile, width), lambda s: (s, 0))],
+        out_specs=whole(shape),
+        out_shape=jax.ShapeDtypeStruct(shape, BF),
+        scratch_shapes=[pltpu.VMEM((2, count, width), F32)],
+        compiler_params=params(62),
+        cost_estimate=cost(4 * count * width * units, 4 * count * units),
+    )(first, second, weight_out)
+
+
+def place_kernel(count, flags_ref, *refs):
+    sources, (in_ref, out_ref, wide, sems) = refs[:count], refs[-4:]
+    rows, width = wide.shape[1:]
+    for index, source in enumerate(sources):
+        wide[index] = source[...].astype(F32)
+        group, first = flags_ref[3 * index], pl.multiple_of(flags_ref[3 * index + 2] * rows, rows)
+        to_in = flags_ref[3 * index + 1] == 0
+
+        @pl.when(to_in)
         def _():
-            in_ref[...] = first[...].astype(F32)
-            out_ref[...] = second[...].astype(F32)
-
-        @pl.when((step == group) & (flag != 0))
+            columns = pl.ds(pl.multiple_of(group * width, width), width)
+            pltpu.make_async_copy(wide.at[index], in_ref.at[pl.ds(first, rows), columns], sems.at[index]).start()
+
+        @pl.when(jnp.logical_not(to_in))
         def _():
-            in_ref[...] = second[...].astype(F32)
-            out_ref[...] = first[...].astype(F32)
-
-
-def assemble(flags, sources):
-    tile, width = sources[0].shape
-    return pl.pallas_call(
-        assemble_kernel,
-        name="assemble",
+            place = pl.ds(pl.multiple_of(group * width + first, rows), rows)
+            pltpu.make_async_copy(wide.at[index], out_ref.at[place, :], sems.at[index]).start()
+
+    for index in range(count):
+        pltpu.make_async_copy(wide.at[index], out_ref.at[pl.ds(0, rows), :], sems.at[index]).wait()
+
+
+def place_blocks(flags, sources, previous=()):
+    rows, width = sources[0].shape
+    count = len(sources)
+    anywhere = pl.BlockSpec(memory_space=pl.ANY)
+    return pl.pallas_call(
+        functools.partial(place_kernel, count),
+        name="place_blocks",
         grid_spec=pltpu.PrefetchScalarGridSpec(
             num_scalar_prefetch=1,
-            grid=(4,),
-            in_specs=[whole((tile, width))] * 8,
-            out_specs=[
-                pl.BlockSpec((tile, width), lambda s, flags: (0, flags[s])),
-                pl.BlockSpec((tile, width), lambda s, flags: (flags[s], 0)),
-            ],
+            grid=(1,),
+            in_specs=[once((rows, width))] * count + [anywhere] * len(previous),
+            out_specs=[anywhere, anywhere],
+            scratch_shapes=[pltpu.VMEM((count, rows, width), F32), pltpu.SemaphoreType.DMA((count,))],
         ),
         out_shape=[
-            jax.ShapeDtypeStruct((width, 4 * tile), F32),
-            jax.ShapeDtypeStruct((4 * tile, width), F32),
-        ],
-        compiler_params=params(48),
-        cost_estimate=cost(8 * tile * width, 48 * tile * width),
-    )(flags, *sources)
+            jax.ShapeDtypeStruct((width, 4 * width), F32),
+            jax.ShapeDtypeStruct((4 * width, width), F32),
+        ],
+        input_output_aliases={count + 1: 0, count + 2: 1} if previous else {},
+        compiler_params=params(62),
+        cost_estimate=cost(rows * width, 6 * rows * width),
+    )(jnp.stack(flags).astype(I32), *sources, *previous)
 
 
 def gather_rows(block, target_ref, sources):
@@ -536,7 +551,7 @@
             jax.ShapeDtypeStruct((16, tokens), F32),
             jax.ShapeDtypeStruct((8, width), F32),
         ],
-        compiler_params=params(48),
+        compiler_params=params(62),
         cost_estimate=cost(2 * slots * tokens * width + 4 * tokens * width * width, 24 * tokens * width),
     )(back_first, back_second, target_col, middle, mixed, out_grad, gain, weight, jnp.asarray(heads, BF))
 
@@ -597,7 +612,7 @@
         out_specs=[pl.BlockSpec((tokens, PAIR), lambda g: (0, g))] * 3,
         out_shape=[out] * 3,
         scratch_shapes=[pltpu.VMEM((tokens, PAIR), F32)],
-        compiler_params=params(48),
+        compiler_params=params(62),
         cost_estimate=cost(20 * tokens * tokens * PAIR * count, 14 * tokens * PAIR * count, 2 * tokens * tokens * count),
     )(qkv, qkv, qkv, grad_mixed, lse, delta, seg_row, seg_col, cosine, sine)
 
@@ -631,7 +646,7 @@
             jax.ShapeDtypeStruct((2, width, columns), F32),
             jax.ShapeDtypeStruct((2, width, columns), BF),
         ],
-        compiler_params=params(40),
+        compiler_params=params(62),
         cost_estimate=cost(8 * tokens * width * columns, 16 * width * columns + 12 * tokens * columns),
     )(side, h_one, *grads, mixed, branch)
 
@@ -678,30 +693,81 @@
             jax.ShapeDtypeStruct((tokens, width), F32),
             jax.ShapeDtypeStruct((8, width), F32),
         ],
-        compiler_params=params(48),
+        compiler_params=params(62),
         cost_estimate=cost(6 * tokens * width * width, 6 * width * width + 16 * tokens * width),
     )(x, *grads, grad_middle, weight, gain)
 
 
-def output_kernel(block, first_ref, second_ref, target_ref, middle_ref, out_ref):
-    out_ref[...] = (middle_ref[...] + gather_rows(block, target_ref, (first_ref, second_ref))).astype(BF)
-
-
-def block_output(first, second, target_col, middle):
+def output_kernel(block, result_ref, target_ref, middle_ref, out_ref):
+    out_ref[...] = (middle_ref[...] + gather_rows(block, target_ref, (result_ref,))).astype(BF)
+
+
+def block_output(result, place_col, middle):
     tokens, width = middle.shape
-    slots = 2 * first.shape[0]
+    slots = result.shape[0]
     block = 256
     row = lambda w: pl.BlockSpec((block, w), lambda s: (s, 0))
     return pl.pallas_call(
         functools.partial(output_kernel, block),
         name="block_output",
         grid=(tokens // block,),
-        in_specs=[once((slots // 2, width)), once((slots // 2, width)), row(1), row(width)],
+        in_specs=[once((slots, width)), row(1), row(width)],
         out_specs=row(width),
         out_shape=jax.ShapeDtypeStruct((tokens, width), BF),
-        compiler_params=params(40),
+        compiler_params=params(62),
         cost_estimate=cost(2 * slots * tokens * width, 10 * tokens * width),
-    )(first, second, target_col, middle)
+    )(result, place_col, middle)
+
+
+def shared_out_kernel(flag_ref, low_ref, high_ref, *refs):
+    qkv_ref, proj_ref, wide, sems = refs[-4:]
+    width, columns = wide.shape[2:]
+    for half in range(2):
+        part = 2 * flag_ref[0] + half
+        for index, source in enumerate((low_ref, high_ref)):
+            slot = 2 * half + index
+            wide[half, index] = source[half].astype(F32)
+            start = pl.multiple_of(part * width + index * columns, columns)
+
+            @pl.when(part < 3)
+            def _():
+                pltpu.make_async_copy(
+                    wide.at[half, index], qkv_ref.at[:, pl.ds(start, columns)], sems.at[slot]
+                ).start()
+
+            @pl.when(part == 3)
+            def _():
+                pltpu.make_async_copy(
+                    wide.at[half, index], proj_ref.at[:, pl.ds(index * columns, columns)], sems.at[slot]
+                ).start()
+
+    for slot in range(4):
+        pltpu.make_async_copy(
+            wide.at[slot // 2, slot % 2], proj_ref.at[:, pl.ds(0, columns)], sems.at[slot]
+        ).wait()
+
+
+def shared_outputs(flag, low, high, previous=()):
+    _, width, columns = low.shape
+    anywhere = pl.BlockSpec(memory_space=pl.ANY)
+    return pl.pallas_call(
+        shared_out_kernel,
+        name="shared_outputs",
+        grid_spec=pltpu.PrefetchScalarGridSpec(
+            num_scalar_prefetch=1,
+            grid=(1,),
+            in_specs=[once(low.shape)] * 2 + [anywhere] * len(previous),
+            out_specs=[anywhere, anywhere],
+            scratch_shapes=[pltpu.VMEM((2, 2, width, columns), F32), pltpu.SemaphoreType.DMA((4,))],
+        ),
+        out_shape=[
+            jax.ShapeDtypeStruct((width, 3 * width), F32),
+            jax.ShapeDtypeStruct((width, width), F32),
+        ],
+        input_output_aliases={3: 0, 4: 1} if previous else {},
+        compiler_params=params(62),
+        cost_estimate=cost(width, width * width),
+    )(flag, low, high, *previous)
 
 
 def partner(axis, bit):
@@ -736,10 +802,8 @@
     return jnp.where(side(axis, bit) == 0, jnp.concatenate([total, got], 0), jnp.concatenate([got, total], 0))
 
 
-def sum_small(rows):
-    for axis, bit in axis_bits("expert") + axis_bits("dp"):
-        rows = rows + lax.ppermute(rows, axis, partner(axis, bit))
-    return rows
+def add_partner(rows, axis, bit):
+    return rows + lax.ppermute(rows, axis, partner(axis, bit))
 
 
 def local(
@@ -769,8 +833,8 @@
     perm = jnp.stack([1 - x_side, 3 - y_side, x_side, 2 + y_side, y_side, x_side]).astype(I32)
     tie = lambda *values: lax.optimization_barrier(values)
 
-    target, counts, sent_grads = route(token_ids, hash_table, out_grad, experts, half)
-    target_col = target.reshape(tokens, 1)
+    target, place, counts, sent_grads = route(token_ids, hash_table, out_grad, experts, half)
+    target_col, place_col = target.reshape(tokens, 1), place.reshape(tokens, 1)
     sent_grads, hidden_in = tie(sent_grads, hidden_in)
     grad_rows = exchange(sent_grads)
     qkv, h_one = first_half(hidden_in, row(ln1_gain), row(ln1_bias), qkv_weight, cosine, sine)
@@ -795,11 +859,8 @@
     back_second = exchange_half(back_second)
     early_x, early_y = across_x(early_x), across_y(early_y)
     late_x, late_y = across_x(late_x), across_y(late_y)
-    result_first = expert_result(act_first, weight_out)
-    result_second = expert_result(act_second, weight_out)
-    result_first, result_second, back_second, early_x, early_y = tie(
-        result_first, result_second, back_second, early_x, early_y
-    )
+    result = expert_result(act_first, act_second, weight_out, experts)
+    result, back_second = tie(result, back_second)
 
     plus = lambda *values: sum(value.astype(F32) for value in values).astype(BF)
     send_x, send_y = plus(keep[0, 0], early_x), plus(keep[1, 0], early_y)
@@ -808,8 +869,8 @@
     grad_middle, grad_mixed, branch, delta, small_two = middle_back(
         back_first, back_second, target_col, middle, mixed, out_grad, row(ln2_gain), proj_weight
     )
-    grad_mixed, late_x, late_y, result_first = tie(grad_mixed, late_x, late_y, result_first)
-    result_first = exchange_half(result_first)
+    grad_mixed, late_x, late_y, result = tie(grad_mixed, late_x, late_y, result)
+    result = exchange(result.reshape(2 * tokens, width))
 
     pairs = width // PAIR
     back_of = lambda grads, start: attend_back(
@@ -818,17 +879,19 @@
     core_side = jnp.reshape(side("expert", 1), (1,)).astype(I32)
     across_core = lambda value: lax.ppermute(value, "expert", partner("expert", 1))
     grads_low = back_of(grad_mixed, 0)
+    other_x, other_y, grads_low, grad_mixed = tie(other_x, other_y, grads_low, grad_mixed)
+    runs = [slice(0, width // 2), slice(width // 2, width)]
+    total_x = [plus(keep[0, 1, run], late_x[run], other_x[run]) for run in runs]
+    total_y = [plus(keep[1, 1, run], late_y[run], other_y[run]) for run in runs]
+    total_x, total_y, grads_low = tie(total_x, total_y, grads_low)
+    near_x, near_y = [across_y(run) for run in total_x], [across_x(run) for run in total_y]
+    far_x, far_y = across_x(total_x[0]), across_y(total_y[0])
     low, send_low = shared_grads(core_side, h_one, grads_low, mixed, branch, 0)
-    other_x, other_y, send_low, grad_mixed = tie(other_x, other_y, send_low, grad_mixed)
-    total_x, total_y = plus(keep[0, 1], late_x, other_x), plus(keep[1, 1], late_y, other_y)
-    total_x, total_y, grad_mixed = tie(total_x, total_y, grad_mixed)
-    near_x, near_y = across_y(total_x), across_x(total_y)
+    send_low, grad_mixed = tie(send_low, grad_mixed)
     got_low = across_core(send_low)
     grads_high = back_of(grad_mixed, pairs // 2)
     high, send_high = shared_grads(core_side, h_one, grads_high, mixed, branch, 1)
-    near_x, near_y, got_low, send_high, result_first = tie(near_x, near_y, got_low, send_high, result_first)
-    result_second = exchange_half(result_second)
-    far_x, far_y = across_x(total_x), across_y(total_y)
+    near_x, near_y, far_x, far_y, got_low, send_high = tie(near_x, near_y, far_x, far_y, got_low, send_high)
 
     low = (low + got_low.astype(F32)).reshape(8, width // 4, width // 2)
     high = (high + across_core(send_high).astype(F32)).reshape(8, width // 4, width // 2)
@@ -843,32 +906,53 @@
     input_grad, small_one = final_part(
         hidden_in, list(grads_low) + list(grads_high), grad_middle, qkv_weight, row(ln1_gain)
     )
-    low, high, far_x, far_y, small_one = tie(low, high, far_x, far_y, small_one)
+    low, high, small_one = tie(low, high, small_one)
     small = jnp.concatenate(
         [small_one[:2], small_two[:2], jnp.pad(counts, (0, width - experts))[None], jnp.zeros((3, width), F32)], 0
     )
+    for axis, bit in axis_bits("dp"):
+        small = add_partner(small, axis, bit)
     low, high = reduce_both(low, high, 1)
-    low, high, small, near_x, near_y = tie(low, high, small, near_x, near_y)
-    last_x, last_y = across_x(near_x), across_y(near_y)
-    small = sum_small(small)
-    for step in range(2, len(low_order)):
-        low, high = reduce_both(low, high, step)
-    block_out = block_output(result_first, result_second, target_col, middle)
-    low, high, last_x, last_y, block_out, small = tie(low, high, last_x, last_y, block_out, small)
-    sums_x = [total_x, near_x, far_x, last_x]
-    sums_y = [total_y, near_y, far_y, last_y]
-    flags = jnp.stack([x_side, 1 - x_side, 2 + y_side, 3 - y_side, y_side, x_side]).astype(I32)
-    grad_in, grad_out = assemble(flags, sums_x + sums_y)
-    low, high = low.astype(BF), high.astype(BF)
-    for step in (2, 1, 0):
-        low, high = gather_step(low, *low_order[step]), gather_step(high, *high_order[step])
-        if step == 1:
-            low, high, grad_in, grad_out = tie(low, high, grad_in, grad_out)
-    low, high = gather_step(low, "expert", 1), gather_step(high, "expert", 1)
-    low = low.reshape(4, width, width // 2).astype(F32)
-    high = high.reshape(4, width, width // 2).astype(F32)
-    qkv_grad = jnp.concatenate([low[0], high[0], low[1], high[1], low[2], high[2]], 1)
-    proj_sum = jnp.concatenate([low[3], high[3]], 1)
+    both_runs = lambda group, which: [group, which, 0, group, which, 1]
+    grad_in, grad_out = place_blocks(
+        both_runs(x_side, y_side) + both_runs(x_side, 1 - y_side)
+        + both_runs(2 + y_side, x_side) + both_runs(2 + y_side, 1 - x_side),
+        [*total_x, *near_x, *total_y, *near_y],
+    )
+    low, high, small, total_x, total_y, near_x, near_y, grad_in, result = tie(
+        low, high, small, total_x, total_y, near_x, near_y, grad_in, result
+    )
+    far_x, far_y = [far_x, across_x(total_x[1])], [far_y, across_y(total_y[1])]
+    last_x, last_y = [across_x(run) for run in near_x], [across_y(run) for run in near_y]
+    both = jnp.concatenate([low, high], 2)
+    small = add_partner(small, "expert", 1)
+    both = reduce_step(both, *far_bits[0])
+    both, small, far_x, far_y = tie(both, small, far_x, far_y)
+    small = add_partner(small, *far_bits[0])
+    both = reduce_step(both, *far_bits[1])
+    both, small, last_x[0], last_y[0] = tie(both, small, last_x[0], last_y[0])
+    for axis, bit in far_bits[2:]:
+        both = reduce_step(both, axis, bit)
+    for axis, bit in far_bits[1:]:
+        small = add_partner(small, axis, bit)
+    both = gather_step(both.astype(BF), *far_bits[0])
+    both, last_x, last_y, small = tie(both, last_x, last_y, small)
+    low, high = both[:, :, : width // 2], both[:, :, width // 2 :]
+    low, high = gather_step(low, *low_order[1]), gather_step(high, *high_order[1])
+    grad_in, grad_out = place_blocks(
+        both_runs(1 - x_side, y_side) + both_runs(1 - x_side, 1 - y_side)
+        + both_runs(3 - y_side, x_side) + both_runs(3 - y_side, 1 - x_side),
+        [*far_x, *last_x, *far_y, *last_y], (grad_in, grad_out),
+    )
+    low, high, grad_in, grad_out = tie(low, high, grad_in, grad_out)
+    low, high = gather_step(low, *low_order[0]), gather_step(high, *high_order[0])
+    block_out = block_output(result.reshape(2 * tokens, width), place_col, middle)
+    low, high, block_out = tie(low, high, block_out)
+    low, high = low.reshape(2, width, width // 2), high.reshape(2, width, width // 2)
+    got_low, got_high = across_core(low), across_core(high)
+    qkv_grad, proj_sum = shared_outputs(core_side, low, high)
+    got_low, got_high, qkv_grad, proj_sum = tie(got_low, got_high, qkv_grad, proj_sum)
+    qkv_grad, proj_sum = shared_outputs(1 - core_side, got_low, got_high, (qkv_grad, proj_sum))
     load = small[4, :experts] * (experts / (tokens * devices))
     return (
         block_out,

time: 515 us -> 474 us (0.920)
  local copies, waits for them, and re-layouts: 51.8 us -> 20 us
  waiting for transfers between devices: 124 us -> 101 us
  Pallas kernels: 226 us -> 248 us
  other arithmetic: 33.1 us -> 26.7 us
    unnamed x151 -> x51, local copies, waits for them, and re-layouts: 41.7 us -> 4.87 us
    ppermute x6 -> x9, waiting for transfers between devices: 6.35 us -> 23.3 us  [local(): across_x = lambda value: lax.ppermute(value, 'dp', partner('dp', 1))]
    ppermute x6 -> x5, waiting for transfers between devices: 19.6 us -> 4.39 us  [reduce_step(): lax.ppermute(send.astype(BF), axis, partner(axis, bit)).astype(F32)]
    ppermute x8 -> x5, waiting for transfers between devices: 15.2 us -> 1.97 us  [gather_step(): got = lax.ppermute(total, axis, partner(axis, bit))]
    pallas_call x1 -> x4, Pallas kernels: 10.2 us -> 21.3 us  [the longest x2 13.5 us: place_blocks(): pl.pallas_call(functools.partial(place_kernel, count), name='place_blocks...]
    ppermute x5, waiting for transfers between devices: 14.3 us -> 4.59 us  [add_partner(): return rows + lax.ppermute(rows, axis, partner(axis, bit))]
    ppermute x6 -> x9, waiting for transfers between devices: 1.65 us -> 8.64 us  [local(): across_y = lambda value: lax.ppermute(value, 'dp', partner('dp', 2))]
    ppermute x2 -> x1, waiting for transfers between devices: 8.46 us -> 3.02 us  [reduce_step(): lax.ppermute(total, axis, partner(axis, bit)).astype(F32)]
  transfers between devices with their start and end apart: 42 -> 44, of which waited for: 17 -> 25; matrix products, arithmetic and copies ran while one was open for 8% -> 8% of each run, Pallas kernels for 43% -> 51%
where the time goes in v2:
time: 474 us; the launch traced here: 465 us
  Pallas kernels  248 us (52%)
  waiting for transfers between devices  101 us (21%)
  starting transfers between devices  68 us (14%)
  other arithmetic  26.7 us (6%)
  local copies, waits for them, and re-layouts  20 us (4%)
    pallas_call x2, Pallas kernels, expert_rows(): pl.pallas_call(functools.partial(expert_kernel, 512, previous is not None...  65.6 us
    all_to_all x6, waiting for transfers between devices, exchange(): lax.all_to_all(sent, 'expert', split_axis=0, concat_axis=0, tiled=True)  55.1 us
    pallas_call x2, Pallas kernels, attend_back(): pl.pallas_call(functools.partial(attend_back_kernel, 256, start), name='a...  31.5 us
    all_to_all x6, starting transfers between devices, exchange(): lax.all_to_all(sent, 'expert', split_axis=0, concat_axis=0, tiled=True)  27.8 us
    pallas_call x1, Pallas kernels, attend(): pl.pallas_call(functools.partial(attend_kernel, 256), name='attend', grid...  23.8 us
    ppermute x9, waiting for transfers between devices, local(): across_x = lambda value: lax.ppermute(value, 'dp', partner('dp', 1))  23.3 us
    pallas_call x1, Pallas kernels, grads_inside(): pl.pallas_call(slope_kernel, name='grads_inside', grid=(units // tile,),...  15.6 us
    pallas_call x2, Pallas kernels, shared_grads(): pl.pallas_call(shared_kernel, name='shared_grads', grid_spec=pltpu.Prefet...  15.2 us
  transfers between devices with their start and end apart: 44, of which 25 were waited for; matrix products, arithmetic and copies ran while one was open for 8% of the time, Pallas kernels for 51%

profile of v2, /device:TPU:0, one launch (start us, length us, event | category | flops | bytes accessed | tf_op | source)
XLA Modules:
  0.0 465.4 jit_solution(7780155120841594044)
XLA Ops:
  2.3 8.1 %route.1 = (s32[1,1024]{1,0:T(1,128)}, s32[1,1024]{1,0:T(1,128)}, f32[16,128]{1,0:T(8,128)}, bf16[2048,768]{1,0:T(8,128)(2,1)}) custom-call(s32[1,1024]{1,0:T(1,128)} %bitcast.77, bf16[512,128]{1,0:T(8,128)(2,1)} %pad_bitcast_fusion.table_ref, bf16[1024,768]{1,0:T(8,128)(2,1)} %out_grad_ref.1), custom_call_target="tpu_custom_call" | custom-call | flops 1 | bytes 1 | tf_op jit(solution)/shard_map/route/pallas_call | solution.py:91
  10.3 6.5 %all-to-all-start = ((bf16[8,256,768]{2,1,0:T(8,128)(2,1)}), bf16[8,256,768]{2,1,0:T(8,128)(2,1)}, u32[]{:S(2)}, u32[]{:S(2)}) async-start(bf16[8,256,768]{2,1,0:T(8,128)(2,1)} %bitcast.69), calls=%async_computation | async-start | bytes 6291456 | tf_op jit(solution)/shard_map/all_to_all | solution.py:824
  17.9 9.1 %norm_project.1 = (bf16[1024,2304]{1,0:T(8,128)(2,1)}, bf16[1024,768]{1,0:T(8,128)(2,1)}) custom-call(bf16[1024,768]{1,0:T(8,128)(2,1)} %x_ref.2, f32[1,768]{1,0:T(1,128)} %reshape.114.gain_ref.refs_8_, f32[1,768]{1,0:T(1,128)} %reshape.115.bias_ref, bf16[768,2304]{1,0:T(8,128)(2,1)} %refs_7_.1, f32[1024,128]{1,0:T(8,128)} %constant.128.clone.cos_ref, ...), custom_call_target="tpu_custom_call" | custom-call | flops 1 | bytes 1 | tf_op jit(solution)/shard_map/norm_project/pallas_call | solution.py:154
  28.1 23.8 %attend.1 = (bf16[1024,768]{1,0:T(8,128)(2,1)}, f32[128,1024]{1,0:T(8,128)}) custom-call(bf16[1024,2304]{1,0:T(8,128)(2,1)} %get-tuple-element.143.q_ref.k_ref.v_ref, bf16[1024,2304]{1,0:T(8,128)(2,1)} %get-tuple-element.143.q_ref.k_ref.v_ref, bf16[1024,2304]{1,0:T(8,128)(2,1)} %get-tuple-element.143.q_ref.k_ref.v_ref, s32[1,1024]{1,0:T(1,128)} %bitcast.72, ...), custom_call_target="tpu_custom_call" | custom-call | flops 1 | bytes 1 | tf_op jit(solution)/shard_map/attend/pallas_call | solution.py:205
  53.1 10.5 %project_dispatch.1 = (f32[1024,768]{1,0:T(8,128)}, bf16[2048,768]{1,0:T(8,128)(2,1)}) custom-call(bf16[1024,768]{1,0:T(8,128)(2,1)} %get-tuple-element.144.mixed_ref, bf16[768,768]{1,0:T(8,128)(2,1)} %weight_ref.5, bf16[1024,768]{1,0:T(8,128)(2,1)} %x_ref.2, f32[1,768]{1,0:T(1,128)} %reshape.118.gain_ref, f32[1,768]{1,0:T(1,128)} %reshape.119.bias_ref, ...), custom_call_target="tpu_custom_call" | custom-call | flops 1 | bytes 1 | tf_op jit(solution)/shard_map/project_dispatch/pallas_call | solution.py:241
  67.3 21.1 %all-to-all-done.grads_ref = bf16[8,256,768]{2,1,0:T(8,128)(2,1)} async-done(((bf16[8,256,768]{2,1,0:T(8,128)(2,1)}), bf16[8,256,768]{2,1,0:T(8,128)(2,1)}, u32[]{:S(2)}, u32[]{:S(2)}) %all-to-all-start) | async-done | bytes 3145760 | tf_op jit(solution)/shard_map/all_to_all | solution.py:824
  92.0 15.6 %grads_inside.1.slope_ref = f32[2048,3072]{1,0:T(8,128)} custom-call(bf16[8,256,768]{2,1,0:T(8,128)(2,1)} %all-to-all-done.grads_ref, bf16[3072,768]{1,0:T(8,128)(2,1)} %bitcast.54), custom_call_target="tpu_custom_call" | custom-call | flops 1 | bytes 1 | tf_op jit(solution)/shard_map/grads_inside/pallas_call | solution.py:281
  107.6 22.1 %all-to-all-done.1 = bf16[8,128,768]{2,1,0:T(8,128)(2,1)S(1)} async-done(((bf16[8,128,768]{2,1,0:T(8,128)(2,1)}), bf16[8,128,768]{2,1,0:T(8,128)(2,1)S(1)}, u32[]{:S(2)}, u32[]{:S(2)}) %all-to-all-start.1) | async-done | bytes 1572896 | tf_op jit(solution)/shard_map/all_to_all | solution.py:824
  130.9 3.9 all-to-all-start.2
  135.5 31.2 %expert_rows.2 = (f32[4,2,768,768]{3,2,1,0:T(8,128)}, bf16[1024,3072]{1,0:T(8,128)(2,1)}, bf16[1024,768]{1,0:T(8,128)(2,1)}) custom-call(s32[6]{0:T(128)} %stack.23.perm_ref, bf16[1024,768]{1,0:T(8,128)(2,1)} %bitcast.63, bf16[8,256,768]{2,1,0:T(8,128)(2,1)} %all-to-all-done.grads_ref, f32[2048,3072]{1,0:T(8,128)} %grads_inside.1.slope_ref, ...), custom_call_target="tpu_custom_call" | custom-call | flops 1 | bytes 1 | tf_op jit(solution)/shard_map/expert_rows/pallas_call | solution.py:378
  166.7 5.8 %all-to-all-done.2 = bf16[8,128,768]{2,1,0:T(8,128)(2,1)S(1)} async-done(((bf16[8,128,768]{2,1,0:T(8,128)(2,1)}), bf16[8,128,768]{2,1,0:T(8,128)(2,1)S(1)}, u32[]{:S(2)}, u32[]{:S(2)}) %all-to-all-start.2) | async-done | bytes 1572896 | tf_op jit(solution)/shard_map/all_to_all | solution.py:824
  173.7 4.8 %all-to-all-start.3 = ((bf16[8,128,768]{2,1,0:T(8,128)(2,1)}), bf16[8,128,768]{2,1,0:T(8,128)(2,1)}, u32[]{:S(2)}, u32[]{:S(2)}) async-start(bf16[8,128,768]{2,1,0:T(8,128)(2,1)} %bitcast.71), calls=%async_computation.3 | async-start | bytes 3145728 | tf_op jit(solution)/shard_map/all_to_all | solution.py:824
  178.5 34.4 %expert_rows.3 = (bf16[768,768]{1,0:T(8,128)(2,1)}, bf16[768,768]{1,0:T(8,128)(2,1)}, bf16[768,768]{1,0:T(8,128)(2,1)}, bf16[768,768]{1,0:T(8,128)(2,1)}, bf16[2...) custom-call(s32[6]{0:T(128)} %stack.23.perm_ref, bf16[1024,768]{1,0:T(8,128)(2,1)} %bitcast.62, ...), custom_call_target="tpu_custom_call" | custom-call | flops 1 | bytes 1 | tf_op jit(solution)/shard_map/expert_rows/pallas_call | solution.py:378
  216.3 3.8 all-to-all-start.4
  224.2 15.1 %expert_result.1 = bf16[8,256,768]{2,1,0:T(8,128)(2,1)} custom-call(bf16[1024,3072]{1,0:T(8,128)(2,1)} %get-tuple-element.162.first_ref, bf16[1024,3072]{1,0:T(8,128)(2,1)} %get-tuple-element.163.second_ref, bf16[3072,768]{1,0:T(8,128)(2,1)} %bitcast.55), custom_call_target="tpu_custom_call" | custom-call | flops 1 | bytes 1 | tf_op jit(solution)/shard_map/expert_result/pallas_call | solution.py:423
  239.3 9.9 %collective-permute-done = bf16[768,768]{1,0:T(8,128)(2,1)} collective-permute-done((bf16[768,768]{1,0:T(8,128)(2,1)}, bf16[768,768]{1,0:T(8,128)(2,1)}, u32[]{:S(2)}, u32[]{:S(2)}) %collective-permute-start) | collective-permute-done | bytes 1179680 | tf_op jit(solution)/shard_map/ppermute | solution.py:856
  250.8 4.4 fusion
  261.8 13.7 %middle_back.1 = (f32[1024,768]{1,0:T(8,128)}, bf16[1024,768]{1,0:T(8,128)(2,1)}, bf16[1024,768]{1,0:T(8,128)(2,1)}, f32[16,1024]{1,0:T(8,128)}, f32[8,768]{1,0:T(8,128)}) custom-call(bf16[1024,768]{1,0:T(8,128)(2,1)} %bitcast.19.back_first_ref, bf16[1024,768]{1,0:T(8,128)(2,1)} %bitcast.66, s32[1024,1]{1,0:T(8,128)} %copy.32.target_ref, ...), custom_call_target="tpu_custom_call" | custom-call | flops 1 | bytes 1 | tf_op jit(solution)/shard_map/middle_back/pallas_call | solution.py:535
  276.0 5.4 %all-to-all-start.5 = ((bf16[8,256,768]{2,1,0:T(8,128)(2,1)}), bf16[8,256,768]{2,1,0:T(8,128)(2,1)}, u32[]{:S(2)}, u32[]{:S(2)}) async-start(bf16[8,256,768]{2,1,0:T(8,128)(2,1)} %expert_result.1), calls=%async_computation.5 | async-start | bytes 6291456 | tf_op jit(solution)/shard_map/all_to_all | solution.py:824
  281.4 15.8 %attend_back.2 = (bf16[1024,384]{1,0:T(8,128)(2,1)}, bf16[1024,384]{1,0:T(8,128)(2,1)}, bf16[1024,384]{1,0:T(8,128)(2,1)}) custom-call(bf16[1024,2304]{1,0:T(8,128)(2,1)} %get-tuple-element.143.q_ref.k_ref.v_ref, bf16[1024,2304]{1,0:T(8,128)(2,1)} %get-tuple-element.143.q_ref.k_ref.v_ref, bf16[1024,2304]{1,0:T(8,128)(2,1)} %get-tuple-element.143.q_ref.k_ref.v_ref, ...), custom_call_target="tpu_custom_call" | custom-call | flops 1 | bytes 1 | tf_op jit(solution)/shard_map/attend_back/pallas_call | solution.py:604
  300.5 4.7 %fusion.3 = (bf16[384,768]{1,0:T(8,128)(2,1)S(1)}, bf16[384,768]{1,0:T(8,128)(2,1)S(1)}, bf16[384,768]{1,0:T(8,128)(2,1)}, bf16[384,768]{1,0:T(8,128)(2,1)S(1)}) fusion(bf16[768,768]{1,0:T(8,128)(2,1)} %collective-permute-done.5, bf16[768,768]{1,0:T(8,128)(2,1)} %collective-permute-done.3, bf16[2,2,768,768]{3,2,1,0:T(8,128)(2,1)} %get-tuple-element.156, ...), kind=kLoop, calls=%fused_computation.10 | loop fusion | flops 7077888 | bytes 9437184 | tf_op jit(solution)/shard_map/convert_element_type | solution.py:865
  307.4 7.4 %shared_grads.2 = (f32[2,768,384]{2,1,0:T(8,128)}, bf16[2,768,384]{2,1,0:T(8,128)(2,1)}) custom-call(s32[1]{0:T(128)} %bitcast.side_ref.flag_ref, bf16[1024,768]{1,0:T(8,128)(2,1)} %get-tuple-element.142.h_ref, bf16[1024,384]{1,0:T(8,128)(2,1)} %get-tuple-element.187.dq_ref.refs_0_, bf16[1024,384]{1,0:T(8,128)(2,1)} %get-tuple-element.188.dk_ref.refs_1_, ...), custom_call_target="tpu_custom_call" | custom-call | flops 1 | bytes 1 | tf_op jit(solution)/shard_map/shared_grads/pallas_call | solution.py:635
  316.9 5.0 %collective-permute-done.10.refs_0_ = bf16[384,768]{1,0:T(8,128)(2,1)} collective-permute-done((bf16[384,768]{1,0:T(8,128)(2,1)}, bf16[384,768]{1,0:T(8,128)(2,1)}, u32[]{:S(2)}, u32[]{:S(2)}) %collective-permute-start.10) | collective-permute-done | bytes 589856 | tf_op jit(solution)/shard_map/ppermute | solution.py:856
  323.7 15.7 %attend_back.3 = (bf16[1024,384]{1,0:T(8,128)(2,1)}, bf16[1024,384]{1,0:T(8,128)(2,1)}, bf16[1024,384]{1,0:T(8,128)(2,1)}) custom-call(bf16[1024,2304]{1,0:T(8,128)(2,1)} %get-tuple-element.143.q_ref.k_ref.v_ref, bf16[1024,2304]{1,0:T(8,128)(2,1)} %get-tuple-element.143.q_ref.k_ref.v_ref, bf16[1024,2304]{1,0:T(8,128)(2,1)} %get-tuple-element.143.q_ref.k_ref.v_ref, ...), custom_call_target="tpu_custom_call" | custom-call | flops 1 | bytes 1 | tf_op jit(solution)/shard_map/attend_back/pallas_call | solution.py:604
  339.4 7.7 %shared_grads.3 = (f32[2,768,384]{2,1,0:T(8,128)}, bf16[2,768,384]{2,1,0:T(8,128)(2,1)}) custom-call(s32[1]{0:T(128)} %bitcast.side_ref.flag_ref, bf16[1024,768]{1,0:T(8,128)(2,1)} %get-tuple-element.142.h_ref, bf16[1024,384]{1,0:T(8,128)(2,1)} %get-tuple-element.200.dq_ref.refs_3_, bf16[1024,384]{1,0:T(8,128)(2,1)} %get-tuple-element.201.dk_ref.refs_4_, ...), custom_call_target="tpu_custom_call" | custom-call | flops 1 | bytes 1 | tf_op jit(solution)/shard_map/shared_grads/pallas_call | solution.py:635
  355.1 11.0 %first_back.1 = (f32[1024,768]{1,0:T(8,128)}, f32[8,768]{1,0:T(8,128)}) custom-call(bf16[1024,768]{1,0:T(8,128)(2,1)} %x_ref.2, bf16[1024,384]{1,0:T(8,128)(2,1)} %get-tuple-element.187.dq_ref.refs_0_, bf16[1024,384]{1,0:T(8,128)(2,1)} %get-tuple-element.188.dk_ref.refs_1_, bf16[1024,384]{1,0:T(8,128)(2,1)} %get-tuple-element.189.dv_ref.refs_2_, ...), custom_call_target="tpu_custom_call" | custom-call | flops 1 | bytes 1 | tf_op jit(solution)/shard_map/first_back/pallas_call | solution.py:686
  376.7 6.7 %place_blocks.2 = (f32[768,3072]{1,0:T(8,128)}, f32[3072,768]{1,0:T(8,128)}) custom-call(s32[24]{0:T(128)} %stack.25.flags_ref, bf16[384,768]{1,0:T(8,128)(2,1)} %get-tuple-element.192.refs_0_, bf16[384,768]{1,0:T(8,128)(2,1)} %copy-done.10, bf16[384,768]{1,0:T(8,128)(2,1)} %collective-permute-done.6.refs_2_, ...), custom_call_target="tpu_custom_call" | custom-call | flops 1 | bytes 1 | tf_op jit(solution)/shard_map/place_blocks/pallas_call | solution.py:462
  398.1 6.2 %collective-permute-done.22.refs_1_ = bf16[384,768]{1,0:T(8,128)(2,1)} collective-permute-done((bf16[384,768]{1,0:T(8,128)(2,1)S(1)}, bf16[384,768]{1,0:T(8,128)(2,1)}, u32[]{:S(2)}, u32[]{:S(2)}) %collective-permute-start.22) | collective-permute-done | bytes 589856 | tf_op jit(solution)/shard_map/ppermute | solution.py:856
  430.4 6.7 %place_blocks.3 = (f32[768,3072]{1,0:T(8,128)}, f32[3072,768]{1,0:T(8,128)}) custom-call(s32[24]{0:T(128)} %stack.26.flags_ref, bf16[384,768]{1,0:T(8,128)(2,1)} %collective-permute-done.10.refs_0_, bf16[384,768]{1,0:T(8,128)(2,1)} %collective-permute-done.22.refs_1_, bf16[384,768]{1,0:T(8,128)(2,1)} %copy-done.15, ...), custom_call_target="tpu_custom_call", output_to_operand_aliasing={{0}: (9, {}), {1}: (10, {})} | custom-call | flops 1 | bytes 1 | tf_op jit(solution)/shard_map/place_blocks/pallas_call | solution.py:462
  442.0 7.4 %block_output.1 = bf16[1024,768]{1,0:T(8,128)(2,1)} custom-call(bf16[2048,768]{1,0:T(8,128)(2,1)} %bitcast.31.result_ref, s32[1024,1]{1,0:T(8,128)} %copy.35.target_ref, f32[1024,768]{1,0:T(8,128)} %get-tuple-element.167.middle_ref), custom_call_target="tpu_custom_call" | custom-call | flops 1 | bytes 1 | tf_op jit(solution)/shard_map/block_output/pallas_call | solution.py:710
  457.1 3.9 shared_outputs.2
  461.0 3.9 shared_outputs.3
  (176 shorter events, 112.3 us)
Async XLA Ops:
  10.3 78.1 %all-to-all-start = ((bf16[8,256,768]{2,1,0:T(8,128)(2,1)}), bf16[8,256,768]{2,1,0:T(8,128)(2,1)}, u32[]{:S(2)}, u32[]{:S(2)}) async-start(bf16[8,256,768]{2,1,0:T(8,128)(2,1)} %bitcast.69), calls=%async_computation | async-start | bytes 6291456 | tf_op jit(solution)/shard_map/all_to_all | solution.py:824
  88.4 41.3 %all-to-all-start.1 = ((bf16[8,128,768]{2,1,0:T(8,128)(2,1)}), bf16[8,128,768]{2,1,0:T(8,128)(2,1)S(1)}, u32[]{:S(2)}, u32[]{:S(2)}) async-start(bf16[8,128,768]{2,1,0:T(8,128)(2,1)} %bitcast.65), calls=%async_computation.1 | async-start | bytes 3145728 | tf_op jit(solution)/shard_map/all_to_all | solution.py:824
  130.9 41.6 %all-to-all-start.2 = ((bf16[8,128,768]{2,1,0:T(8,128)(2,1)}), bf16[8,128,768]{2,1,0:T(8,128)(2,1)S(1)}, u32[]{:S(2)}, u32[]{:S(2)}) async-start(bf16[8,128,768]{2,1,0:T(8,128)(2,1)} %bitcast.64), calls=%async_computation.2 | async-start | bytes 3145728 | tf_op jit(solution)/shard_map/all_to_all | solution.py:824
  173.7 42.6 %all-to-all-start.3 = ((bf16[8,128,768]{2,1,0:T(8,128)(2,1)}), bf16[8,128,768]{2,1,0:T(8,128)(2,1)}, u32[]{:S(2)}, u32[]{:S(2)}) async-start(bf16[8,128,768]{2,1,0:T(8,128)(2,1)} %bitcast.71), calls=%async_computation.3 | async-start | bytes 3145728 | tf_op jit(solution)/shard_map/all_to_all | solution.py:824
  216.3 41.5 %all-to-all-start.4 = ((bf16[8,128,768]{2,1,0:T(8,128)(2,1)}), bf16[8,128,768]{2,1,0:T(8,128)(2,1)S(1)}, u32[]{:S(2)}, u32[]{:S(2)}) async-start(bf16[8,128,768]{2,1,0:T(8,128)(2,1)} %bitcast.70), calls=%async_computation.4 | async-start | bytes 3145728 | tf_op jit(solution)/shard_map/all_to_all | solution.py:824
  220.1 29.2 %collective-permute-start = (bf16[768,768]{1,0:T(8,128)(2,1)}, bf16[768,768]{1,0:T(8,128)(2,1)}, u32[]{:S(2)}, u32[]{:S(2)}) collective-permute-start(bf16[768,768]{1,0:T(8,128)(2,1)} %get-tuple-element.160), channel_id=1, source_target_pairs={{0,8},{8,0},{16,24},{24,16},{1,9},{9,1},{17,25},{25,17},{2,10},{10... | collective-permute-start | bytes 3538952 | tf_op jit(solution)/shard_map/ppermute | solution.py:856
  221.6 29.1 %collective-permute-start.1 = (bf16[768,768]{1,0:T(8,128)(2,1)}, bf16[768,768]{1,0:T(8,128)(2,1)}, u32[]{:S(2)}, u32[]{:S(2)}) collective-permute-start(bf16[768,768]{1,0:T(8,128)(2,1)} %get-tuple-element.161), channel_id=1, source_target_pairs={{0,16},{8,24},{16,0},{24,8},{1,17},{9,25},{17,1},{25,9},{2,18},{10... | collective-permute-start | bytes 3538952 | tf_op jit(solution)/shard_map/ppermute | solution.py:857
  223.2 52.4 %collective-permute-start.2 = (bf16[768,768]{1,0:T(8,128)(2,1)}, bf16[768,768]{1,0:T(8,128)(2,1)}, u32[]{:S(2)}, u32[]{:S(2)}) collective-permute-start(bf16[768,768]{1,0:T(8,128)(2,1)} %get-tuple-element.169), channel_id=1, source_target_pairs={{0,8},{8,0},{16,24},{24,16},{1,9},{9,1},{17,25},{25,17},{2,10},{10... | collective-permute-start | bytes 3538952 | tf_op jit(solution)/shard_map/ppermute | solution.py:856
  223.7 52.4 %collective-permute-start.3 = (bf16[768,768]{1,0:T(8,128)(2,1)}, bf16[768,768]{1,0:T(8,128)(2,1)}, u32[]{:S(2)}, u32[]{:S(2)}) collective-permute-start(bf16[768,768]{1,0:T(8,128)(2,1)} %get-tuple-element.170), channel_id=1, source_target_pairs={{0,16},{8,24},{16,0},{24,8},{1,17},{9,25},{17,1},{25,9},{2,18},{10... | collective-permute-start | bytes 3538952 | tf_op jit(solution)/shard_map/ppermute | solution.py:857
  257.8 42.7 %collective-permute-start.4 = (bf16[768,768]{1,0:T(8,128)(2,1)}, bf16[768,768]{1,0:T(8,128)(2,1)}, u32[]{:S(2)}, u32[]{:S(2)}) collective-permute-start(bf16[768,768]{1,0:T(8,128)(2,1)} %get-tuple-element.173), channel_id=1, source_target_pairs={{0,16},{8,24},{16,0},{24,8},{1,17},{9,25},{17,1},{25,9},{2,18},{10... | collective-permute-start | bytes 3538952 | tf_op jit(solution)/shard_map/ppermute | solution.py:857
  259.3 41.2 %collective-permute-start.5 = (bf16[768,768]{1,0:T(8,128)(2,1)}, bf16[768,768]{1,0:T(8,128)(2,1)}, u32[]{:S(2)}, u32[]{:S(2)}) collective-permute-start(bf16[768,768]{1,0:T(8,128)(2,1)} %get-tuple-element.174), channel_id=1, source_target_pairs={{0,8},{8,0},{16,24},{24,16},{1,9},{9,1},{17,25},{25,17},{2,10},{10... | collective-permute-start | bytes 3538952 | tf_op jit(solution)/shard_map/ppermute | solution.py:856
  276.0 110.7 %all-to-all-start.5 = ((bf16[8,256,768]{2,1,0:T(8,128)(2,1)}), bf16[8,256,768]{2,1,0:T(8,128)(2,1)}, u32[]{:S(2)}, u32[]{:S(2)}) async-start(bf16[8,256,768]{2,1,0:T(8,128)(2,1)} %expert_result.1), calls=%async_computation.5 | async-start | bytes 6291456 | tf_op jit(solution)/shard_map/all_to_all | solution.py:824
  305.2 16.6 %collective-permute-start.10 = (bf16[384,768]{1,0:T(8,128)(2,1)}, bf16[384,768]{1,0:T(8,128)(2,1)}, u32[]{:S(2)}, u32[]{:S(2)}) collective-permute-start(bf16[384,768]{1,0:T(8,128)(2,1)} %get-tuple-element.192.refs_0_), channel_id=1, source_target_pairs={{0,8},{8,0},{16,24},{24,16},{1,9},{9,1},{17,25},{25,17},{2,10},{10... | collective-permute-start | bytes 1769480 | tf_op jit(solution)/shard_map/ppermute | solution.py:856
  305.8 17.6 %collective-permute-start.11 = (bf16[384,768]{1,0:T(8,128)(2,1)S(1)}, bf16[384,768]{1,0:T(8,128)(2,1)}, u32[]{:S(2)}, u32[]{:S(2)}) collective-permute-start(bf16[384,768]{1,0:T(8,128)(2,1)S(1)} %get-tuple-element.194.refs_4_), channel_id=1, source_target_pairs={{0,16},{8,24},{16,0},{24,8},{1,17},{9,25},{17,1},{25,9},{2,18},{10... | collective-permute-start | bytes 1769480 | tf_op jit(solution)/shard_map/ppermute | solution.py:857
  314.8 32.4 %collective-permute-start.12 = (bf16[2,768,384]{2,1,0:T(8,128)(2,1)}, bf16[2,768,384]{2,1,0:T(8,128)(2,1)}, u32[]{:S(2)}, u32[]{:S(2)}) collective-permute-start(bf16[2,768,384]{2,1,0:T(8,128)(2,1)} %get-tuple-element.198), channel_id=1, source_target_pairs={{0,1},{1,0},{2,3},{3,2},{4,5},{5,4},{6,7},{7,6},{8,9},{9,8},{10,11... | collective-permute-start | bytes 3538952 | tf_op jit(solution)/shard_map/ppermute | solution.py:880
  314.8 32.3 %collective-permute-start.6 = (bf16[384,768]{1,0:T(8,128)(2,1)}, bf16[384,768]{1,0:T(8,128)(2,1)}, u32[]{:S(2)}, u32[]{:S(2)}) collective-permute-start(bf16[384,768]{1,0:T(8,128)(2,1)} %get-tuple-element.192.refs_0_), channel_id=1, source_target_pairs={{0,16},{8,24},{16,0},{24,8},{1,17},{9,25},{17,1},{25,9},{2,18},{10... | collective-permute-start | bytes 1769480 | tf_op jit(solution)/shard_map/ppermute | solution.py:857
  315.4 31.8 %collective-permute-start.8 = (bf16[384,768]{1,0:T(8,128)(2,1)S(1)}, bf16[384,768]{1,0:T(8,128)(2,1)}, u32[]{:S(2)}, u32[]{:S(2)}) collective-permute-start(bf16[384,768]{1,0:T(8,128)(2,1)S(1)} %get-tuple-element.194.refs_4_), channel_id=1, source_target_pairs={{0,8},{8,0},{16,24},{24,16},{1,9},{9,1},{17,25},{25,17},{2,10},{10... | collective-permute-start | bytes 1769480 | tf_op jit(solution)/shard_map/ppermute | solution.py:856
  321.9 25.3 %collective-permute-start.7 = (bf16[384,768]{1,0:T(8,128)(2,1)S(1)}, bf16[384,768]{1,0:T(8,128)(2,1)}, u32[]{:S(2)}, u32[]{:S(2)}) collective-permute-start(bf16[384,768]{1,0:T(8,128)(2,1)S(1)} %get-tuple-element.224.refs_1_), channel_id=1, source_target_pairs={{0,16},{8,24},{16,0},{24,8},{1,17},{9,25},{17,1},{25,9},{2,18},{10... | collective-permute-start | bytes 1769480 | tf_op jit(solution)/shard_map/ppermute | solution.py:857
  323.4 23.8 %collective-permute-start.9 = (bf16[384,768]{1,0:T(8,128)(2,1)S(1)}, bf16[384,768]{1,0:T(8,128)(2,1)}, u32[]{:S(2)}, u32[]{:S(2)}) collective-permute-start(bf16[384,768]{1,0:T(8,128)(2,1)S(1)} %get-tuple-element.226.refs_5_), channel_id=1, source_target_pairs={{0,8},{8,0},{16,24},{24,16},{1,9},{9,1},{17,25},{25,17},{2,10},{10... | collective-permute-start | bytes 1769480 | tf_op jit(solution)/shard_map/ppermute | solution.py:856
  349.7 16.4 %collective-permute-start.13 = (bf16[4,192,384]{2,1,0:T(8,128)(2,1)S(1)}, bf16[4,192,384]{2,1,0:T(8,128)(2,1)}, u32[]{:S(2)}, u32[]{:S(2)}) collective-permute-start(bf16[4,192,384]{2,1,0:T(8,128)(2,1)S(1)} %dynamic-slice_convert_fusion.1), channel_id=1, source_target_pairs={{0,8},{8,0},{16,24},{24,16},{1,9},{9,1},{17,25},{25,17},{2,10},{10... | collective-permute-start | bytes 1769480 | tf_op jit(solution)/shard_map/ppermute | solution.py:797
  353.3 15.6 %collective-permute-start.15 = (bf16[4,192,384]{2,1,0:T(8,128)(2,1)S(1)}, bf16[4,192,384]{2,1,0:T(8,128)(2,1)}, u32[]{:S(2)}, u32[]{:S(2)}) collective-permute-start(bf16[4,192,384]{2,1,0:T(8,128)(2,1)S(1)} %dynamic-slice_convert_fusion), channel_id=1, source_target_pairs={{0,16},{8,24},{16,0},{24,8},{1,17},{9,25},{17,1},{25,9},{2,18},{10... | collective-permute-start | bytes 1769480 | tf_op jit(solution)/shard_map/ppermute | solution.py:797
  372.2 11.3 %collective-permute-start.17 = (bf16[2,192,384]{2,1,0:T(8,128)(2,1)S(1)}, bf16[2,192,384]{2,1,0:T(8,128)(2,1)}, u32[]{:S(2)}, u32[]{:S(2)}) collective-permute-start(bf16[2,192,384]{2,1,0:T(8,128)(2,1)S(1)} %dynamic-slice_convert_fusion.3), channel_id=1, source_target_pairs={{0,8},{8,0},{16,24},{24,16},{1,9},{9,1},{17,25},{25,17},{2,10},{10... | collective-permute-start | bytes 884744 | tf_op jit(solution)/shard_map/ppermute | solution.py:797
  373.8 11.0 %collective-permute-start.16 = (bf16[2,192,384]{2,1,0:T(8,128)(2,1)}, bf16[2,192,384]{2,1,0:T(8,128)(2,1)}, u32[]{:S(2)}, u32[]{:S(2)}) collective-permute-start(bf16[2,192,384]{2,1,0:T(8,128)(2,1)} %dynamic-slice_convert_fusion.4), channel_id=1, source_target_pairs={{0,16},{8,24},{16,0},{24,8},{1,17},{9,25},{17,1},{25,9},{2,18},{10... | collective-permute-start | bytes 884744 | tf_op jit(solution)/shard_map/ppermute | solution.py:797
  387.8 16.4 %collective-permute-start.22 = (bf16[384,768]{1,0:T(8,128)(2,1)S(1)}, bf16[384,768]{1,0:T(8,128)(2,1)}, u32[]{:S(2)}, u32[]{:S(2)}) collective-permute-start(bf16[384,768]{1,0:T(8,128)(2,1)S(1)} %copy-done.11), channel_id=1, source_target_pairs={{0,8},{8,0},{16,24},{24,16},{1,9},{9,1},{17,25},{25,17},{2,10},{10... | collective-permute-start | bytes 1769480 | tf_op jit(solution)/shard_map/ppermute | solution.py:856
  388.9 16.4 %collective-permute-start.23 = (bf16[384,768]{1,0:T(8,128)(2,1)S(1)}, bf16[384,768]{1,0:T(8,128)(2,1)}, u32[]{:S(2)}, u32[]{:S(2)}) collective-permute-start(bf16[384,768]{1,0:T(8,128)(2,1)S(1)} %copy-done.9), channel_id=1, source_target_pairs={{0,16},{8,24},{16,0},{24,8},{1,17},{9,25},{17,1},{25,9},{2,18},{10... | collective-permute-start | bytes 1769480 | tf_op jit(solution)/shard_map/ppermute | solution.py:857
  391.5 25.3 %collective-permute-start.26 = (bf16[384,768]{1,0:T(8,128)(2,1)}, bf16[384,768]{1,0:T(8,128)(2,1)S(1)}, u32[]{:S(2)}, u32[]{:S(2)}) collective-permute-start(bf16[384,768]{1,0:T(8,128)(2,1)} %collective-permute-done.6.refs_2_), channel_id=1, source_target_pairs={{0,8},{8,0},{16,24},{24,16},{1,9},{9,1},{17,25},{25,17},{2,10},{10... | collective-permute-start | bytes 1769480 | tf_op jit(solution)/shard_map/ppermute | solution.py:856
  392.7 25.3 %collective-permute-start.27 = (bf16[384,768]{1,0:T(8,128)(2,1)}, bf16[384,768]{1,0:T(8,128)(2,1)}, u32[]{:S(2)}, u32[]{:S(2)}) collective-permute-start(bf16[384,768]{1,0:T(8,128)(2,1)} %collective-permute-done.8.refs_6_), channel_id=1, source_target_pairs={{0,16},{8,24},{16,0},{24,8},{1,17},{9,25},{17,1},{25,9},{2,18},{10... | collective-permute-start | bytes 1769480 | tf_op jit(solution)/shard_map/ppermute | solution.py:857
  405.3 10.9 %collective-permute-start.24 = (bf16[1,192,768]{2,1,0:T(8,128)(2,1)S(1)}, bf16[1,192,768]{2,1,0:T(8,128)(2,1)S(1)}, u32[]{:S(2)}, u32[]{:S(2)}) collective-permute-start(bf16[1,192,768]{2,1,0:T(8,128)(2,1)S(1)} %convert_add_fusion.11), channel_id=1, source_target_pairs={{0,4},{1,5},{2,6},{3,7},{4,0},{5,1},{6,2},{7,3},{8,12},{9,13},{10,... | collective-permute-start | bytes 884744 | tf_op jit(solution)/shard_map/ppermute | solution.py:792
  409.1 17.6 %collective-permute-start.29 = (bf16[384,768]{1,0:T(8,128)(2,1)}, bf16[384,768]{1,0:T(8,128)(2,1)S(1)}, u32[]{:S(2)}, u32[]{:S(2)}) collective-permute-start(bf16[384,768]{1,0:T(8,128)(2,1)} %collective-permute-done.7.refs_3_), channel_id=1, source_target_pairs={{0,8},{8,0},{16,24},{24,16},{1,9},{9,1},{17,25},{25,17},{2,10},{10... | collective-permute-start | bytes 1769480 | tf_op jit(solution)/shard_map/ppermute | solution.py:856
  412.2 15.6 %collective-permute-start.30 = (bf16[384,768]{1,0:T(8,128)(2,1)}, bf16[384,768]{1,0:T(8,128)(2,1)}, u32[]{:S(2)}, u32[]{:S(2)}) collective-permute-start(bf16[384,768]{1,0:T(8,128)(2,1)} %collective-permute-done.9.refs_7_), channel_id=1, source_target_pairs={{0,16},{8,24},{16,0},{24,8},{1,17},{9,25},{17,1},{25,9},{2,18},{10... | collective-permute-start | bytes 1769480 | tf_op jit(solution)/shard_map/ppermute | solution.py:857
  438.7 12.0 %collective-permute-start.35 = (bf16[4,192,384]{2,1,0:T(8,128)(2,1)S(1)}, bf16[4,192,384]{2,1,0:T(8,128)(2,1)}, u32[]{:S(2)}, u32[]{:S(2)}) collective-permute-start(bf16[4,192,384]{2,1,0:T(8,128)(2,1)S(1)} %maximum_select_fusion.4), channel_id=1, source_target_pairs={{0,16},{8,24},{16,0},{24,8},{1,17},{9,25},{17,1},{25,9},{2,18},{10... | collective-permute-start | bytes 1769480 | tf_op jit(solution)/shard_map/ppermute | solution.py:801
  439.7 12.9 %collective-permute-start.34 = (bf16[4,192,384]{2,1,0:T(8,128)(2,1)S(1)}, bf16[4,192,384]{2,1,0:T(8,128)(2,1)}, u32[]{:S(2)}, u32[]{:S(2)}) collective-permute-start(bf16[4,192,384]{2,1,0:T(8,128)(2,1)S(1)} %maximum_select_fusion.3), channel_id=1, source_target_pairs={{0,8},{8,0},{16,24},{24,16},{1,9},{9,1},{17,25},{25,17},{2,10},{10... | collective-permute-start | bytes 1769480 | tf_op jit(solution)/shard_map/ppermute | solution.py:801
  (37 other events, 258.6 us)

commit v3 on v2

--- a/solution.py
+++ b/solution.py
@@ -55,7 +55,10 @@
     return (iota((count, target.shape[1]), 0) + first == target).astype(F32).astype(BF)
 
 
-def route_kernel(experts, half, block, ids_ref, table_ref, grad_ref, target_ref, place, counts_ref, sent_ref):
+def route_kernel(
+    experts, half, block, me_ref, ids_ref, segments_ref, table_ref, grad_ref,
+    columns_ref, leaving_ref, counts_ref, sent_ref, place,
+):
     tokens = ids_ref.shape[1]
     rows = table_ref.shape[0]
     padded = counts_ref.shape[0]
@@ -74,41 +77,49 @@
         rank = dot(member.astype(BF), earlier)
         slot = jnp.sum(member * rank, 0, keepdims=True).astype(I32)
         place[...] = chosen * (2 * half) + slot
-        later = (slot >= half).astype(I32)
-        target_ref[...] = later * (experts * half) + chosen * half + slot - later * half
+        late = slot >= half
+        second = experts * half + chosen * half + slot - half
+        target = jnp.where(late, second, chosen * half + slot)
+        lines = [target, place[...], segments_ref[...], jnp.zeros((5, tokens), I32)]
+        columns_ref[...] = jnp.concatenate(lines, 0).T
+        leaving_ref[...] = jnp.where(late, second, (chosen ^ me_ref[0]) * half + slot)
         counts_ref[...] = jnp.broadcast_to(jnp.sum(member, 1, keepdims=True), counts_ref.shape)
 
     sent_ref[...] = dot(one_hot_rows(place[...], step * block, block), grad_ref[...]).astype(BF)
 
 
-def route(token_ids, hash_table, out_grad, experts, half):
+def route(me, token_ids, segments, hash_table, out_grad, experts, half):
     tokens, width = out_grad.shape
     slots = 2 * tokens
     block = 256
     padded = max(experts, 16)
     rows = -(-hash_table.shape[0] // (128 * 128)) * 128
     table = jnp.pad(hash_table, (0, rows * 128 - hash_table.shape[0])).reshape(rows, 128).astype(BF)
-    target, place, counts, sent = pl.pallas_call(
+    columns, leaving, counts, sent = pl.pallas_call(
         functools.partial(route_kernel, experts, half, block),
         name="route",
-        grid=(slots // block,),
-        in_specs=[whole((1, tokens)), whole((rows, 128)), whole((tokens, width))],
-        out_specs=[
-            whole((1, tokens)),
-            whole((1, tokens)),
-            whole((padded, 128)),
-            pl.BlockSpec((block, width), lambda s: (s, 0)),
-        ],
+        grid_spec=pltpu.PrefetchScalarGridSpec(
+            num_scalar_prefetch=1,
+            grid=(slots // block,),
+            in_specs=[whole((1, tokens)), whole((1, tokens)), whole((rows, 128)), whole((tokens, width))],
+            out_specs=[
+                whole((tokens, 8)),
+                whole((1, tokens)),
+                whole((padded, 128)),
+                pl.BlockSpec((block, width), lambda s, me: (s, 0)),
+            ],
+            scratch_shapes=[pltpu.VMEM((1, tokens), I32)],
+        ),
         out_shape=[
-            jax.ShapeDtypeStruct((1, tokens), I32),
+            jax.ShapeDtypeStruct((tokens, 8), I32),
             jax.ShapeDtypeStruct((1, tokens), I32),
             jax.ShapeDtypeStruct((padded, 128), F32),
             jax.ShapeDtypeStruct((slots, width), BF),
         ],
         compiler_params=params(62),
         cost_estimate=cost(2 * slots * tokens * width, 8 * tokens * width),
-    )(token_ids.reshape(1, tokens), table, out_grad)
-    return target, place, counts[:experts, 0], sent
+    )(me, token_ids.reshape(1, tokens), segments, table, out_grad)
+    return columns, leaving, counts[:experts, 0], sent
 
 
 def swap_halves(rows):
@@ -122,7 +133,7 @@
     width = x_ref.shape[1]
     normed, _ = norm_parts(x_ref[...].astype(F32))
     h_one = (normed * gain_ref[...] + bias_ref[...]).astype(BF)
-    h_ref[...] = h_one
+    h_ref[...] = h_one.T
     cosine, sine = cos_ref[...], sin_ref[...]
     for part in range(3):
         raw = dot(h_one, weight_ref[:, part * width : (part + 1) * width])
@@ -158,10 +169,10 @@
         in_specs=[
             row(width), whole((1, width)), whole((1, width)), whole(weight.shape), row(PAIR), row(PAIR),
         ],
-        out_specs=[row(3 * width), row(width)],
+        out_specs=[row(3 * width), pl.BlockSpec((width, block), lambda s: (0, s))],
         out_shape=[
             jax.ShapeDtypeStruct((tokens, 3 * width), BF),
-            jax.ShapeDtypeStruct((tokens, width), BF),
+            jax.ShapeDtypeStruct((width, tokens), BF),
         ],
         compiler_params=params(62),
         cost_estimate=cost(6 * tokens * width * width, 6 * width * width + 12 * tokens * width),
@@ -172,14 +183,14 @@
     return jnp.where((iota((1, PAIR), 1) >= HEAD) == bool(head), rows, jnp.zeros_like(rows))
 
 
-def attend_kernel(block, q_ref, k_ref, v_ref, seg_row_ref, seg_col_ref, mixed_ref, lse_ref, stats):
+def attend_kernel(block, q_ref, k_ref, v_ref, seg_row_ref, seg_col_ref, mixed_ref, turned_ref, lse_ref, stats):
     tokens = q_ref.shape[0]
     pair = pl.program_id(0)
     upper = iota((1, PAIR), 1) >= HEAD
     for first in range(0, tokens, block):
         last = first + block
         query = q_ref[first:last, :]
-        allowed = seg_col_ref[first:last, :] == seg_row_ref[:, :last]
+        allowed = seg_col_ref[first:last, 2:3] == seg_row_ref[:, :last]
         allowed &= iota((block, last), 1) <= iota((block, last), 0) + first
         halves = []
         for head in range(2):
@@ -192,6 +203,7 @@
             lane = iota((1, 128), 1) == 2 * pair + head
             stats[first:last, :] = jnp.where(lane, top + jnp.log(total), stats[first:last, :])
         mixed_ref[first:last, :] = jnp.where(upper, halves[1], halves[0]).astype(BF)
+    turned_ref[...] = mixed_ref[...].T
 
     @pl.when(pair == pl.num_programs(0) - 1)
     def _():
@@ -206,10 +218,11 @@
         functools.partial(attend_kernel, 256),
         name="attend",
         grid=(pairs,),
-        in_specs=[column(0), column(1), column(2), whole((1, tokens)), whole((tokens, 1))],
-        out_specs=[column(0), whole((128, tokens))],
+        in_specs=[column(0), column(1), column(2), whole((1, tokens)), whole((tokens, 8))],
+        out_specs=[column(0), pl.BlockSpec((PAIR, tokens), lambda g: (g, 0)), whole((128, tokens))],
         out_shape=[
             jax.ShapeDtypeStruct((tokens, width), BF),
+            jax.ShapeDtypeStruct((width, tokens), BF),
             jax.ShapeDtypeStruct((128, tokens), F32),
         ],
         scratch_shapes=[pltpu.VMEM((tokens, 128), F32)],
@@ -265,49 +278,76 @@
     return pl.BlockSpec(shape, lambda *_: (0,) * len(shape), pipeline_mode=pl.Buffered(1))
 
 
-def slope_kernel(grads_ref, wout_ref, out_ref):
+def in_distance_order(me, source_ref, target_ref, half):
+    experts = source_ref.shape[0]
+    for distance in range(experts):
+        target_ref[distance * half : (distance + 1) * half, :] = source_ref[me ^ distance, :half, :]
+
+
+def slope_kernel(me_ref, grads_ref, wout_ref, out_ref, near):
     experts, rows, width = grads_ref.shape
     half = rows // 2
-    for chunk in range(2):
-        grads = grads_ref[:, chunk * half : (chunk + 1) * half, :].reshape(experts * half, width)
-        out_ref[chunk * experts * half : (chunk + 1) * experts * half, :] = dot(grads, wout_ref[...], 1, 1)
-
-
-def grads_inside(grads, weight_out):
+    count = experts * half
+
+    @pl.when(pl.program_id(0) == 0)
+    def _():
+        in_distance_order(me_ref[0], grads_ref, near, half)
+
+    weight_out = wout_ref[...]
+    out_ref[:count, :] = dot(near[...], weight_out, 1, 1).astype(BF)
+    out_ref[count:, :] = dot(grads_ref[:, half:, :].reshape(count, width), weight_out, 1, 1).astype(BF)
+
+
+def grads_inside(me, grads, weight_out):
     experts, rows, width = grads.shape
     count = experts * rows
     units = weight_out.shape[0]
-    tile = 512
+    tile = 768
     return pl.pallas_call(
         slope_kernel,
         name="grads_inside",
-        grid=(units // tile,),
-        in_specs=[once(grads.shape), pl.BlockSpec((tile, width), lambda s: (s, 0))],
-        out_specs=pl.BlockSpec((count, tile), lambda s: (0, s)),
-        out_shape=jax.ShapeDtypeStruct((count, units), F32),
+        grid_spec=pltpu.PrefetchScalarGridSpec(
+            num_scalar_prefetch=1,
+            grid=(units // tile,),
+            in_specs=[once(grads.shape), pl.BlockSpec((tile, width), lambda s, me: (s, 0))],
+            out_specs=pl.BlockSpec((count, tile), lambda s, me: (0, s)),
+            scratch_shapes=[pltpu.VMEM((count // 2, width), BF)],
+        ),
+        out_shape=jax.ShapeDtypeStruct((count, units), BF),
         compiler_params=params(62),
         cost_estimate=cost(2 * count * width * units, 4 * count * units),
-    )(grads, weight_out)
-
-
-def expert_kernel(block, has_previous, groups, perm_ref, rows_ref, grads_ref, slope_ref, win_ref, *refs):
+    )(me, grads, weight_out)
+
+
+def expert_kernel(block, pieces, groups, perm_ref, *refs):
     refs = list(refs)
-    previous_ref = refs.pop(0) if has_previous else None
-    act_ref, back_ref, back = refs[-3:]
-    grad_refs = refs[:-3]
-    count, width = rows_ref.shape
+    rows_refs = [refs.pop(0) for _ in range(pieces)]
+    grads_ref, slope_ref, win_ref = refs[:3]
+    del refs[:3]
+    first_chunk = pieces > 1
+    if first_chunk:
+        grad_ref, act_ref, back_ref, back, rows_ref, all_grads = refs
+    else:
+        previous_ref, *grad_refs, act_ref, back_ref, back = refs
+        rows_ref = rows_refs[0]
+    experts, half, width = grads_ref.shape
+    count = experts * half
     step = pl.program_id(0)
 
     @pl.when(step == 0)
     def _():
         back[...] = jnp.zeros_like(back)
+        if first_chunk:
+            in_distance_order(perm_ref[groups + 2], grads_ref, all_grads, half)
+            for distance, piece in enumerate(rows_refs):
+                rows_ref[distance * half : (distance + 1) * half, :] = piece[...]
 
     weight_in = win_ref[...]
-    all_grads = grads_ref[...].reshape(count, width)
+    grads_all = all_grads[...] if first_chunk else grads_ref[...].reshape(count, width)
     din = dout = None
     for first in range(0, count, block):
         span = slice(first, first + block)
-        rows, grads = rows_ref[span, :], all_grads[span, :]
+        rows, grads = rows_ref[span, :], grads_all[span, :]
         inner = dot(rows, weight_in)
         square = inner * inner
         tanh = jnp.tanh(inner * (ROOT + (ROOT * CUBE) * square))
@@ -322,7 +362,10 @@
         part_out = dot(act, grads, 0, 0)
         din = part_in if din is None else din + part_in
         dout = part_out if dout is None else dout + part_out
-    if has_previous:
+    if first_chunk:
+        grad_ref[0, 0] = din
+        grad_ref[0, 1] = dout
+    else:
         din = din + previous_ref[0, 0]
         dout = dout + previous_ref[0, 1]
         swap = perm_ref[groups + step % 2] == 1
@@ -340,32 +383,37 @@
         def _():
             keep_ref[0, 0] = early
             keep_ref[0, 1] = late
-    else:
-        grad_refs[0][0, 0] = din
-        grad_refs[0][0, 1] = dout
 
     @pl.when(step == groups - 1)
     def _():
-        back_ref[...] = back[...].astype(BF)
-
-
-def expert_rows(chunk, rows, grads, slopes, weight_in, perm, previous=None):
-    count, width = rows.shape
-    experts, slots, _ = grads.shape
+        if first_chunk:
+            for distance in range(experts):
+                place = pl.multiple_of((perm_ref[groups + 2] ^ distance) * half, half)
+                back_ref[pl.ds(place, half), :] = back[distance * half : (distance + 1) * half, :].astype(BF)
+        else:
+            back_ref[...] = back[...].astype(BF)
+
+
+def expert_rows(rows, grads, slopes, weight_in, perm, previous=None):
+    chunk = 0 if previous is None else 1
+    experts, slots, width = grads.shape
+    half = slots // 2
+    count = experts * half
     groups = 4
     units = weight_in.shape[1]
     tile = units // groups
     grad_spec = pl.BlockSpec((1, 2, tile, width), lambda s, perm: (s, 0, 0, 0))
-    in_specs = [
-        once((count, width)),
-        pl.BlockSpec((experts, slots // 2, width), lambda s, perm: (0, chunk, 0), pipeline_mode=pl.Buffered(1)),
+    in_specs = [once(piece.shape) for piece in rows] + [
+        pl.BlockSpec((experts, half, width), lambda s, perm: (0, chunk, 0), pipeline_mode=pl.Buffered(1)),
         pl.BlockSpec((count, tile), lambda s, perm: (chunk, perm[s])),
         pl.BlockSpec((width, tile), lambda s, perm: (0, perm[s])),
     ]
-    operands = [rows, grads, slopes, weight_in]
+    operands = [*rows, grads, slopes, weight_in]
+    scratch = [pltpu.VMEM((count, width), F32)]
     if previous is None:
         grad_specs = [grad_spec]
         grad_shapes = [jax.ShapeDtypeStruct((groups, 2, tile, width), F32)]
+        scratch += [pltpu.VMEM((count, width), BF)] * 2
     else:
         in_specs.append(grad_spec)
         operands.append(previous)
@@ -376,7 +424,7 @@
         grad_shapes = [jax.ShapeDtypeStruct((tile, width), BF)] * 4
         grad_shapes += [jax.ShapeDtypeStruct((2, 2, tile, width), BF)]
     return pl.pallas_call(
-        functools.partial(expert_kernel, 512, previous is not None, groups),
+        functools.partial(expert_kernel, 512, len(rows), groups),
         name="expert_rows",
         grid_spec=pltpu.PrefetchScalarGridSpec(
             num_scalar_prefetch=1,
@@ -384,7 +432,7 @@
             in_specs=in_specs,
             out_specs=grad_specs
             + [pl.BlockSpec((count, tile), lambda s, perm: (0, perm[s])), whole((count, width))],
-            scratch_shapes=[pltpu.VMEM((count, width), F32)],
+            scratch_shapes=scratch,
         ),
         out_shape=grad_shapes
         + [jax.ShapeDtypeStruct((count, units), BF), jax.ShapeDtypeStruct((count, width), BF)],
@@ -393,7 +441,7 @@
     )(perm, *operands)
 
 
-def result_kernel(first_ref, second_ref, wout_ref, out_ref, total):
+def result_kernel(me_ref, first_ref, second_ref, wout_ref, out_ref, total):
     step = pl.program_id(0)
     experts, rows, width = out_ref.shape
     half = rows // 2
@@ -408,29 +456,32 @@
 
     @pl.when(step == pl.num_programs(0) - 1)
     def _():
-        for chunk in range(2):
-            out_ref[:, chunk * half : (chunk + 1) * half, :] = (
-                total[chunk].astype(BF).reshape(experts, half, width)
-            )
-
-
-def expert_result(first, second, weight_out, experts):
+        out_ref[:, half:, :] = total[1].astype(BF).reshape(experts, half, width)
+        for distance in range(experts):
+            piece = total[0, distance * half : (distance + 1) * half, :]
+            out_ref[me_ref[0] ^ distance, :half, :] = piece.astype(BF)
+
+
+def expert_result(me, first, second, weight_out, experts):
     count, units = first.shape
     width = weight_out.shape[1]
     tile = 768
-    col = pl.BlockSpec((count, tile), lambda s: (0, s))
+    col = pl.BlockSpec((count, tile), lambda s, me: (0, s))
     shape = (experts, 2 * count // experts, width)
     return pl.pallas_call(
         result_kernel,
         name="expert_result",
-        grid=(units // tile,),
-        in_specs=[col, col, pl.BlockSpec((tile, width), lambda s: (s, 0))],
-        out_specs=whole(shape),
+        grid_spec=pltpu.PrefetchScalarGridSpec(
+            num_scalar_prefetch=1,
+            grid=(units // tile,),
+            in_specs=[col, col, pl.BlockSpec((tile, width), lambda s, me: (s, 0))],
+            out_specs=whole(shape),
+            scratch_shapes=[pltpu.VMEM((2, count, width), F32)],
+        ),
         out_shape=jax.ShapeDtypeStruct(shape, BF),
-        scratch_shapes=[pltpu.VMEM((2, count, width), F32)],
         compiler_params=params(62),
         cost_estimate=cost(4 * count * width * units, 4 * count * units),
-    )(first, second, weight_out)
+    )(me, first, second, weight_out)
 
 
 def place_kernel(count, flags_ref, *refs):
@@ -479,9 +530,8 @@
     )(jnp.stack(flags).astype(I32), *sources, *previous)
 
 
-def gather_rows(block, target_ref, sources):
+def gather_rows(block, target, sources):
     count = sources[0].shape[0]
-    target = target_ref[...]
     total = None
     for chunk, source in enumerate(sources):
         picked = (iota((block, count), 1) + chunk * count == target).astype(F32).astype(BF)
@@ -495,7 +545,7 @@
     grad_middle_ref, grad_mixed_ref, branch_ref, delta_ref, small_ref,
 ):
     step = pl.program_id(0)
-    grad_h = gather_rows(block, target_ref, (back_first_ref, back_second_ref))
+    grad_h = gather_rows(block, target_ref[:, 0:1], (back_first_ref, back_second_ref))
     normed, inv_scale = norm_parts(middle_ref[...])
     gain = gain_ref[...]
     grad_middle = out_grad_ref[...].astype(F32) + norm_back(grad_h, normed, inv_scale, gain)
@@ -537,7 +587,7 @@
         name="middle_back",
         grid=(tokens // block,),
         in_specs=[
-            once((slots // 2, width)), once((slots // 2, width)), row(1), row(width), row(width), row(width),
+            once((slots // 2, width)), once((slots // 2, width)), row(8), row(width), row(width), row(width),
             whole((1, width)), whole(weight.shape), whole((16, width)),
         ],
         out_specs=[
@@ -557,8 +607,8 @@
 
 
 def attend_back_kernel(
-    block, start, q_ref, k_ref, v_ref, do_ref, lse_ref, delta_ref, seg_row_ref, seg_col_ref, cos_ref, sin_ref,
-    dq_ref, dk_ref, dv_ref, total,
+    block, start, side_ref, q_ref, k_ref, v_ref, do_ref, lse_ref, delta_ref, seg_row_ref, seg_col_ref, cos_ref, sin_ref,
+    h_ref, turned_ref, branch_ref, dq_ref, dk_ref, dv_ref, keep_ref, send_ref, total, gathered,
 ):
     tokens = q_ref.shape[0]
     pair = pl.program_id(0) + start
@@ -569,7 +619,7 @@
         last = first + block
         span = tokens - first
         keys, values = k_ref[first:last, :], v_ref[first:last, :]
-        allowed = seg_col_ref[first:last, :] == seg_row_ref[:, first:]
+        allowed = seg_col_ref[first:last, 2:3] == seg_row_ref[:, first:]
         allowed &= iota((block, span), 0) <= iota((block, span), 1)
         dk = dv = dq = None
         for head in range(2):
@@ -594,61 +644,55 @@
             total[first:, :] += dq
     dq = total[...] * 0.125
     dq_ref[...] = (dq * cosine - swap_halves(dq) * sine).astype(BF)
-
-
-def attend_back(qkv, grad_mixed, lse, delta, seg_row, seg_col, cosine, sine, start, count):
+    columns = branch_ref.shape[1]
+    for part, ref in enumerate((dq_ref, dk_ref, dv_ref)):
+        place = pl.ds(pl.multiple_of(part * columns + pl.program_id(0) * PAIR, PAIR), PAIR)
+        gathered[:, place] = ref[...]
+
+    @pl.when(pl.program_id(0) == pl.num_programs(0) - 1)
+    def _():
+        second = side_ref[0] == 1
+        for rows in range(0, h_ref.shape[0], block):
+            rows = slice(rows, rows + block)
+            early = dot(h_ref[rows, :], gathered[:, : 2 * columns])
+            late = [dot(h_ref[rows, :], gathered[:, 2 * columns :]), dot(turned_ref[rows, :], branch_ref[...])]
+            for part in range(2):
+                first = early[:, part * columns : (part + 1) * columns]
+                keep_ref[part, rows, :] = jnp.where(second, late[part], first)
+                send_ref[part, rows, :] = jnp.where(second, first, late[part]).astype(BF)
+
+
+def attend_back(side, qkv, grad_mixed, lse, delta, seg_row, seg_col, cosine, sine, h_turned, mixed_turned, branch, start, count):
     tokens, width = grad_mixed.shape
     pairs = width // PAIR
-    column = lambda part: pl.BlockSpec((tokens, PAIR), lambda g: (0, part * pairs + start + g))
+    column = lambda part: pl.BlockSpec((tokens, PAIR), lambda g, side: (0, part * pairs + start + g))
+    shared = whole((2, width, count * PAIR))
+    branches = pl.BlockSpec(
+        (tokens, count * PAIR), lambda g, side: (0, start // count), pipeline_mode=pl.Buffered(1)
+    )
     out = jax.ShapeDtypeStruct((tokens, count * PAIR), BF)
     return pl.pallas_call(
         functools.partial(attend_back_kernel, 256, start),
         name="attend_back",
-        grid=(count,),
-        in_specs=[
-            column(0), column(1), column(2), column(0), whole(lse.shape), whole(delta.shape),
-            whole((1, tokens)), whole((tokens, 1)), whole((tokens, PAIR)), whole((tokens, PAIR)),
-        ],
-        out_specs=[pl.BlockSpec((tokens, PAIR), lambda g: (0, g))] * 3,
-        out_shape=[out] * 3,
-        scratch_shapes=[pltpu.VMEM((tokens, PAIR), F32)],
-        compiler_params=params(62),
-        cost_estimate=cost(20 * tokens * tokens * PAIR * count, 14 * tokens * PAIR * count, 2 * tokens * tokens * count),
-    )(qkv, qkv, qkv, grad_mixed, lse, delta, seg_row, seg_col, cosine, sine)
-
-
-def shared_kernel(side_ref, h_ref, dq_ref, dk_ref, dv_ref, mixed_ref, branch_ref, keep_ref, send_ref):
-    parts = [dot(h_ref[...], ref[...], 0, 0) for ref in (dq_ref, dk_ref, dv_ref)]
-    parts.append(dot(mixed_ref[...], branch_ref[...], 0, 0))
-    second = side_ref[0] == 1
-    for part in range(2):
-        keep_ref[part] = jnp.where(second, parts[2 + part], parts[part])
-        send_ref[part] = jnp.where(second, parts[part], parts[2 + part]).astype(BF)
-
-
-def shared_grads(side, h_one, grads, mixed, branch, which):
-    tokens, width = h_one.shape
-    columns = grads[0].shape[1]
-    block = 256
-    row = pl.BlockSpec((tokens, block), lambda s, side: (0, s))
-    out = pl.BlockSpec((2, block, columns), lambda s, side: (0, s, 0))
-    return pl.pallas_call(
-        shared_kernel,
-        name="shared_grads",
         grid_spec=pltpu.PrefetchScalarGridSpec(
             num_scalar_prefetch=1,
-            grid=(width // block,),
-            in_specs=[row] + [once((tokens, columns))] * 3
-            + [row, pl.BlockSpec((tokens, columns), lambda s, side: (0, which), pipeline_mode=pl.Buffered(1))],
-            out_specs=[out, out],
+            grid=(count,),
+            in_specs=[
+                column(0), column(1), column(2), column(0), once(lse.shape), once(delta.shape),
+                once((1, tokens)), once((tokens, 8)), once((tokens, PAIR)), once((tokens, PAIR)),
+                once((width, tokens)), once((width, tokens)), branches,
+            ],
+            out_specs=[pl.BlockSpec((tokens, PAIR), lambda g, side: (0, g))] * 3 + [shared, shared],
+            scratch_shapes=[pltpu.VMEM((tokens, PAIR), F32), pltpu.VMEM((tokens, 3 * count * PAIR), BF)],
         ),
-        out_shape=[
-            jax.ShapeDtypeStruct((2, width, columns), F32),
-            jax.ShapeDtypeStruct((2, width, columns), BF),
-        ],
-        compiler_params=params(62),
-        cost_estimate=cost(8 * tokens * width * columns, 16 * width * columns + 12 * tokens * columns),
-    )(side, h_one, *grads, mixed, branch)
+        out_shape=[out] * 3
+        + [
+            jax.ShapeDtypeStruct((2, width, count * PAIR), F32),
+            jax.ShapeDtypeStruct((2, width, count * PAIR), BF),
+        ],
+        compiler_params=params(62),
+        cost_estimate=cost(20 * tokens * tokens * PAIR * count, 14 * tokens * PAIR * count, 2 * tokens * tokens * count),
+    )(side, qkv, qkv, qkv, grad_mixed, lse, delta, seg_row, seg_col, cosine, sine, h_turned, mixed_turned, branch)
 
 
 def final_kernel(x_ref, *refs):
@@ -699,7 +743,7 @@
 
 
 def output_kernel(block, result_ref, target_ref, middle_ref, out_ref):
-    out_ref[...] = (middle_ref[...] + gather_rows(block, target_ref, (result_ref,))).astype(BF)
+    out_ref[...] = (middle_ref[...] + gather_rows(block, target_ref[:, 1:2], (result_ref,))).astype(BF)
 
 
 def block_output(result, place_col, middle):
@@ -711,7 +755,7 @@
         functools.partial(output_kernel, block),
         name="block_output",
         grid=(tokens // block,),
-        in_specs=[once((slots, width)), row(1), row(width)],
+        in_specs=[once((slots, width)), row(8), row(width)],
         out_specs=row(width),
         out_shape=jax.ShapeDtypeStruct((tokens, width), BF),
         compiler_params=params(62),
@@ -816,7 +860,7 @@
     half = tokens // experts
     row = lambda vector: vector.reshape(1, width)
     cosine, sine = (jnp.asarray(table) for table in angle_tables(tokens))
-    seg_row, seg_col = segment_ids.reshape(1, tokens), segment_ids.reshape(tokens, 1)
+    seg_row = segment_ids.reshape(1, tokens)
     weight_in, weight_out = expert_in[0], expert_out[0]
 
     def exchange(rows):
@@ -830,28 +874,31 @@
         return rows[:tokens], rows[tokens:]
 
     x_side, y_side = side("dp", 1), side("dp", 2)
-    perm = jnp.stack([1 - x_side, 3 - y_side, x_side, 2 + y_side, y_side, x_side]).astype(I32)
+    place_here = lax.axis_index("expert")
+    perm = jnp.stack([1 - x_side, 3 - y_side, x_side, 2 + y_side, y_side, x_side, place_here]).astype(I32)
+    me = jnp.reshape(place_here, (1,)).astype(I32)
     tie = lambda *values: lax.optimization_barrier(values)
 
-    target, place, counts, sent_grads = route(token_ids, hash_table, out_grad, experts, half)
-    target_col, place_col = target.reshape(tokens, 1), place.reshape(tokens, 1)
+    columns, leaving, counts, sent_grads = route(me, token_ids, seg_row, hash_table, out_grad, experts, half)
     sent_grads, hidden_in = tie(sent_grads, hidden_in)
     grad_rows = exchange(sent_grads)
-    qkv, h_one = first_half(hidden_in, row(ln1_gain), row(ln1_bias), qkv_weight, cosine, sine)
-    mixed, lse = attend(qkv, seg_row, seg_col)
-    middle, sent_rows = middle_part(mixed, proj_weight, hidden_in, row(ln2_gain), row(ln2_bias), target)
+    qkv, h_turned = first_half(hidden_in, row(ln1_gain), row(ln1_bias), qkv_weight, cosine, sine)
+    mixed, mixed_turned, lse = attend(qkv, seg_row, columns)
+    middle, sent_rows = middle_part(mixed, proj_weight, hidden_in, row(ln2_gain), row(ln2_bias), leaving)
     sent_first, sent_second = split(sent_rows)
-    sent_first, grad_rows = tie(sent_first, grad_rows)
-    rows_first = exchange_half(sent_first)
-    slopes = grads_inside(grad_rows, weight_out)
-    sent_second, rows_first, slopes = tie(sent_second, rows_first, slopes)
+    sent_first = sent_first.reshape(experts, half, width)
+    rows_first = [sent_first[0]] + [
+        lax.ppermute(sent_first[bits], "expert", partner("expert", bits)) for bits in range(1, experts)
+    ]
+    slopes = grads_inside(me, grad_rows, weight_out)
+    sent_second, grad_rows, slopes, *rows_first = tie(sent_second, grad_rows, slopes, *rows_first)
     rows_second = exchange_half(sent_second)
 
-    previous, act_first, back_first = expert_rows(0, rows_first, grad_rows, slopes, weight_in, perm)
+    previous, act_first, back_first = expert_rows(rows_first, grad_rows, slopes, weight_in, perm)
     back_first, rows_second = tie(back_first, rows_second)
     back_first = exchange_half(back_first)
     early_x, late_x, early_y, late_y, keep, act_second, back_second = expert_rows(
-        1, rows_second, grad_rows, slopes, weight_in, perm, previous
+        [rows_second], grad_rows, slopes, weight_in, perm, previous
     )
     across_x = lambda value: lax.ppermute(value, "dp", partner("dp", 1))
     across_y = lambda value: lax.ppermute(value, "dp", partner("dp", 2))
@@ -859,7 +906,7 @@
     back_second = exchange_half(back_second)
     early_x, early_y = across_x(early_x), across_y(early_y)
     late_x, late_y = across_x(late_x), across_y(late_y)
-    result = expert_result(act_first, act_second, weight_out, experts)
+    result = expert_result(me, act_first, act_second, weight_out, experts)
     result, back_second = tie(result, back_second)
 
     plus = lambda *values: sum(value.astype(F32) for value in values).astype(BF)
@@ -867,34 +914,38 @@
     send_x, send_y, back_second = tie(send_x, send_y, back_second)
     other_x, other_y = across_y(send_x), across_x(send_y)
     grad_middle, grad_mixed, branch, delta, small_two = middle_back(
-        back_first, back_second, target_col, middle, mixed, out_grad, row(ln2_gain), proj_weight
-    )
-    grad_mixed, late_x, late_y, result = tie(grad_mixed, late_x, late_y, result)
-    result = exchange(result.reshape(2 * tokens, width))
+        back_first, back_second, columns, middle, mixed, out_grad, row(ln2_gain), proj_weight
+    )
+    grad_mixed, late_x, late_y = tie(grad_mixed, late_x, late_y)
 
     pairs = width // PAIR
     back_of = lambda grads, start: attend_back(
-        qkv, grads, lse, delta, seg_row, seg_col, cosine, sine, start, pairs // 2
+        core_side, qkv, grads, lse, delta, seg_row, columns, cosine, sine, h_turned, mixed_turned, branch, start, pairs // 2
     )
     core_side = jnp.reshape(side("expert", 1), (1,)).astype(I32)
     across_core = lambda value: lax.ppermute(value, "expert", partner("expert", 1))
-    grads_low = back_of(grad_mixed, 0)
-    other_x, other_y, grads_low, grad_mixed = tie(other_x, other_y, grads_low, grad_mixed)
+    *grads_low, low, send_low = back_of(grad_mixed, 0)
+    other_x, other_y, send_low, grad_mixed = tie(other_x, other_y, send_low, grad_mixed)
     runs = [slice(0, width // 2), slice(width // 2, width)]
-    total_x = [plus(keep[0, 1, run], late_x[run], other_x[run]) for run in runs]
-    total_y = [plus(keep[1, 1, run], late_y[run], other_y[run]) for run in runs]
-    total_x, total_y, grads_low = tie(total_x, total_y, grads_low)
-    near_x, near_y = [across_y(run) for run in total_x], [across_x(run) for run in total_y]
-    far_x, far_y = across_x(total_x[0]), across_y(total_y[0])
-    low, send_low = shared_grads(core_side, h_one, grads_low, mixed, branch, 0)
-    send_low, grad_mixed = tie(send_low, grad_mixed)
+    total_x = plus(keep[0, 1], late_x, other_x)
+    total_y = plus(keep[1, 1], late_y, other_y)
+    total_x, total_y, send_low, grad_mixed, result = tie(total_x, total_y, send_low, grad_mixed, result)
+    result = exchange(result.reshape(2 * tokens, width))
+    near_x, near_y = across_y(total_x), across_x(total_y)
+    far_x, far_y = across_x(total_x[runs[0]]), across_y(total_y[runs[0]])
     got_low = across_core(send_low)
-    grads_high = back_of(grad_mixed, pairs // 2)
-    high, send_high = shared_grads(core_side, h_one, grads_high, mixed, branch, 1)
-    near_x, near_y, far_x, far_y, got_low, send_high = tie(near_x, near_y, far_x, far_y, got_low, send_high)
+    *grads_high, high, send_high = back_of(grad_mixed, pairs // 2)
+    near_x, near_y, got_low, send_high = tie(near_x, near_y, got_low, send_high)
+    both_runs = lambda group, which: [group, which, 0, group, which, 1]
+    grad_in, grad_out = place_blocks(
+        [x_side, y_side, 0, x_side, 1 - y_side, 0, 2 + y_side, x_side, 0, 2 + y_side, 1 - x_side, 0],
+        [total_x, near_x, total_y, near_y],
+    )
+    send_high, grad_in, grad_out, far_x, far_y = tie(send_high, grad_in, grad_out, far_x, far_y)
+    got_high = across_core(send_high)
 
     low = (low + got_low.astype(F32)).reshape(8, width // 4, width // 2)
-    high = (high + across_core(send_high).astype(F32)).reshape(8, width // 4, width // 2)
+    high = (high + got_high.astype(F32)).reshape(8, width // 4, width // 2)
     far_bits = axis_bits("expert")[1:]
     low_order = axis_bits("dp") + far_bits
     high_order = axis_bits("dp")[::-1] + far_bits
@@ -913,14 +964,11 @@
     for axis, bit in axis_bits("dp"):
         small = add_partner(small, axis, bit)
     low, high = reduce_both(low, high, 1)
-    both_runs = lambda group, which: [group, which, 0, group, which, 1]
-    grad_in, grad_out = place_blocks(
-        both_runs(x_side, y_side) + both_runs(x_side, 1 - y_side)
-        + both_runs(2 + y_side, x_side) + both_runs(2 + y_side, 1 - x_side),
-        [*total_x, *near_x, *total_y, *near_y],
-    )
-    low, high, small, total_x, total_y, near_x, near_y, grad_in, result = tie(
-        low, high, small, total_x, total_y, near_x, near_y, grad_in, result
+    total_x, total_y, near_x, near_y = (
+        [value[run] for run in runs] for value in (total_x, total_y, near_x, near_y)
+    )
+    low, high, small, total_x, total_y, near_x, near_y, result = tie(
+        low, high, small, total_x, total_y, near_x, near_y, result
     )
     far_x, far_y = [far_x, across_x(total_x[1])], [far_y, across_y(total_y[1])]
     last_x, last_y = [across_x(run) for run in near_x], [across_y(run) for run in near_y]
@@ -946,7 +994,7 @@
     )
     low, high, grad_in, grad_out = tie(low, high, grad_in, grad_out)
     low, high = gather_step(low, *low_order[0]), gather_step(high, *high_order[0])
-    block_out = block_output(result.reshape(2 * tokens, width), place_col, middle)
+    block_out = block_output(result.reshape(2 * tokens, width), columns, middle)
     low, high, block_out = tie(low, high, block_out)
     low, high = low.reshape(2, width, width // 2), high.reshape(2, width, width // 2)
     got_low, got_high = across_core(low), across_core(high)

time: 474 us -> 466 us (0.983)
  waiting for transfers between devices: 101 us -> 87.5 us
  starting transfers between devices: 68 us -> 73.5 us
    all_to_all x6 -> x5, waiting for transfers between devices: 55.1 us -> 35.8 us  [exchange(): lax.all_to_all(sent, 'expert', split_axis=0, concat_axis=0, tiled=True)]
    pallas_call x6 -> x4, Pallas kernels: 112 us -> 95.5 us  [the longest x2 65.7 us: expert_rows(): pl.pallas_call(functools.partial(expert_kernel, 512, len(rows), groups),...]
    ppermute x0 -> x7, starting transfers between devices: none -> 12.6 us  [local(): lax.ppermute(sent_first[bits], 'expert', partner('expert', bits))]
    pallas_call x2, Pallas kernels: 31.5 us -> 43.9 us  [attend_back(): pl.pallas_call(functools.partial(attend_back_kernel, 256, start), name='a...]
    slice x1 -> x5, local copies, waits for them, and re-layouts: 0.11 us -> 8.77 us  [the longest x3 6.21 us: local(): value[run]]
    all_to_all x6 -> x5, starting transfers between devices: 27.8 us -> 23.9 us  [exchange(): lax.all_to_all(sent, 'expert', split_axis=0, concat_axis=0, tiled=True)]
    ppermute x9 -> x8, waiting for transfers between devices: 23.3 us -> 25 us  [local(): across_x = lambda value: lax.ppermute(value, 'dp', partner('dp', 1))]
    ppermute x9 -> x8, starting transfers between devices: 10.4 us -> 9.1 us  [local(): across_y = lambda value: lax.ppermute(value, 'dp', partner('dp', 2))]
  transfers between devices with their start and end apart: 44 -> 48, of which waited for: 25 -> 25; matrix products, arithmetic and copies ran while one was open for 8% -> 7% of each run, Pallas kernels for 51% -> 51%
where the time goes in v3:
time: 466 us; the launch traced here: 457 us
  Pallas kernels  246 us (53%)
  waiting for transfers between devices  87.5 us (19%)
  starting transfers between devices  73.5 us (16%)
  other arithmetic  24.9 us (5%)
  local copies, waits for them, and re-layouts  23.1 us (5%)
    pallas_call x2, Pallas kernels, expert_rows(): pl.pallas_call(functools.partial(expert_kernel, 512, len(rows), groups),...  65.7 us
    pallas_call x2, Pallas kernels, attend_back(): pl.pallas_call(functools.partial(attend_back_kernel, 256, start), name='a...  43.9 us
    all_to_all x5, waiting for transfers between devices, exchange(): lax.all_to_all(sent, 'expert', split_axis=0, concat_axis=0, tiled=True)  35.8 us
    ppermute x8, waiting for transfers between devices, local(): across_x = lambda value: lax.ppermute(value, 'dp', partner('dp', 1))  25 us
    pallas_call x1, Pallas kernels, attend(): pl.pallas_call(functools.partial(attend_kernel, 256), name='attend', grid...  25 us
    all_to_all x5, starting transfers between devices, exchange(): lax.all_to_all(sent, 'expert', split_axis=0, concat_axis=0, tiled=True)  23.9 us
    pallas_call x1, Pallas kernels, expert_result(): pl.pallas_call(result_kernel, name='expert_result', grid_spec=pltpu.Prefe...  15.1 us
    pallas_call x1, Pallas kernels, grads_inside(): pl.pallas_call(slope_kernel, name='grads_inside', grid_spec=pltpu.Prefetc...  14.7 us
  transfers between devices with their start and end apart: 48, of which 25 were waited for; matrix products, arithmetic and copies ran while one was open for 7% of the time, Pallas kernels for 51%

profile of v3, /device:TPU:0, one launch (start us, length us, event | category | flops | bytes accessed | tf_op | source)
XLA Modules:
  0.0 456.7 jit_solution(1184678983596917846)
XLA Ops:
  2.3 8.3 %route.1 = (s32[1024,8]{1,0:T(8,128)}, s32[1,1024]{1,0:T(1,128)}, f32[16,128]{1,0:T(8,128)}, bf16[2048,768]{1,0:T(8,128)(2,1)}) custom-call(s32[1]{0:T(128)} %bitcast.1.me_ref, s32[1,1024]{1,0:T(1,128)} %bitcast.64, s32[1,1024]{1,0:T(1,128)} %bitcast.60, bf16[512,128]{1,0:T(8,128)(2,1)} %pad_bitcast_fusion.table_ref, bf16[1024,768]{1,0:T(8,128)(2,1)} %out_grad_ref.1), custom_call_target="tpu_custom_call" | custom-call | flops 1 | bytes 1 | tf_op jit(solution)/shard_map/route/pallas_call | solution.py:98
  10.6 6.5 %all-to-all-start = ((bf16[8,256,768]{2,1,0:T(8,128)(2,1)}), bf16[8,256,768]{2,1,0:T(8,128)(2,1)}, u32[]{:S(2)}, u32[]{:S(2)}) async-start(bf16[8,256,768]{2,1,0:T(8,128)(2,1)} %bitcast.57), calls=%async_computation | async-start | bytes 6291456 | tf_op jit(solution)/shard_map/all_to_all | solution.py:868
  18.2 9.1 %norm_project.1 = (bf16[1024,2304]{1,0:T(8,128)(2,1)}, bf16[768,1024]{1,0:T(8,128)(2,1)}) custom-call(bf16[1024,768]{1,0:T(8,128)(2,1)} %x_ref.2, f32[1,768]{1,0:T(1,128)} %reshape.117.gain_ref.refs_8_, f32[1,768]{1,0:T(1,128)} %reshape.118.bias_ref, bf16[768,2304]{1,0:T(8,128)(2,1)} %refs_7_.1, f32[1024,128]{1,0:T(8,128)} %constant.128.clone.cos_ref, ...), custom_call_target="tpu_custom_call" | custom-call | flops 1 | bytes 1 | tf_op jit(solution)/shard_map/norm_project/pallas_call | solution.py:165
  27.3 25.0 %attend.1 = (bf16[1024,768]{1,0:T(8,128)(2,1)}, bf16[768,1024]{1,0:T(8,128)(2,1)}, f32[128,1024]{1,0:T(8,128)}) custom-call(bf16[1024,2304]{1,0:T(8,128)(2,1)} %get-tuple-element.142.q_ref.k_ref.v_ref, bf16[1024,2304]{1,0:T(8,128)(2,1)} %get-tuple-element.142.q_ref.k_ref.v_ref, bf16[1024,2304]{1,0:T(8,128)(2,1)} %get-tuple-element.142.q_ref.k_ref.v_ref, ...), custom_call_target="tpu_custom_call" | custom-call | flops 1 | bytes 1 | tf_op jit(solution)/shard_map/attend/pallas_call | solution.py:217
  53.5 10.5 %project_dispatch.1 = (f32[1024,768]{1,0:T(8,128)}, bf16[2048,768]{1,0:T(8,128)(2,1)}) custom-call(bf16[1024,768]{1,0:T(8,128)(2,1)} %get-tuple-element.144.mixed_ref, bf16[768,768]{1,0:T(8,128)(2,1)} %weight_ref.5, bf16[1024,768]{1,0:T(8,128)(2,1)} %x_ref.2, f32[1,768]{1,0:T(1,128)} %reshape.119.gain_ref, f32[1,768]{1,0:T(1,128)} %reshape.120.bias_ref, ...), custom_call_target="tpu_custom_call" | custom-call | flops 1 | bytes 1 | tf_op jit(solution)/shard_map/project_dispatch/pallas_call | solution.py:254
  76.7 4.2 collective-permute-start.6
  82.1 23.9 %all-to-all-done.grads_ref.refs_8_.refs_1_ = bf16[8,256,768]{2,1,0:T(8,128)(2,1)} async-done(((bf16[8,256,768]{2,1,0:T(8,128)(2,1)}), bf16[8,256,768]{2,1,0:T(8,128)(2,1)}, u32[]{:S(2)}, u32[]{:S(2)}) %all-to-all-start) | async-done | bytes 3145760 | tf_op jit(solution)/shard_map/all_to_all | solution.py:868
  106.0 14.7 %grads_inside.1.refs_9_.refs_2_ = bf16[2048,3072]{1,0:T(8,128)(2,1)} custom-call(s32[1]{0:T(128)} %bitcast.1.me_ref, bf16[8,256,768]{2,1,0:T(8,128)(2,1)} %all-to-all-done.grads_ref.refs_8_.refs_1_, bf16[3072,768]{1,0:T(8,128)(2,1)} %bitcast.44), custom_call_target="tpu_custom_call" | custom-call | flops 1 | bytes 1 | tf_op jit(solution)/shard_map/grads_inside/pallas_call | solution.py:306
  121.7 3.8 all-to-all-start.1
  126.2 31.4 %expert_rows.2 = (f32[4,2,768,768]{3,2,1,0:T(8,128)}, bf16[1024,3072]{1,0:T(8,128)(2,1)}, bf16[1024,768]{1,0:T(8,128)(2,1)}) custom-call(s32[7]{0:T(128)} %stack.23.perm_ref, bf16[128,768]{1,0:T(8,128)(2,1)} %get-tuple-element.148.refs_0_, bf16[128,768]{1,0:T(8,128)(2,1)} %copy-done.15, bf16[128,768]{1,0:T(8,128)(2,1)} %copy-done.16, ...), custom_call_target="tpu_custom_call" | custom-call | flops 1 | bytes 1 | tf_op jit(solution)/shard_map/expert_rows/pallas_call | solution.py:426
  157.6 5.7 %all-to-all-done.1 = bf16[8,128,768]{2,1,0:T(8,128)(2,1)S(1)} async-done(((bf16[8,128,768]{2,1,0:T(8,128)(2,1)}), bf16[8,128,768]{2,1,0:T(8,128)(2,1)S(1)}, u32[]{:S(2)}, u32[]{:S(2)}) %all-to-all-start.1) | async-done | bytes 1572896 | tf_op jit(solution)/shard_map/all_to_all | solution.py:868
  164.4 4.5 all-to-all-start.2
  169.0 34.3 %expert_rows.3 = (bf16[768,768]{1,0:T(8,128)(2,1)}, bf16[768,768]{1,0:T(8,128)(2,1)}, bf16[768,768]{1,0:T(8,128)(2,1)}, bf16[768,768]{1,0:T(8,128)(2,1)}, bf16[2...) custom-call(s32[7]{0:T(128)} %stack.23.perm_ref, bf16[1024,768]{1,0:T(8,128)(2,1)} %bitcast.52, ...), custom_call_target="tpu_custom_call" | custom-call | flops 1 | bytes 1 | tf_op jit(solution)/shard_map/expert_rows/pallas_call | solution.py:426
  203.3 3.5 all-to-all-done.2
  206.8 4.0 all-to-all-start.3
  215.0 15.1 %expert_result.1 = bf16[8,256,768]{2,1,0:T(8,128)(2,1)} custom-call(s32[1]{0:T(128)} %bitcast.1.me_ref, bf16[1024,3072]{1,0:T(8,128)(2,1)} %get-tuple-element.168.first_ref, bf16[1024,3072]{1,0:T(8,128)(2,1)} %get-tuple-element.169.second_ref, bf16[3072,768]{1,0:T(8,128)(2,1)} %bitcast.45), custom_call_target="tpu_custom_call" | custom-call | flops 1 | bytes 1 | tf_op jit(solution)/shard_map/expert_result/pallas_call | solution.py:471
  230.1 10.0 %collective-permute-done.7 = bf16[768,768]{1,0:T(8,128)(2,1)} collective-permute-done((bf16[768,768]{1,0:T(8,128)(2,1)}, bf16[768,768]{1,0:T(8,128)(2,1)}, u32[]{:S(2)}, u32[]{:S(2)}) %collective-permute-start.7) | collective-permute-done | bytes 1179680 | tf_op jit(solution)/shard_map/ppermute | solution.py:903
  241.6 4.3 fusion.4
  251.6 13.7 %middle_back.1 = (f32[1024,768]{1,0:T(8,128)}, bf16[1024,768]{1,0:T(8,128)(2,1)}, bf16[1024,768]{1,0:T(8,128)(2,1)}, f32[16,1024]{1,0:T(8,128)}, f32[8,768]{1,0:T(8,128)}) custom-call(bf16[1024,768]{1,0:T(8,128)(2,1)} %bitcast.16.back_first_ref, bf16[1024,768]{1,0:T(8,128)(2,1)} %bitcast.54, s32[1024,8]{1,0:T(8,128)} %get-tuple-element.143.seg_col_ref.target_ref, ...), custom_call_target="tpu_custom_call" | custom-call | flops 1 | bytes 1 | tf_op jit(solution)/shard_map/middle_back/pallas_call | solution.py:585
  266.8 22.1 %attend_back.2 = (bf16[1024,384]{1,0:T(8,128)(2,1)}, bf16[1024,384]{1,0:T(8,128)(2,1)}, bf16[1024,384]{1,0:T(8,128)(2,1)}, f32[2,768,384]{2,1,0:T(8,128)}, bf16[2,768,384]{2,1,0:T(8,128)(2,1)}) custom-call(s32[1]{0:T(128)} %bitcast.side_ref.flag_ref, bf16[1024,2304]{1,0:T(8,128)(2,1)} %get-tuple-element.142.q_ref.k_ref.v_ref, ...), custom_call_target="tpu_custom_call" | custom-call | flops 1 | bytes 1 | tf_op jit(solution)/shard_map/attend_back/pallas_call | solution.py:674
  291.3 5.0 %fusion.1 = (bf16[768,768]{1,0:T(8,128)(2,1)S(1)}, bf16[768,768]{1,0:T(8,128)(2,1)}) fusion(bf16[768,768]{1,0:T(8,128)(2,1)} %collective-permute-done.12, bf16[768,768]{1,0:T(8,128)(2,1)} %collective-permute-done.10, bf16[2,2,768,768]{3,2,1,0:T(8,128)(2,1)} %get-tuple-element.165, bf16[768,768]{1,0:T(8,128)(2,1)} %collective-permute-done.11, ...), kind=kLoop, calls=%fused_computation.2 | loop fusion | flops 7077888 | bytes 9437184 | tf_op jit(solution)/shard_map/convert_element_type | solution.py:912
  296.3 5.0 %all-to-all-start.4 = ((bf16[8,256,768]{2,1,0:T(8,128)(2,1)}), bf16[8,256,768]{2,1,0:T(8,128)(2,1)}, u32[]{:S(2)}, u32[]{:S(2)}) async-start(bf16[8,256,768]{2,1,0:T(8,128)(2,1)} %expert_result.1), calls=%async_computation.4 | async-start | bytes 6291456 | tf_op jit(solution)/shard_map/all_to_all | solution.py:868
  309.6 21.8 %attend_back.3 = (bf16[1024,384]{1,0:T(8,128)(2,1)}, bf16[1024,384]{1,0:T(8,128)(2,1)}, bf16[1024,384]{1,0:T(8,128)(2,1)}, f32[2,768,384]{2,1,0:T(8,128)}, bf16[2,768,384]{2,1,0:T(8,128)(2,1)}) custom-call(s32[1]{0:T(128)} %bitcast.side_ref.flag_ref, bf16[1024,2304]{1,0:T(8,128)(2,1)} %get-tuple-element.142.q_ref.k_ref.v_ref, ...), custom_call_target="tpu_custom_call" | custom-call | flops 1 | bytes 1 | tf_op jit(solution)/shard_map/attend_back/pallas_call | solution.py:674
  331.8 6.9 %place_blocks.2 = (f32[768,3072]{1,0:T(8,128)}, f32[3072,768]{1,0:T(8,128)}) custom-call(s32[12]{0:T(128)} %stack.25.flags_ref, bf16[768,768]{1,0:T(8,128)(2,1)} %get-tuple-element.194.refs_0_, bf16[768,768]{1,0:T(8,128)(2,1)} %collective-permute-done.13.refs_1_, bf16[768,768]{1,0:T(8,128)(2,1)} %copy-done, bf16[768,768]{1,0:T(8,128)(2,1)} %collective-permute-done.14.refs_3_), custom_call_target="tpu_custom_call" | custom-call | flops 1 | bytes 1 | tf_op jit(solution)/shard_map/place_blocks/pallas_call | solution.py:513
  338.7 5.0 %collective-permute-done.17.refs_0_ = bf16[384,768]{1,0:T(8,128)(2,1)S(1)} collective-permute-done((bf16[384,768]{1,0:T(8,128)(2,1)}, bf16[384,768]{1,0:T(8,128)(2,1)S(1)}, u32[]{:S(2)}, u32[]{:S(2)}) %collective-permute-start.17) | collective-permute-done | bytes 589856 | tf_op jit(solution)/shard_map/ppermute | solution.py:903
  350.6 11.2 %first_back.1 = (f32[1024,768]{1,0:T(8,128)}, f32[8,768]{1,0:T(8,128)}) custom-call(bf16[1024,768]{1,0:T(8,128)(2,1)} %x_ref.2, bf16[1024,384]{1,0:T(8,128)(2,1)} %get-tuple-element.207.refs_0_, bf16[1024,384]{1,0:T(8,128)(2,1)} %get-tuple-element.208.refs_1_, bf16[1024,384]{1,0:T(8,128)(2,1)} %get-tuple-element.209.refs_2_, ...), custom_call_target="tpu_custom_call" | custom-call | flops 1 | bytes 1 | tf_op jit(solution)/shard_map/first_back/pallas_call | solution.py:730
  387.3 7.7 %collective-permute-done.27.refs_1_ = bf16[384,768]{1,0:T(8,128)(2,1)S(1)} collective-permute-done((bf16[384,768]{1,0:T(8,128)(2,1)}, bf16[384,768]{1,0:T(8,128)(2,1)S(1)}, u32[]{:S(2)}, u32[]{:S(2)}) %collective-permute-start.27) | collective-permute-done | bytes 589856 | tf_op jit(solution)/shard_map/ppermute | solution.py:903
  421.5 6.7 %place_blocks.3 = (f32[768,3072]{1,0:T(8,128)}, f32[3072,768]{1,0:T(8,128)}) custom-call(s32[24]{0:T(128)} %stack.26.flags_ref, bf16[384,768]{1,0:T(8,128)(2,1)} %copy-done.10, bf16[384,768]{1,0:T(8,128)(2,1)} %copy-done.11, bf16[384,768]{1,0:T(8,128)(2,1)} %copy-done.12, ...), custom_call_target="tpu_custom_call", output_to_operand_aliasing={{0}: (9, {}), {1}: (10, {})} | custom-call | flops 1 | bytes 1 | tf_op jit(solution)/shard_map/place_blocks/pallas_call | solution.py:513
  430.6 7.4 %block_output.1 = bf16[1024,768]{1,0:T(8,128)(2,1)} custom-call(bf16[2048,768]{1,0:T(8,128)(2,1)} %bitcast.26.result_ref, s32[1024,8]{1,0:T(8,128)} %get-tuple-element.143.seg_col_ref.target_ref, f32[1024,768]{1,0:T(8,128)} %get-tuple-element.173.middle_ref), custom_call_target="tpu_custom_call" | custom-call | flops 1 | bytes 1 | tf_op jit(solution)/shard_map/block_output/pallas_call | solution.py:754
  438.0 3.9 collective-permute-done.40
  448.4 3.9 shared_outputs.2
  452.3 3.9 shared_outputs.3
  (189 shorter events, 111.9 us)
Async XLA Ops:
  10.6 95.4 %all-to-all-start = ((bf16[8,256,768]{2,1,0:T(8,128)(2,1)}), bf16[8,256,768]{2,1,0:T(8,128)(2,1)}, u32[]{:S(2)}, u32[]{:S(2)}) async-start(bf16[8,256,768]{2,1,0:T(8,128)(2,1)} %bitcast.57), calls=%async_computation | async-start | bytes 6291456 | tf_op jit(solution)/shard_map/all_to_all | solution.py:868
  68.6 52.1 %collective-permute-start.2 = (bf16[128,768]{1,0:T(8,128)(2,1)}, bf16[128,768]{1,0:T(8,128)(2,1)S(1)}, u32[]{:S(2)}, u32[]{:S(2)}) collective-permute-start(bf16[128,768]{1,0:T(8,128)(2,1)} %get-tuple-element.281), channel_id=1, source_target_pairs={{0,3},{1,2},{2,1},{3,0},{4,7},{5,6},{6,5},{7,4},{8,11},{9,10},{10,... | collective-permute-start | bytes 589832 | tf_op jit(solution)/shard_map/ppermute | solution.py:891
  68.6 52.1 %collective-permute-start.3 = (bf16[128,768]{1,0:T(8,128)(2,1)}, bf16[128,768]{1,0:T(8,128)(2,1)S(1)}, u32[]{:S(2)}, u32[]{:S(2)}) collective-permute-start(bf16[128,768]{1,0:T(8,128)(2,1)} %get-tuple-element.280), channel_id=1, source_target_pairs={{0,4},{1,5},{2,6},{3,7},{4,0},{5,1},{6,2},{7,3},{8,12},{9,13},{10,... | collective-permute-start | bytes 589832 | tf_op jit(solution)/shard_map/ppermute | solution.py:891
  71.2 49.6 %collective-permute-start.4 = (bf16[128,768]{1,0:T(8,128)(2,1)S(1)}, bf16[128,768]{1,0:T(8,128)(2,1)S(1)}, u32[]{:S(2)}, u32[]{:S(2)}) collective-permute-start(bf16[128,768]{1,0:T(8,128)(2,1)S(1)} %get-tuple-element.279), channel_id=1, source_target_pairs={{0,5},{1,4},{2,7},{3,6},{4,1},{5,0},{6,3},{7,2},{8,13},{9,12},{10,... | collective-permute-start | bytes 589832 | tf_op jit(solution)/shard_map/ppermute | solution.py:891
  71.4 49.4 %collective-permute-start.5 = (bf16[128,768]{1,0:T(8,128)(2,1)S(1)}, bf16[128,768]{1,0:T(8,128)(2,1)S(1)}, u32[]{:S(2)}, u32[]{:S(2)}) collective-permute-start(bf16[128,768]{1,0:T(8,128)(2,1)S(1)} %get-tuple-element.278), channel_id=1, source_target_pairs={{0,6},{1,7},{2,4},{3,5},{4,2},{5,3},{6,0},{7,1},{8,14},{9,15},{10,... | collective-permute-start | bytes 589832 | tf_op jit(solution)/shard_map/ppermute | solution.py:891
  76.7 44.1 %collective-permute-start.6 = (bf16[128,768]{1,0:T(8,128)(2,1)S(1)}, bf16[128,768]{1,0:T(8,128)(2,1)S(1)}, u32[]{:S(2)}, u32[]{:S(2)}) collective-permute-start(bf16[128,768]{1,0:T(8,128)(2,1)S(1)} %get-tuple-element.277), channel_id=1, source_target_pairs={{0,7},{1,6},{2,5},{3,4},{4,3},{5,2},{6,1},{7,0},{8,15},{9,14},{10,... | collective-permute-start | bytes 589832 | tf_op jit(solution)/shard_map/ppermute | solution.py:891
  121.7 41.5 %all-to-all-start.1 = ((bf16[8,128,768]{2,1,0:T(8,128)(2,1)}), bf16[8,128,768]{2,1,0:T(8,128)(2,1)S(1)}, u32[]{:S(2)}, u32[]{:S(2)}) async-start(bf16[8,128,768]{2,1,0:T(8,128)(2,1)} %bitcast.53), calls=%async_computation.1 | async-start | bytes 3145728 | tf_op jit(solution)/shard_map/all_to_all | solution.py:868
  164.4 42.4 %all-to-all-start.2 = ((bf16[8,128,768]{2,1,0:T(8,128)(2,1)}), bf16[8,128,768]{2,1,0:T(8,128)(2,1)}, u32[]{:S(2)}, u32[]{:S(2)}) async-start(bf16[8,128,768]{2,1,0:T(8,128)(2,1)} %bitcast.59), calls=%async_computation.2 | async-start | bytes 3145728 | tf_op jit(solution)/shard_map/all_to_all | solution.py:868
  206.8 41.8 %all-to-all-start.3 = ((bf16[8,128,768]{2,1,0:T(8,128)(2,1)}), bf16[8,128,768]{2,1,0:T(8,128)(2,1)S(1)}, u32[]{:S(2)}, u32[]{:S(2)}) async-start(bf16[8,128,768]{2,1,0:T(8,128)(2,1)} %bitcast.58), calls=%async_computation.3 | async-start | bytes 3145728 | tf_op jit(solution)/shard_map/all_to_all | solution.py:868
  210.9 29.2 %collective-permute-start.7 = (bf16[768,768]{1,0:T(8,128)(2,1)}, bf16[768,768]{1,0:T(8,128)(2,1)}, u32[]{:S(2)}, u32[]{:S(2)}) collective-permute-start(bf16[768,768]{1,0:T(8,128)(2,1)} %get-tuple-element.166), channel_id=1, source_target_pairs={{0,8},{8,0},{16,24},{24,16},{1,9},{9,1},{17,25},{25,17},{2,10},{10... | collective-permute-start | bytes 3538952 | tf_op jit(solution)/shard_map/ppermute | solution.py:903
  212.4 29.1 %collective-permute-start.8 = (bf16[768,768]{1,0:T(8,128)(2,1)}, bf16[768,768]{1,0:T(8,128)(2,1)}, u32[]{:S(2)}, u32[]{:S(2)}) collective-permute-start(bf16[768,768]{1,0:T(8,128)(2,1)} %get-tuple-element.167), channel_id=1, source_target_pairs={{0,16},{8,24},{16,0},{24,8},{1,17},{9,25},{17,1},{25,9},{2,18},{10... | collective-permute-start | bytes 3538952 | tf_op jit(solution)/shard_map/ppermute | solution.py:904
  214.0 52.9 %collective-permute-start.10 = (bf16[768,768]{1,0:T(8,128)(2,1)}, bf16[768,768]{1,0:T(8,128)(2,1)}, u32[]{:S(2)}, u32[]{:S(2)}) collective-permute-start(bf16[768,768]{1,0:T(8,128)(2,1)} %get-tuple-element.176), channel_id=1, source_target_pairs={{0,16},{8,24},{16,0},{24,8},{1,17},{9,25},{17,1},{25,9},{2,18},{10... | collective-permute-start | bytes 3538952 | tf_op jit(solution)/shard_map/ppermute | solution.py:904
  214.5 52.4 %collective-permute-start.9 = (bf16[768,768]{1,0:T(8,128)(2,1)}, bf16[768,768]{1,0:T(8,128)(2,1)}, u32[]{:S(2)}, u32[]{:S(2)}) collective-permute-start(bf16[768,768]{1,0:T(8,128)(2,1)} %get-tuple-element.175), channel_id=1, source_target_pairs={{0,8},{8,0},{16,24},{24,16},{1,9},{9,1},{17,25},{25,17},{2,10},{10... | collective-permute-start | bytes 3538952 | tf_op jit(solution)/shard_map/ppermute | solution.py:903
  248.6 42.7 %collective-permute-start.11 = (bf16[768,768]{1,0:T(8,128)(2,1)}, bf16[768,768]{1,0:T(8,128)(2,1)}, u32[]{:S(2)}, u32[]{:S(2)}) collective-permute-start(bf16[768,768]{1,0:T(8,128)(2,1)} %get-tuple-element.185), channel_id=1, source_target_pairs={{0,16},{8,24},{16,0},{24,8},{1,17},{9,25},{17,1},{25,9},{2,18},{10... | collective-permute-start | bytes 3538952 | tf_op jit(solution)/shard_map/ppermute | solution.py:904
  250.1 41.2 %collective-permute-start.12 = (bf16[768,768]{1,0:T(8,128)(2,1)}, bf16[768,768]{1,0:T(8,128)(2,1)}, u32[]{:S(2)}, u32[]{:S(2)}) collective-permute-start(bf16[768,768]{1,0:T(8,128)(2,1)} %get-tuple-element.186), channel_id=1, source_target_pairs={{0,8},{8,0},{16,24},{24,16},{1,9},{9,1},{17,25},{25,17},{2,10},{10... | collective-permute-start | bytes 3538952 | tf_op jit(solution)/shard_map/ppermute | solution.py:903
  296.3 82.0 %all-to-all-start.4 = ((bf16[8,256,768]{2,1,0:T(8,128)(2,1)}), bf16[8,256,768]{2,1,0:T(8,128)(2,1)}, u32[]{:S(2)}, u32[]{:S(2)}) async-start(bf16[8,256,768]{2,1,0:T(8,128)(2,1)} %expert_result.1), calls=%async_computation.4 | async-start | bytes 6291456 | tf_op jit(solution)/shard_map/all_to_all | solution.py:868
  301.4 30.1 %collective-permute-start.13 = (bf16[768,768]{1,0:T(8,128)(2,1)}, bf16[768,768]{1,0:T(8,128)(2,1)}, u32[]{:S(2)}, u32[]{:S(2)}) collective-permute-start(bf16[768,768]{1,0:T(8,128)(2,1)} %get-tuple-element.194.refs_0_), channel_id=1, source_target_pairs={{0,16},{8,24},{16,0},{24,8},{1,17},{9,25},{17,1},{25,9},{2,18},{10... | collective-permute-start | bytes 3538952 | tf_op jit(solution)/shard_map/ppermute | solution.py:904
  302.9 28.9 %collective-permute-start.14 = (bf16[768,768]{1,0:T(8,128)(2,1)S(1)}, bf16[768,768]{1,0:T(8,128)(2,1)}, u32[]{:S(2)}, u32[]{:S(2)}) collective-permute-start(bf16[768,768]{1,0:T(8,128)(2,1)S(1)} %get-tuple-element.195.refs_2_), channel_id=1, source_target_pairs={{0,8},{8,0},{16,24},{24,16},{1,9},{9,1},{17,25},{25,17},{2,10},{10... | collective-permute-start | bytes 3538952 | tf_op jit(solution)/shard_map/ppermute | solution.py:903
  303.5 28.4 %collective-permute-start.15 = (bf16[2,768,384]{2,1,0:T(8,128)(2,1)}, bf16[2,768,384]{2,1,0:T(8,128)(2,1)}, u32[]{:S(2)}, u32[]{:S(2)}) collective-permute-start(bf16[2,768,384]{2,1,0:T(8,128)(2,1)} %get-tuple-element.196), channel_id=1, source_target_pairs={{0,1},{1,0},{2,3},{3,2},{4,5},{5,4},{6,7},{7,6},{8,9},{9,8},{10,11... | collective-permute-start | bytes 3538952 | tf_op jit(solution)/shard_map/ppermute | solution.py:926
  305.8 37.8 %collective-permute-start.17 = (bf16[384,768]{1,0:T(8,128)(2,1)}, bf16[384,768]{1,0:T(8,128)(2,1)S(1)}, u32[]{:S(2)}, u32[]{:S(2)}) collective-permute-start(bf16[384,768]{1,0:T(8,128)(2,1)} %get-tuple-element.292), channel_id=1, source_target_pairs={{0,8},{8,0},{16,24},{24,16},{1,9},{9,1},{17,25},{25,17},{2,10},{10... | collective-permute-start | bytes 1769480 | tf_op jit(solution)/shard_map/ppermute | solution.py:903
  308.4 35.3 %collective-permute-start.18 = (bf16[384,768]{1,0:T(8,128)(2,1)}, bf16[384,768]{1,0:T(8,128)(2,1)}, u32[]{:S(2)}, u32[]{:S(2)}) collective-permute-start(bf16[384,768]{1,0:T(8,128)(2,1)} %get-tuple-element.290), channel_id=1, source_target_pairs={{0,16},{8,24},{16,0},{24,8},{1,17},{9,25},{17,1},{25,9},{2,18},{10... | collective-permute-start | bytes 1769480 | tf_op jit(solution)/shard_map/ppermute | solution.py:904
  346.2 15.7 %collective-permute-start.16 = (bf16[4,192,384]{2,1,0:T(8,128)(2,1)S(1)}, bf16[4,192,384]{2,1,0:T(8,128)(2,1)S(1)}, u32[]{:S(2)}, u32[]{:S(2)}) collective-permute-start(bf16[4,192,384]{2,1,0:T(8,128)(2,1)S(1)} %dynamic-slice_convert_fusion.1), channel_id=1, source_target_pairs={{0,8},{8,0},{16,24},{24,16},{1,9},{9,1},{17,25},{25,17},{2,10},{10... | collective-permute-start | bytes 1769480 | tf_op jit(solution)/shard_map/ppermute | solution.py:841
  349.1 15.8 %collective-permute-start.20 = (bf16[4,192,384]{2,1,0:T(8,128)(2,1)S(1)}, bf16[4,192,384]{2,1,0:T(8,128)(2,1)}, u32[]{:S(2)}, u32[]{:S(2)}) collective-permute-start(bf16[4,192,384]{2,1,0:T(8,128)(2,1)S(1)} %dynamic-slice_convert_fusion), channel_id=1, source_target_pairs={{0,16},{8,24},{16,0},{24,8},{1,17},{9,25},{17,1},{25,9},{2,18},{10... | collective-permute-start | bytes 1769480 | tf_op jit(solution)/shard_map/ppermute | solution.py:841
  378.4 16.5 %collective-permute-start.27 = (bf16[384,768]{1,0:T(8,128)(2,1)}, bf16[384,768]{1,0:T(8,128)(2,1)S(1)}, u32[]{:S(2)}, u32[]{:S(2)}) collective-permute-start(bf16[384,768]{1,0:T(8,128)(2,1)} %get-tuple-element.225), channel_id=1, source_target_pairs={{0,8},{8,0},{16,24},{24,16},{1,9},{9,1},{17,25},{25,17},{2,10},{10... | collective-permute-start | bytes 1769480 | tf_op jit(solution)/shard_map/ppermute | solution.py:903
  378.9 16.6 %collective-permute-start.28 = (bf16[384,768]{1,0:T(8,128)(2,1)}, bf16[384,768]{1,0:T(8,128)(2,1)}, u32[]{:S(2)}, u32[]{:S(2)}) collective-permute-start(bf16[384,768]{1,0:T(8,128)(2,1)} %get-tuple-element.227), channel_id=1, source_target_pairs={{0,16},{8,24},{16,0},{24,8},{1,17},{9,25},{17,1},{25,9},{2,18},{10... | collective-permute-start | bytes 1769480 | tf_op jit(solution)/shard_map/ppermute | solution.py:904
  382.1 25.4 %collective-permute-start.31 = (bf16[384,768]{1,0:T(8,128)(2,1)}, bf16[384,768]{1,0:T(8,128)(2,1)S(1)}, u32[]{:S(2)}, u32[]{:S(2)}) collective-permute-start(bf16[384,768]{1,0:T(8,128)(2,1)} %get-tuple-element.230), channel_id=1, source_target_pairs={{0,8},{8,0},{16,24},{24,16},{1,9},{9,1},{17,25},{25,17},{2,10},{10... | collective-permute-start | bytes 1769480 | tf_op jit(solution)/shard_map/ppermute | solution.py:903
  383.7 24.7 %collective-permute-start.32 = (bf16[384,768]{1,0:T(8,128)(2,1)}, bf16[384,768]{1,0:T(8,128)(2,1)S(1)}, u32[]{:S(2)}, u32[]{:S(2)}) collective-permute-start(bf16[384,768]{1,0:T(8,128)(2,1)} %get-tuple-element.231), channel_id=1, source_target_pairs={{0,16},{8,24},{16,0},{24,8},{1,17},{9,25},{17,1},{25,9},{2,18},{10... | collective-permute-start | bytes 1769480 | tf_op jit(solution)/shard_map/ppermute | solution.py:904
  395.5 10.8 %collective-permute-start.29 = (bf16[1,192,768]{2,1,0:T(8,128)(2,1)S(1)}, bf16[1,192,768]{2,1,0:T(8,128)(2,1)S(1)}, u32[]{:S(2)}, u32[]{:S(2)}) collective-permute-start(bf16[1,192,768]{2,1,0:T(8,128)(2,1)S(1)} %convert_add_fusion.9), channel_id=1, source_target_pairs={{0,4},{1,5},{2,6},{3,7},{4,0},{5,1},{6,2},{7,3},{8,12},{9,13},{10,... | collective-permute-start | bytes 884744 | tf_op jit(solution)/shard_map/ppermute | solution.py:836
  399.5 17.7 %collective-permute-start.34 = (bf16[384,768]{1,0:T(8,128)(2,1)S(1)}, bf16[384,768]{1,0:T(8,128)(2,1)S(1)}, u32[]{:S(2)}, u32[]{:S(2)}) collective-permute-start(bf16[384,768]{1,0:T(8,128)(2,1)S(1)} %get-tuple-element.234), channel_id=1, source_target_pairs={{0,8},{8,0},{16,24},{24,16},{1,9},{9,1},{17,25},{25,17},{2,10},{10... | collective-permute-start | bytes 1769480 | tf_op jit(solution)/shard_map/ppermute | solution.py:903
  402.6 14.8 %collective-permute-start.35 = (bf16[384,768]{1,0:T(8,128)(2,1)S(1)}, bf16[384,768]{1,0:T(8,128)(2,1)}, u32[]{:S(2)}, u32[]{:S(2)}) collective-permute-start(bf16[384,768]{1,0:T(8,128)(2,1)S(1)} %get-tuple-element.236), channel_id=1, source_target_pairs={{0,16},{8,24},{16,0},{24,8},{1,17},{9,25},{17,1},{25,9},{2,18},{10... | collective-permute-start | bytes 1769480 | tf_op jit(solution)/shard_map/ppermute | solution.py:904
  429.7 12.2 %collective-permute-start.40 = (bf16[4,192,384]{2,1,0:T(8,128)(2,1)S(1)}, bf16[4,192,384]{2,1,0:T(8,128)(2,1)}, u32[]{:S(2)}, u32[]{:S(2)}) collective-permute-start(bf16[4,192,384]{2,1,0:T(8,128)(2,1)S(1)} %maximum_select_fusion.4), channel_id=1, source_target_pairs={{0,16},{8,24},{16,0},{24,8},{1,17},{9,25},{17,1},{25,9},{2,18},{10... | collective-permute-start | bytes 1769480 | tf_op jit(solution)/shard_map/ppermute | solution.py:845
  430.2 13.6 %collective-permute-start.39 = (bf16[4,192,384]{2,1,0:T(8,128)(2,1)S(1)}, bf16[4,192,384]{2,1,0:T(8,128)(2,1)}, u32[]{:S(2)}, u32[]{:S(2)}) collective-permute-start(bf16[4,192,384]{2,1,0:T(8,128)(2,1)S(1)} %maximum_select_fusion.3), channel_id=1, source_target_pairs={{0,8},{8,0},{16,24},{24,16},{1,9},{9,1},{17,25},{25,17},{2,10},{10... | collective-permute-start | bytes 1769480 | tf_op jit(solution)/shard_map/ppermute | solution.py:845
  (44 other events, 278.3 us)
